TPU v7x, 32 devices: a whole 2x2x4 slice. The times are simulated.
32 devices in a mesh: groups: 2 (over y), ctx: 4 (over z), head: 2 (over x), fsdp: 2 (over core).
Axes of the slice: x: 2, y: 2, z: 4, core: 2. Of those that a mesh axis runs over, the one named last changes fastest.
Arguments:
- queries: float32 [2048, 4096], P(('groups', 'ctx'), ('head', 'fsdp')), parts along dimension 0, may hold values from -6 to 6
- key_input: float32 [2048, 4096], P(('groups', 'ctx'), ('head', 'fsdp')), parts along dimension 0, may hold values from -6 to 6
- value_input: float32 [2048, 4096], P(('groups', 'ctx'), ('head', 'fsdp')), parts along dimension 0, may hold values from -6 to 6
- log_decay: float32 [2048, 4096], P(('groups', 'ctx'), ('head', 'fsdp')), parts along dimension 0, may hold values from -1 to 0
- write_rate: float32 [2048, 32], P(('groups', 'ctx'), ('head', 'fsdp')), parts along dimension 0, may hold values from 0.02 to 0.2
- start_state: float32 [64, 128, 128], P(('groups', 'head', 'fsdp')), parts along dimension 0, may hold values from -4 to 4
- out_grad: float32 [2048, 4096], P(('groups', 'ctx'), ('head', 'fsdp')), parts along dimension 0, may hold values from -6 to 6
- end_grad: float32 [64, 128, 128], P(('groups', 'head', 'fsdp')), parts along dimension 0, may hold values from -4 to 4
- moe_input: bfloat16 [2048, 1152], P(('groups', 'ctx', 'fsdp')), parts along dimension 0, may hold values from -6 to 6
- moe_grad: float32 [2048, 1152], P(('groups', 'ctx', 'fsdp')), parts along dimension 0, may hold values from -6 to 6
- expert_ids: int32 [2048, 8], P(('groups', 'ctx', 'fsdp')), parts along dimension 0, may hold values from 0 to 31, all different within a row; in each aligned block of 128 rows (0 to 127, 128 to 255, ...) at most 48 rows name the same one
- gate_weights: float32 [2048, 8], P(('groups', 'ctx', 'fsdp')), parts along dimension 0, may hold values from 0.05 to 0.25
- gate_matrix: bfloat16 [32, 1152, 1024], P('ctx', 'fsdp', 'head'), may hold values from -0.1875 to 0.1875
- up_matrix: bfloat16 [32, 1152, 1024], P('ctx', 'fsdp', 'head'), may hold values from -0.1875 to 0.1875
- down_matrix: bfloat16 [32, 1024, 1152], P('ctx', 'head', 'fsdp'), may hold values from -0.1875 to 0.1875
Outputs:
- query_grad: float32 [2048, 4096], P(('groups', 'ctx'), ('head', 'fsdp')), parts along dimension 0
- key_grad: float32 [2048, 4096], P(('groups', 'ctx'), ('head', 'fsdp')), parts along dimension 0
- value_grad: float32 [2048, 4096], P(('groups', 'ctx'), ('head', 'fsdp')), parts along dimension 0
- decay_grad: float32 [2048, 4096], P(('groups', 'ctx'), ('head', 'fsdp')), parts along dimension 0
- rate_grad: float32 [2048, 32], P(('groups', 'ctx'), ('head', 'fsdp')), parts along dimension 0
- state_grads: float32 [8, 32, 128, 128], P(('groups', 'ctx'), ('head', 'fsdp')), parts along dimension 0
- input_grads: float32 [2048, 1152], P(('groups', 'ctx', 'fsdp'), 'head'), parts along dimension 0
- gate_grads: float32 [2048, 8], P(('groups', 'ctx', 'fsdp'), 'head'), parts along dimension 0
There are 2 independent parts, one for each index of `groups`. A program takes and returns all parts, laid end to end along the dimension named above; an argument that names none is the same for every part. Nothing has to cross between parts.
Inputs may be any that keep to these rules, and one draw needn't show every extreme that they name: `expert_ids`: each row names 8 different experts; within the 128 rows of one device no expert is named more than 48 times, a bound that some block reaches.
All inputs are finite; a program needn't handle non-finite values.
Results may differ from a plain program's by a relative error of at most 0.014.
Values may be sent and summed in bfloat16 or wider, within the bound.
No kernel may reach another device: no remote copies, remote signals or barrier semaphores. Data moves between devices by JAX's collectives and lax.ppermute only.
A program may use at most 192 MiB of HBM per device.

v0:
```python
import jax
import jax.numpy as jnp
from jax import lax
from jax.sharding import PartitionSpec as P

HIGHEST = lax.Precision.HIGHEST


def shifted(x, axis, by):
    count = lax.axis_size(axis)
    pairs = [(i, i + by) for i in range(count) if 0 <= i + by < count]
    return lax.ppermute(x, axis, pairs)


def unit_rows(matrix):
    return matrix * lax.rsqrt(jnp.sum(matrix * matrix, axis=-1, keepdims=True) + 1e-06)


def block_step(memory, inputs):
    query_b, key_b, value_b, decay_b, rate_b = inputs
    block_size = key_b.shape[0]
    cumulative = jnp.cumsum(decay_b, axis=0)
    middle = 0.5 * cumulative[-1]
    lifted = jnp.exp(cumulative - middle)
    sunk_keys = key_b * jnp.exp(middle - cumulative)
    places = lax.iota(jnp.int32, block_size)
    later_mask = places[:, None] > places[None, :]
    within_mask = places[:, None] >= places[None, :]
    rate_cols = jnp.transpose(rate_b)[:, None, :]
    key_scores = (
        jnp.einsum("thk,shk->hts", key_b * lifted, sunk_keys, precision=HIGHEST) * rate_cols
    )
    key_scores = jnp.where(later_mask[None], key_scores, 0.0)
    query_scores = (
        jnp.einsum("thk,shk->hts", query_b * lifted, sunk_keys, precision=HIGHEST) * rate_cols
    )
    query_scores = jnp.where(within_mask[None], query_scores, 0.0)
    decayed = jnp.exp(cumulative)
    residual_values = value_b - jnp.einsum(
        "thk,hkw->thw", key_b * decayed, memory, precision=HIGHEST
    )
    updates = jax.scipy.linalg.solve_triangular(
        key_scores, jnp.transpose(residual_values, (1, 0, 2)), lower=True, unit_diagonal=True
    )
    outputs = jnp.einsum("thk,hkw->thw", query_b * decayed, memory, precision=HIGHEST) + jnp.einsum(
        "hts,hsw->thw", query_scores, updates, precision=HIGHEST
    )
    tail_keys = key_b * jnp.exp(cumulative[-1][None] - cumulative) * rate_b[:, :, None]
    memory = jnp.exp(cumulative[-1])[:, :, None] * memory + jnp.einsum(
        "shk,hsw->hkw", tail_keys, updates, precision=HIGHEST
    )
    return (memory, outputs)


def spanned(memory_in, unit_query, unit_key, written, decays, write_rates):
    tokens_here = unit_key.shape[0]
    block_size = min(64, tokens_here)
    block_total = tokens_here // block_size

    def into_blocks(matrix):
        return matrix.reshape((block_total, block_size) + matrix.shape[1:])

    last_memory, outputs = lax.scan(
        jax.checkpoint(block_step),
        memory_in,
        (
            into_blocks(unit_query),
            into_blocks(unit_key),
            into_blocks(written),
            into_blocks(decays),
            into_blocks(write_rates),
        ),
    )
    return (last_memory, outputs.reshape((tokens_here,) + outputs.shape[2:]))


def section(memory_in, queries, key_input, value_input, log_decay, write_rate):
    tokens_here = queries.shape[0]
    shaped = (tokens_here, write_rate.shape[1], -1)
    last_memory, outputs = spanned(
        memory_in,
        unit_rows(queries.reshape(shaped)),
        unit_rows(key_input.reshape(shaped)),
        value_input.reshape(shaped),
        log_decay.reshape(shaped),
        write_rate,
    )
    return (outputs.reshape(tokens_here, -1), last_memory)


def apply_map(pair, memory_in):
    return jnp.einsum("hij,hjk->hik", pair[0], memory_in, precision=HIGHEST) + pair[1]


def per_device(
    queries,
    key_input,
    value_input,
    log_decay,
    write_rate,
    start_state,
    out_grad,
    end_grad,
    moe_input,
    moe_grad,
    expert_ids,
    gate_weights,
    gate_matrix,
    up_matrix,
    down_matrix,
):
    sections = lax.axis_size("ctx")
    position = lax.axis_index("ctx")
    heads_here, key_width, value_width = start_state.shape
    identity = jnp.broadcast_to(
        jnp.eye(key_width, dtype=jnp.float32), (heads_here, key_width, key_width)
    )
    zero_state = jnp.zeros_like(start_state)
    tokens_here = queries.shape[0]
    shaped = (tokens_here, heads_here, -1)
    widened = jnp.concatenate(
        [jnp.zeros((tokens_here, heads_here, key_width), jnp.float32), value_input.reshape(shaped)],
        axis=-1,
    )
    combined, ignored = spanned(
        jnp.concatenate([identity, zero_state], axis=-1),
        unit_rows(queries.reshape(shaped)),
        unit_rows(key_input.reshape(shaped)),
        widened,
        log_decay.reshape(shaped),
        write_rate,
    )
    transfer = combined[..., :key_width]
    carried = combined[..., key_width:]

    def forward_turn(turn_index, memory_in):
        leaving = apply_map((transfer, carried), memory_in)
        arrived = shifted(leaving.astype(jnp.bfloat16), "ctx", 1).astype(leaving.dtype)
        return jnp.where(position == 0, start_state, arrived)

    entry_state = lax.fori_loop(0, sections - 1, forward_turn, start_state)
    outputs, pullback = jax.vjp(
        section, entry_state, queries, key_input, value_input, log_decay, write_rate
    )
    own_grad = pullback((out_grad, zero_state))[0]
    backward_map = jnp.swapaxes(transfer, 1, 2)

    def backward_turn(turn_index, grad_out):
        grad_in = apply_map((backward_map, own_grad), grad_out)
        arrived = shifted(grad_in.astype(jnp.bfloat16), "ctx", -1).astype(grad_in.dtype)
        return jnp.where(position == sections - 1, end_grad, arrived)

    exit_grad = lax.fori_loop(0, sections - 1, backward_turn, end_grad)
    gradients = pullback((out_grad, exit_grad))
    gate_full, up_full, down_full = (
        lax.all_gather(gate_matrix, "fsdp", axis=1, tiled=True),
        lax.all_gather(up_matrix, "fsdp", axis=1, tiled=True),
        lax.all_gather(down_matrix, "fsdp", axis=2, tiled=True),
    )
    token_count, top_count = expert_ids.shape
    experts_here = gate_matrix.shape[0]
    total_experts = experts_here * sections
    capacity = 3 * token_count // 8
    flat_ids = expert_ids.reshape(-1)
    chosen = (flat_ids[:, None] == lax.iota(jnp.int32, total_experts)[None, :]).astype(jnp.int32)
    ranks = jnp.sum((jnp.cumsum(chosen, axis=0) - chosen) * chosen, axis=1)
    target = flat_ids * capacity + ranks
    width = moe_input.shape[1]
    slots = total_experts * capacity
    layout = (sections, experts_here, capacity)
    send_rows = (
        jnp.zeros((slots, width), jnp.bfloat16)
        .at[target]
        .set(jnp.repeat(moe_input, top_count, axis=0))
        .reshape(layout + (width,))
    )
    send_grads = (
        jnp.zeros((slots, width), jnp.bfloat16)
        .at[target]
        .set(jnp.repeat(moe_grad.astype(jnp.bfloat16), top_count, axis=0))
        .reshape(layout + (width,))
    )
    send_weights = (
        jnp.zeros((slots,), jnp.float32).at[target].set(gate_weights.reshape(-1)).reshape(layout)
    )
    rows_in = lax.all_to_all(send_rows, "ctx", split_axis=0, concat_axis=0, tiled=True)
    grads_in = lax.all_to_all(send_grads, "ctx", split_axis=0, concat_axis=0, tiled=True)
    weights_in = lax.all_to_all(
        send_weights.astype(jnp.bfloat16), "ctx", split_axis=0, concat_axis=0, tiled=True
    ).astype(send_weights.dtype)
    gate_pre = jnp.einsum("sjcd,jdf->sjcf", rows_in, gate_full, preferred_element_type=jnp.float32)
    up_pre = jnp.einsum("sjcd,jdf->sjcf", rows_in, up_full, preferred_element_type=jnp.float32)
    raw_grad = jnp.einsum("sjcd,jfd->sjcf", grads_in, down_full, preferred_element_type=jnp.float32)
    sigmoid_gate = jax.nn.sigmoid(gate_pre)
    activated = gate_pre * sigmoid_gate
    hidden = (activated * up_pre).astype(jnp.bfloat16)
    gate_part = jnp.sum(hidden.astype(jnp.float32) * raw_grad, axis=-1)
    scaled = raw_grad * weights_in[..., None]
    gate_back = (scaled * up_pre * sigmoid_gate * (1.0 + gate_pre * (1.0 - sigmoid_gate))).astype(
        jnp.bfloat16
    )
    up_back = (scaled * activated).astype(jnp.bfloat16)
    pieces = jnp.einsum("sjcf,jdf->sjcd", gate_back, gate_full, preferred_element_type=jnp.float32)
    pieces = pieces + jnp.einsum(
        "sjcf,jdf->sjcd", up_back, up_full, preferred_element_type=jnp.float32
    )
    returned_pieces = lax.all_to_all(
        pieces.astype(jnp.bfloat16), "ctx", split_axis=0, concat_axis=0, tiled=True
    )
    returned_gates = lax.all_to_all(
        gate_part.astype(jnp.bfloat16), "ctx", split_axis=0, concat_axis=0, tiled=True
    ).astype(gate_part.dtype)
    piece_rows = (
        returned_pieces.reshape(slots, -1)[target]
        .astype(jnp.float32)
        .reshape(token_count, top_count, -1)
        .sum(axis=1)
    )
    gate_rows = returned_gates.reshape(slots)[target].reshape(token_count, top_count)
    input_grads, gate_grads = (
        lax.psum_scatter(
            piece_rows.astype(jnp.bfloat16), "head", scatter_dimension=1, tiled=True
        ).astype(jnp.float32),
        lax.psum_scatter(
            gate_rows.astype(jnp.bfloat16), "head", scatter_dimension=1, tiled=True
        ).astype(jnp.float32),
    )
    return (
        gradients[1],
        gradients[2],
        gradients[3],
        gradients[4],
        gradients[5],
        gradients[0][None],
        input_grads,
        gate_grads,
    )


def solution(mesh):
    in_specs = (
        P(("groups", "ctx"), ("head", "fsdp")),
        P(("groups", "ctx"), ("head", "fsdp")),
        P(("groups", "ctx"), ("head", "fsdp")),
        P(("groups", "ctx"), ("head", "fsdp")),
        P(("groups", "ctx"), ("head", "fsdp")),
        P(("groups", "head", "fsdp"), None, None),
        P(("groups", "ctx"), ("head", "fsdp")),
        P(("groups", "head", "fsdp"), None, None),
        P(("groups", "ctx", "fsdp"), None),
        P(("groups", "ctx", "fsdp"), None),
        P(("groups", "ctx", "fsdp"), None),
        P(("groups", "ctx", "fsdp"), None),
        P("ctx", "fsdp", "head"),
        P("ctx", "fsdp", "head"),
        P("ctx", "head", "fsdp"),
    )
    out_specs = (
        P(("groups", "ctx"), ("head", "fsdp")),
        P(("groups", "ctx"), ("head", "fsdp")),
        P(("groups", "ctx"), ("head", "fsdp")),
        P(("groups", "ctx"), ("head", "fsdp")),
        P(("groups", "ctx"), ("head", "fsdp")),
        P(("groups", "ctx"), ("head", "fsdp"), None, None),
        P(("groups", "ctx", "fsdp"), "head"),
        P(("groups", "ctx", "fsdp"), "head"),
    )
    return jax.shard_map(
        per_device, mesh=mesh, in_specs=in_specs, out_specs=out_specs, check_vma=False
    )
```

profile of v0, /device:TPU:0, one launch (start us, length us, event | category | flops | bytes accessed | tf_op | source)
XLA Modules:
  0.0 1323.5 jit_solution(1441272677743282998)
XLA Ops:
  39.3 241.4 %while.92 = (s32[]{:T(128)}, f32[8,128,128]{2,1,0:T(8,128)S(1)}, f32[4,64,8,128]{3,2,1,0:T(8,128)}, f32[4,64,8,128]{3,2,1,0:T(8,128)}, f32[4,64,8,128]{3,2,1,0:T...) while((s32[]{:T(128)}, f32[8,128,128]{2,1,0:T(8,128)S(1)}, ...), condition=%wide.region_7.9_spmd.clone, body=%wide.region_5.8_spmd.clone.sunk | while | flops 508974144 | bytes 14260903 | solution.py:63
  52.8 40.7 %custom-call.39 = f32[8,1,64,64]{2,3,1,0:T(8,128)} custom-call(f32[8,1,64,64]{3,2,1,0:T(8,128)} %fusion.414), custom_call_target="InvertDiagBlocksLowerTriangular" | custom-call | tf_op jit(solution)/shard_map/transpose(jvp())/while/body/eval_jaxpr/checkpoint/jit(_solve_triangular)/vmap()/triangular_solve/custom-call.2 | solution.py:42
  113.2 40.7 %custom-call.39 = f32[8,1,64,64]{2,3,1,0:T(8,128)} custom-call(f32[8,1,64,64]{3,2,1,0:T(8,128)} %fusion.414), custom_call_target="InvertDiagBlocksLowerTriangular" | custom-call | tf_op jit(solution)/shard_map/transpose(jvp())/while/body/eval_jaxpr/checkpoint/jit(_solve_triangular)/vmap()/triangular_solve/custom-call.2 | solution.py:42
  173.5 40.7 %custom-call.39 = f32[8,1,64,64]{2,3,1,0:T(8,128)} custom-call(f32[8,1,64,64]{3,2,1,0:T(8,128)} %fusion.414), custom_call_target="InvertDiagBlocksLowerTriangular" | custom-call | tf_op jit(solution)/shard_map/transpose(jvp())/while/body/eval_jaxpr/checkpoint/jit(_solve_triangular)/vmap()/triangular_solve/custom-call.2 | solution.py:42
  233.8 40.7 %custom-call.39 = f32[8,1,64,64]{2,3,1,0:T(8,128)} custom-call(f32[8,1,64,64]{3,2,1,0:T(8,128)} %fusion.414), custom_call_target="InvertDiagBlocksLowerTriangular" | custom-call | tf_op jit(solution)/shard_map/transpose(jvp())/while/body/eval_jaxpr/checkpoint/jit(_solve_triangular)/vmap()/triangular_solve/custom-call.2 | solution.py:42
  297.1 195.9 %while.87 = (s32[]{:T(128)}, f32[8,128,256]{2,1,0:T(8,128)S(1)}, f32[4,64,8,128]{3,2,1,0:T(8,128)S(1)}, f32[4,64,8,128]{3,2,1,0:T(8,128)}, f32[4,64,8]{1,2,0:T(8,128)S(1)}, /*index=5*/f32[4,64,8,256]{3,2,1,0:T(8,128)}, s32[]{:T(128)}) while((s32[]{:T(128)}, f32[8,128,256]{2,1,0:T(8,128)S(1)}, f32[4,64,8,128]{3,2,1,0:T(8,128)S(1)}, ...), condition=%wide.region_3.4_spmd, body=%wide.region_1.3_spmd.sunk | while | flops 559105088 | bytes 11893397 | solution.py:63
  300.5 40.7 %custom-call.36 = f32[8,1,64,64]{2,3,1,0:T(8,128)} custom-call(f32[8,1,64,64]{3,2,1,0:T(8,128)} %fusion.325), custom_call_target="InvertDiagBlocksLowerTriangular" | custom-call | tf_op jit(solution)/shard_map/while/body/eval_jaxpr/checkpoint/jit(_solve_triangular)/vmap()/triangular_solve | solution.py:42
  349.5 40.7 %custom-call.36 = f32[8,1,64,64]{2,3,1,0:T(8,128)} custom-call(f32[8,1,64,64]{3,2,1,0:T(8,128)} %fusion.325), custom_call_target="InvertDiagBlocksLowerTriangular" | custom-call | tf_op jit(solution)/shard_map/while/body/eval_jaxpr/checkpoint/jit(_solve_triangular)/vmap()/triangular_solve | solution.py:42
  398.5 40.7 %custom-call.36 = f32[8,1,64,64]{2,3,1,0:T(8,128)} custom-call(f32[8,1,64,64]{3,2,1,0:T(8,128)} %fusion.325), custom_call_target="InvertDiagBlocksLowerTriangular" | custom-call | tf_op jit(solution)/shard_map/while/body/eval_jaxpr/checkpoint/jit(_solve_triangular)/vmap()/triangular_solve | solution.py:42
  447.5 40.7 %custom-call.36 = f32[8,1,64,64]{2,3,1,0:T(8,128)} custom-call(f32[8,1,64,64]{3,2,1,0:T(8,128)} %fusion.325), custom_call_target="InvertDiagBlocksLowerTriangular" | custom-call | tf_op jit(solution)/shard_map/while/body/eval_jaxpr/checkpoint/jit(_solve_triangular)/vmap()/triangular_solve | solution.py:42
  511.7 105.2 %while.89 = (s32[]{:T(128)}, f32[8,128,128]{2,1,0:T(8,128)S(1)}, pred[]{:T(512)}, f32[8,128,128]{2,1,0:T(8,128)}, f32[8,128,128]{2,1,0:T(8,128)S(1)}, /*index=5*/f32[8,128,128]{2,1,0:T(8,128)S(1)}, s32[]{:T(128)}) while((s32[]{:T(128)}, f32[8,128,128]{2,1,0:T(8,128)S(1)}, pred[]{:T(512)}, f32[8,128,128]{2,1,0:T(8,128)}, ...), condition=%wide.region_11.13_spmd, body=%wide.region_10.12_spmd.sunk | while | flops 201850880 | bytes 5243026 | solution.py:141
  517.3 56.3 %collective-permute-done.1 = bf16[8,128,128]{2,1,0:T(8,128)(2,1)S(1)} collective-permute-done((bf16[8,128,128]{2,1,0:T(8,128)(2,1)S(1)}, bf16[8,128,128]{2,1,0:T(8,128)(2,1)S(1)}, u32[]{:S(2)}, u32[]{:S(2)}) %collective-permute-start.1) | collective-permute-done | bytes 262176 | tf_op jit(solution)/shard_map/while/body/eval_jaxpr/ppermute | solution.py:12
  616.9 194.1 %while.91 = (s32[]{:T(128)}, f32[8,128,128]{2,1,0:T(8,128)S(1)}, f32[4,8,128,128]{3,2,1,0:T(8,128)}, f32[4,64,8,128]{3,2,1,0:T(8,128)S(1)}, f32[4,64,8,128]{3,2,...) while((s32[]{:T(128)}, f32[8,128,128]{2,1,0:T(8,128)S(1)}, ...), condition=%wide.region_14.17_spmd.clone, body=%wide.region_12.16_spmd.clone.sunk | while | flops 307115072 | bytes 7433325 | solution.py:63
  619.6 40.7 %custom-call.38 = f32[8,1,64,64]{2,3,1,0:T(8,128)} custom-call(f32[8,1,64,64]{3,2,1,0:T(8,128)} %fusion.390), custom_call_target="InvertDiagBlocksLowerTriangular" | custom-call | tf_op jit(solution)/shard_map/jvp()/while/body/eval_jaxpr/jit(_solve_triangular)/vmap()/triangular_solve/custom-call.0 | solution.py:42
  668.1 40.7 %custom-call.38 = f32[8,1,64,64]{2,3,1,0:T(8,128)} custom-call(f32[8,1,64,64]{3,2,1,0:T(8,128)} %fusion.390), custom_call_target="InvertDiagBlocksLowerTriangular" | custom-call | tf_op jit(solution)/shard_map/jvp()/while/body/eval_jaxpr/jit(_solve_triangular)/vmap()/triangular_solve/custom-call.0 | solution.py:42
  716.6 40.7 %custom-call.38 = f32[8,1,64,64]{2,3,1,0:T(8,128)} custom-call(f32[8,1,64,64]{3,2,1,0:T(8,128)} %fusion.390), custom_call_target="InvertDiagBlocksLowerTriangular" | custom-call | tf_op jit(solution)/shard_map/jvp()/while/body/eval_jaxpr/jit(_solve_triangular)/vmap()/triangular_solve/custom-call.0 | solution.py:42
  765.1 40.7 %custom-call.38 = f32[8,1,64,64]{2,3,1,0:T(8,128)} custom-call(f32[8,1,64,64]{3,2,1,0:T(8,128)} %fusion.390), custom_call_target="InvertDiagBlocksLowerTriangular" | custom-call | tf_op jit(solution)/shard_map/jvp()/while/body/eval_jaxpr/jit(_solve_triangular)/vmap()/triangular_solve/custom-call.0 | solution.py:42
  875.6 106.4 %while.88 = (s32[]{:T(128)}, f32[8,128,128]{2,1,0:T(8,128)S(1)}, pred[]{:T(512)}, f32[8,128,128]{2,1,0:T(8,128)S(1)}, f32[8,128,128]{2,1,0:T(8,128)S(1)}, /*index=5*/f32[8,128,128]{2,1,0:T(8,128)S(1)}, s32[]{:T(128)}) while((s32[]{:T(128)}, f32[8,128,128]{2,1,0:T(8,128)S(1)}, pred[]{:T(512)}, f32[8,128,128]{2,1,0:T(8,128)S(1)}, ...), condition=%wide.region_9.11_spmd, body=%wide.region_8.10_spmd.sunk | while | flops 201850880 | bytes 5243026 | solution.py:153
  877.5 40.1 %collective-permute-done = bf16[8,128,128]{2,1,0:T(8,128)(2,1)S(1)} collective-permute-done((bf16[8,128,128]{2,1,0:T(8,128)(2,1)S(1)}, bf16[8,128,128]{2,1,0:T(8,128)(2,1)S(1)}, u32[]{:S(2)}, u32[]{:S(2)}) %collective-permute-start) | collective-permute-done | bytes 262176 | tf_op jit(solution)/shard_map/while/body/eval_jaxpr/ppermute | solution.py:12
  921.3 47.0 %collective-permute-done = bf16[8,128,128]{2,1,0:T(8,128)(2,1)S(1)} collective-permute-done((bf16[8,128,128]{2,1,0:T(8,128)(2,1)S(1)}, bf16[8,128,128]{2,1,0:T(8,128)(2,1)S(1)}, u32[]{:S(2)}, u32[]{:S(2)}) %collective-permute-start) | collective-permute-done | bytes 262176 | tf_op jit(solution)/shard_map/while/body/eval_jaxpr/ppermute | solution.py:12
  986.2 280.0 %while.90 = (s32[]{:T(128)}, f32[8,128,128]{2,1,0:T(8,128)S(1)}, f32[4,64,8,128]{3,2,1,0:T(8,128)}, f32[4,64,8,128]{3,2,1,0:T(8,128)}, f32[4,64,8,128]{3,2,1,0:T...) while((s32[]{:T(128)}, f32[8,128,128]{2,1,0:T(8,128)S(1)}, ...), condition=%wide.region_25.28_spmd, body=%wide.region_15.27_spmd.sunk | while | flops 1298158080 | bytes 41386764 | solution.py:63
  999.2 39.3 %custom-call.37 = f32[8,1,64,64]{2,3,1,0:T(8,128)S(1)} custom-call(f32[8,1,64,64]{3,2,1,0:T(8,128)S(1)} %add_bitcast_fusion.6), custom_call_target="InvertDiagBlocksLowerTriangular" | custom-call | tf_op jit(solution)/shard_map/transpose(jvp())/while/body/eval_jaxpr/checkpoint/jit(_solve_triangular)/vmap()/triangular_solve/custom-call.2 | solution.py:42
  1139.0 39.3 %custom-call.37 = f32[8,1,64,64]{2,3,1,0:T(8,128)S(1)} custom-call(f32[8,1,64,64]{3,2,1,0:T(8,128)S(1)} %add_bitcast_fusion.6), custom_call_target="InvertDiagBlocksLowerTriangular" | custom-call | tf_op jit(solution)/shard_map/transpose(jvp())/while/body/eval_jaxpr/checkpoint/jit(_solve_triangular)/vmap()/triangular_solve/custom-call.2 | solution.py:42
  1208.9 39.3 %custom-call.37 = f32[8,1,64,64]{2,3,1,0:T(8,128)S(1)} custom-call(f32[8,1,64,64]{3,2,1,0:T(8,128)S(1)} %add_bitcast_fusion.6), custom_call_target="InvertDiagBlocksLowerTriangular" | custom-call | tf_op jit(solution)/shard_map/transpose(jvp())/while/body/eval_jaxpr/checkpoint/jit(_solve_triangular)/vmap()/triangular_solve/custom-call.2 | solution.py:42
  (620 shorter events, 555.4 us)
Async XLA Ops:
  7.2 276.8 %copy-start = (bf16[128,1152]{1,0:T(8,128)(2,1)S(1)}, bf16[128,1152]{1,0:T(8,128)(2,1)}, u32[]{:S(2)}) copy-start(bf16[128,1152]{1,0:T(8,128)(2,1)} %param.39) | copy-start | bytes 884740
  7.2 805.3 %all-gather.8.cloned.1.call-start = ((), (), s32[]{:S(2)}) async-start(), calls=%async_computation.8 | async-start | bytes 14155776 | tf_op jit(solution)/shard_map/all_gather | solution.py:156
  7.9 813.3 %all-gather.6.cloned.1.call-start = ((), (), s32[]{:S(2)}) async-start(), calls=%async_computation.7 | async-start | bytes 14155776 | tf_op jit(solution)/shard_map/all_gather | solution.py:157
  9.0 22.1 %copy-start.19 = (f32[256,1024]{1,0:T(8,128)S(1)}, f32[256,1024]{1,0:T(8,128)}, u32[]{:S(2)}) copy-start(f32[256,1024]{1,0:T(8,128)} %param.32) | copy-start | bytes 3145732
  24.1 267.9 %all-to-all-start.1 = ((bf16[4,2,192]{2,1,0:T(2,128)(2,1)}), bf16[4,2,192]{2,1,0:T(2,128)(2,1)S(1)}, u32[]{:S(2)}, u32[]{:S(2)}) async-start(bf16[4,2,192]{2,1,0:T(2,128)(2,1)} %reshape.509), calls=%async_computation.1 | async-start | bytes 8192 | tf_op jit(solution)/shard_map/all_to_all | solution.py:188
  30.4 799.4 %all-gather.4.cloned.1.call-start = ((), (), s32[]{:S(2)}) async-start(), calls=%async_computation.6 | async-start | bytes 14155776 | tf_op jit(solution)/shard_map/all_gather | solution.py:158
  51.4 46.2 %copy-start.5 = (f32[64,8,128]{2,1,0:T(8,128)S(1)}, f32[64,8,128]{2,1,0:T(8,128)}, u32[]{:S(2)}) copy-start(f32[64,8,128]{2,1,0:T(8,128)} %get-tuple-element.1535) | copy-start | bytes 786436 | tf_op jit(solution)/shard_map/transpose(jvp())/while
  111.8 46.2 %copy-start.5 = (f32[64,8,128]{2,1,0:T(8,128)S(1)}, f32[64,8,128]{2,1,0:T(8,128)}, u32[]{:S(2)}) copy-start(f32[64,8,128]{2,1,0:T(8,128)} %get-tuple-element.1535) | copy-start | bytes 786436 | tf_op jit(solution)/shard_map/transpose(jvp())/while
  172.1 46.2 %copy-start.5 = (f32[64,8,128]{2,1,0:T(8,128)S(1)}, f32[64,8,128]{2,1,0:T(8,128)}, u32[]{:S(2)}) copy-start(f32[64,8,128]{2,1,0:T(8,128)} %get-tuple-element.1535) | copy-start | bytes 786436 | tf_op jit(solution)/shard_map/transpose(jvp())/while
  232.4 46.2 %copy-start.5 = (f32[64,8,128]{2,1,0:T(8,128)S(1)}, f32[64,8,128]{2,1,0:T(8,128)}, u32[]{:S(2)}) copy-start(f32[64,8,128]{2,1,0:T(8,128)} %get-tuple-element.1535) | copy-start | bytes 786436 | tf_op jit(solution)/shard_map/transpose(jvp())/while
  292.0 214.5 %all-to-all-start.2 = ((bf16[4,8,48,1152]{3,2,1,0:T(8,128)(2,1)}), bf16[4,8,48,1152]{3,2,1,0:T(8,128)(2,1)}, u32[]{:S(2)}, u32[]{:S(2)}) async-start(bf16[4,8,48,1152]{3,2,1,0:T(8,128)(2,1)} %bitcast.613), calls=%async_computation.2 | async-start | bytes 7077888 | tf_op jit(solution)/shard_map/all_to_all | solution.py:186
  506.4 323.4 %all-to-all-start = ((bf16[4,8,48,1152]{3,2,1,0:T(8,128)(2,1)}), bf16[4,8,48,1152]{3,2,1,0:T(8,128)(2,1)}, u32[]{:S(2)}, u32[]{:S(2)}) async-start(bf16[4,8,48,1152]{3,2,1,0:T(8,128)(2,1)} %bitcast.612), calls=%async_computation | async-start | bytes 7077888 | tf_op jit(solution)/shard_map/all_to_all | solution.py:187
  513.4 60.2 %collective-permute-start.1 = (bf16[8,128,128]{2,1,0:T(8,128)(2,1)S(1)}, bf16[8,128,128]{2,1,0:T(8,128)(2,1)S(1)}, u32[]{:S(2)}, u32[]{:S(2)}) collective-permute-start(bf16[8,128,128]{2,1,0:T(8,128)(2,1)S(1)} %fusion.333), channel_id=1, source_target_pairs={{0,4},{4,8},{8,12},{1,5},{5,9},{9,13},{2,6},{6,10},{10,14},{3,7},{... | collective-permute-start | bytes 786440 | tf_op jit(solution)/shard_map/while/body/eval_jaxpr/ppermute | solution.py:12
  577.1 26.5 %collective-permute-start.1 = (bf16[8,128,128]{2,1,0:T(8,128)(2,1)S(1)}, bf16[8,128,128]{2,1,0:T(8,128)(2,1)S(1)}, u32[]{:S(2)}, u32[]{:S(2)}) collective-permute-start(bf16[8,128,128]{2,1,0:T(8,128)(2,1)S(1)} %fusion.333), channel_id=1, source_target_pairs={{0,4},{4,8},{8,12},{1,5},{5,9},{9,13},{2,6},{6,10},{10,14},{3,7},{... | collective-permute-start | bytes 786440 | tf_op jit(solution)/shard_map/while/body/eval_jaxpr/ppermute | solution.py:12
  606.9 8.3 collective-permute-start.1
  616.9 195.4 %copy-start.8 = (f32[8,128,128]{2,1,0:T(8,128)S(1)}, f32[8,128,128]{2,1,0:T(8,128)}, u32[]{:S(2)}) copy-start(f32[8,128,128]{2,1,0:T(8,128)} %param.38) | copy-start | bytes 1572868
  869.9 403.0 %all-to-all-start.3 = ((bf16[4,8,48,1152]{3,2,1,0:T(8,128)(2,1)}), bf16[4,8,48,1152]{3,2,1,0:T(8,128)(2,1)}, u32[]{:S(2)}, u32[]{:S(2)}) async-start(bf16[4,8,48,1152]{3,2,1,0:T(8,128)(2,1)} %copy.300), calls=%async_computation.3 | async-start | bytes 7077888 | tf_op jit(solution)/shard_map/all_to_all | solution.py:207
  875.6 439.0 %reduce-scatter.5.cloned.1.call-start = ((), (), s32[]{:S(2)}) async-start(), calls=%async_computation.9 | async-start | bytes 442368
  876.2 41.4 %collective-permute-start = (bf16[8,128,128]{2,1,0:T(8,128)(2,1)S(1)}, bf16[8,128,128]{2,1,0:T(8,128)(2,1)S(1)}, u32[]{:S(2)}, u32[]{:S(2)}) collective-permute-start(bf16[8,128,128]{2,1,0:T(8,128)(2,1)S(1)} %fusion.330), channel_id=1, source_target_pairs={{4,0},{8,4},{12,8},{5,1},{9,5},{13,9},{6,2},{10,6},{14,10},{7,3},{... | collective-permute-start | bytes 786440 | tf_op jit(solution)/shard_map/while/body/eval_jaxpr/ppermute | solution.py:12
  920.0 48.3 %collective-permute-start = (bf16[8,128,128]{2,1,0:T(8,128)(2,1)S(1)}, bf16[8,128,128]{2,1,0:T(8,128)(2,1)S(1)}, u32[]{:S(2)}, u32[]{:S(2)}) collective-permute-start(bf16[8,128,128]{2,1,0:T(8,128)(2,1)S(1)} %fusion.330), channel_id=1, source_target_pairs={{4,0},{8,4},{12,8},{5,1},{9,5},{13,9},{6,2},{10,6},{14,10},{7,3},{... | collective-permute-start | bytes 786440 | tf_op jit(solution)/shard_map/while/body/eval_jaxpr/ppermute | solution.py:12
  970.6 9.6 collective-permute-start
  1266.2 15.5 %copy-start.2 = (f32[8,128,128]{2,1,0:T(8,128)}, f32[8,128,128]{2,1,0:T(8,128)S(1)}, u32[]{:S(2)}) copy-start(f32[8,128,128]{2,1,0:T(8,128)S(1)} %get-tuple-element.701) | copy-start | bytes 1572868
  1287.4 11.0 all-to-all-start.4
  1294.2 22.3 %copy-start.1 = (bf16[128,1152]{1,0:T(8,128)(2,1)S(1)}, bf16[128,1152]{1,0:T(8,128)(2,1)}, u32[]{:S(2)}) copy-start(bf16[128,1152]{1,0:T(8,128)(2,1)} %param.39) | copy-start | bytes 884740
  (47 other events, 211.2 us)
Sparse Core Ops, SparseCore 0:
  9.6 24.4 all-gather.7
  35.6 23.0 all-gather.5
  60.3 22.9 all-gather.3
  1286.2 11.1 reduce-scatter.4
where the time goes:
time: 1340 us; the launch traced here: 1320 us
  other arithmetic  754 us (56%)
  matrix products  192 us (14%)
  waiting for transfers between devices  162 us (12%)
  local copies, waits for them, and re-layouts  128 us (10%)
  starting transfers between devices  60.5 us (5%)
  between operations  15.5 us (1%)
    another operation x60, other arithmetic, block_step(): jax.scipy.linalg.solve_triangular(key_scores, jnp.transpose(residual_valu...  647 us
    ppermute x6, waiting for transfers between devices, shifted(): return lax.ppermute(x, axis, pairs)  159 us
    another operation x20, other arithmetic, block_step(): cumulative = jnp.cumsum(decay_b, axis=0)  55.4 us
    ppermute x6, starting transfers between devices, shifted(): return lax.ppermute(x, axis, pairs)  34.8 us
    dot_general x24, matrix products, block_step(): jnp.einsum('thk,hkw->thw', key_b * decayed, memory, precision=HIGHEST)  28.3 us
    squeeze x36, local copies, waits for them, and re-layouts, spanned(): lax.scan(jax.checkpoint(block_step), memory_in, (into_blocks(unit_query),...  26.9 us
  transfers between devices with their start and end apart: 15, of which 6 were waited for; matrix products, arithmetic and copies ran while one was open for 77% of the time, Pallas kernels for 0%

commit v1 on v0

v1 whole, which is shorter than its diff:
```python
import functools

import jax
import jax.numpy as jnp
from jax import lax
from jax.experimental import pallas as pl
from jax.experimental.pallas import tpu as pltpu
from jax.sharding import PartitionSpec as P

BF = jnp.bfloat16
F32 = jnp.float32
VMEM_BYTES = 48 * 1024 * 1024


def dot(a, b):
    return lax.dot_general(
        a.astype(BF), b.astype(BF), (((1,), (0,)), ((), ())), preferred_element_type=F32
    )


def dot_t(a, b):
    return lax.dot_general(
        a.astype(BF), b.astype(BF), (((1,), (1,)), ((), ())), preferred_element_type=F32
    )


def tdot(a, b):
    return lax.dot_general(
        a.astype(BF), b.astype(BF), (((0,), (0,)), ((), ())), preferred_element_type=F32
    )


def halves(x, axis):
    high = x.astype(BF)
    return jnp.concatenate([high, (x - high.astype(F32)).astype(BF)], axis=axis)


def places(size, axis):
    return lax.broadcasted_iota(jnp.int32, (size, size), axis)


def column(matrix, at):
    lanes = lax.broadcasted_iota(jnp.int32, matrix.shape, 1)
    return jnp.sum(jnp.where(lanes == at, matrix, 0.0), axis=1, keepdims=True)


def to_column(row):
    size = row.shape[1]
    spread = jnp.broadcast_to(row, (size, size))
    return jnp.sum(jnp.where(places(size, 0) == places(size, 1), spread, 0.0), axis=1, keepdims=True)


def inverse_less_one(scores):
    size = scores[0].shape[0]
    rows, cols = places(size, 0), places(size, 1)
    eye = (rows == cols).astype(F32)
    span, off = 1, None
    while span < size:
        joins = (rows // (2 * span) == cols // (2 * span)) & (rows // span != cols // span)
        parts = [jnp.where(joins, a, 0.0).astype(BF) for a in scores]
        if off is None:
            off = [-p.astype(F32) for p in parts]
        else:
            full = [(o + eye).astype(BF) for o in off]
            half = [dot(p, f) for p, f in zip(parts, full)]
            off = [o - dot(f, h) for o, f, h in zip(off, full, half)]
        span *= 2
    return off


def maps_kernel(
    chunk,
    width,
    heads_step,
    query_ref,
    key_ref,
    value_ref,
    decay_ref,
    rate_ref,
    grad_ref,
    transfer_ref,
    carried_ref,
    own_ref,
    cum_ref,
    query_l_ref,
    key_l_ref,
    back_ref,
    lower_ref,
    score_ref,
):
    tokens = query_ref.shape[0]
    chunks = tokens // chunk
    rows, cols = places(chunk, 0), places(chunk, 1)
    tri = (rows >= cols).astype(BF)
    tri = jnp.concatenate([tri, tri], axis=1)
    units = [(h, i) for h in range(heads_step) for i in range(chunks)]
    first = pl.program_id(0) * heads_step
    rates = [column(rate_ref[...], first + h) for h in range(heads_step)]

    def part(ref, unit):
        h, i = unit
        return ref[i * chunk : (i + 1) * chunk, h * width : (h + 1) * width]

    def unit_rows(x):
        return x * lax.rsqrt(jnp.sum(x * x, axis=-1, keepdims=True) + 1e-06)

    cums = [dot(tri, halves(part(decay_ref, u), 0)) for u in units]
    queries = [unit_rows(part(query_ref, u)) for u in units]
    keys = [unit_rows(part(key_ref, u)) for u in units]
    values = [part(value_ref, u) for u in units]
    middles = [0.5 * c[chunk - 1 : chunk, :] for c in cums]
    lifts = [jnp.exp(c - m) for c, m in zip(cums, middles)]
    sinks = [jnp.exp(m - c) for c, m in zip(cums, middles)]
    key_l = [(k * e).astype(BF) for k, e in zip(keys, lifts)]
    query_l = [(q * e).astype(BF) for q, e in zip(queries, lifts)]
    back = [
        (k * e * rates[h][i * chunk : (i + 1) * chunk]).astype(BF)
        for k, e, (h, i) in zip(keys, sinks, units)
    ]
    both = [dot_t(jnp.concatenate([k, q], axis=0), b) for k, q, b in zip(key_l, query_l, back)]
    key_scores = [jnp.where(rows > cols, s[:chunk], 0.0) for s in both]
    scores = [jnp.where(rows >= cols, s[chunk:], 0.0).astype(BF) for s in both]
    lower = [o.astype(BF) for o in inverse_less_one(key_scores)]
    wide = [jnp.concatenate([k, v.astype(BF)], axis=1) for k, v in zip(key_l, values)]
    solved = [
        dot(o, w) + jnp.concatenate([k.astype(F32), v], axis=1)
        for o, w, k, v in zip(lower, wide, key_l, values)
    ]
    solved = [s.astype(BF) for s in solved]
    stepped = [tdot(b, s) for b, s in zip(back, solved)]
    reads = [q.astype(F32) - dot(p, s[:, :width]) for q, p, s in zip(query_l, scores, solved)]
    mids = [to_column(jnp.exp(m)) for m in middles]
    owns = [m * tdot(r, part(grad_ref, u)) for m, r, u in zip(mids, reads, units)]
    for n, u in enumerate(units):
        h, i = u
        span = slice(i * chunk, (i + 1) * chunk)
        lanes = slice(h * width, (h + 1) * width)
        cum_ref[span, lanes] = cums[n]
        query_l_ref[span, lanes] = query_l[n]
        key_l_ref[span, lanes] = key_l[n]
        back_ref[span, lanes] = back[n]
        lower_ref[h, span, :] = lower[n]
        score_ref[h, span, :] = scores[n]
    eye = (places(width, 0) == places(width, 1)).astype(F32)
    for h in range(heads_step):
        state = None
        for i in range(chunks):
            n = h * chunks + i
            mid, step = mids[n], stepped[n][:, :width]
            entering = jnp.concatenate([eye, jnp.zeros_like(eye)], axis=1) if i == 0 else state
            scaled = mid * entering
            moved = scaled - dot(step, scaled)
            carried = jnp.concatenate([jnp.zeros_like(eye), stepped[n][:, width:]], axis=1)
            state = mid * (moved + carried)
        transfer_ref[h] = state[:, :width]
        carried_ref[h] = state[:, width:]
        total = owns[h * chunks + chunks - 1]
        for i in range(chunks - 2, -1, -1):
            n = h * chunks + i
            scaled = mids[n] * total
            total = owns[n] + mids[n] * (scaled - tdot(stepped[n][:, :width], scaled))
        own_ref[h] = total


def grads_kernel(
    chunk,
    width,
    heads_step,
    query_ref,
    key_ref,
    value_ref,
    rate_ref,
    grad_ref,
    cum_ref,
    query_l_ref,
    key_l_ref,
    back_ref,
    lower_ref,
    score_ref,
    entry_ref,
    exit_ref,
    query_grad_ref,
    key_grad_ref,
    value_grad_ref,
    decay_grad_ref,
    rate_grad_ref,
    state_grad_ref,
):
    tokens = query_ref.shape[0]
    chunks = tokens // chunk
    rows, cols = places(chunk, 0), places(chunk, 1)
    tri = (rows <= cols).astype(BF)
    tri = jnp.concatenate([tri, tri], axis=1)
    first = pl.program_id(0) * heads_step
    heads = range(heads_step)
    rates = [column(rate_ref[...], first + h) for h in heads]

    def part(ref, h, i):
        return ref[i * chunk : (i + 1) * chunk, h * width : (h + 1) * width]

    def mat(ref, h, i):
        return ref[h, i * chunk : (i + 1) * chunk, :]

    cums = {(h, i): part(cum_ref, h, i) for i in range(chunks) for h in heads}
    middles = {u: 0.5 * c[chunk - 1 : chunk, :] for u, c in cums.items()}
    mids = {u: to_column(jnp.exp(m)) for u, m in middles.items()}
    states = {(h, 0): entry_ref[h] for h in heads}
    scaled, updates = {}, {}
    for i in range(chunks):
        for h in heads:
            u = (h, i)
            scaled[u] = mids[u] * states[u]
        rests = [part(value_ref, h, i) - dot(part(key_l_ref, h, i), scaled[h, i]) for h in heads]
        for h in heads:
            updates[h, i] = (rests[h] + dot(mat(lower_ref, h, i), rests[h])).astype(BF)
        for h in heads:
            moved = scaled[h, i] + tdot(part(back_ref, h, i), updates[h, i])
            states[h, i + 1] = mids[h, i] * moved
    out = {(h, chunks): exit_ref[h] for h in heads}
    rest_grads, lifted, out_grads = {}, {}, {}
    for i in range(chunks - 1, -1, -1):
        update_grads = []
        for h in heads:
            lifted[h, i] = mids[h, i] * out[h, i + 1]
            out_grads[h, i] = part(grad_ref, h, i).astype(BF)
            got = tdot(mat(score_ref, h, i), out_grads[h, i])
            update_grads.append(got + dot(part(back_ref, h, i), lifted[h, i]))
        for h in heads:
            rest = update_grads[h] + tdot(mat(lower_ref, h, i), update_grads[h])
            value_grad_ref[i * chunk : (i + 1) * chunk, h * width : (h + 1) * width] = rest
            rest_grads[h, i] = rest.astype(BF)
        for h in heads:
            left = jnp.concatenate([part(query_l_ref, h, i), part(key_l_ref, h, i)], axis=0)
            right = jnp.concatenate([out_grads[h, i], -rest_grads[h, i]], axis=0)
            out[h, i] = mids[h, i] * (lifted[h, i] + tdot(left, right))
    for h in heads:
        state_grad_ref[h] = out[h, 0]
    units = [(h, i) for i in range(chunks) for h in heads]
    joint = [jnp.concatenate([-rest_grads[u], out_grads[u]], axis=0) for u in units]
    pairs = [dot_t(j, updates[u]) for j, u in zip(joint, units)]
    key_pairs = [jnp.where(rows > cols, p[:chunk], 0.0).astype(BF) for p in pairs]
    query_pairs = [jnp.where(rows >= cols, p[chunk:], 0.0).astype(BF) for p in pairs]
    pairs = [jnp.concatenate([k, q], axis=0) for k, q in zip(key_pairs, query_pairs)]
    left_grads = [
        dot(p, part(back_ref, *u)) + dot_t(j, scaled[u]) for p, j, u in zip(pairs, joint, units)
    ]
    back_grads = [
        tdot(p, jnp.concatenate([part(key_l_ref, *u), part(query_l_ref, *u)], axis=0))
        + dot_t(updates[u], lifted[u])
        for p, u in zip(pairs, units)
    ]
    ones = jnp.ones((8, 2 * width), BF)
    crossing = [
        dot_t(ones, halves(out[h, i + 1] * states[h, i + 1], 1))[:1] for h, i in units
    ]
    slopes = [
        part(key_l_ref, *u).astype(F32) * l[:chunk]
        + part(query_l_ref, *u).astype(F32) * l[chunk:]
        - part(back_ref, *u).astype(F32) * b
        for u, l, b in zip(units, left_grads, back_grads)
    ]
    decays = [dot(tri, halves(s, 0)) + c for s, c in zip(slopes, crossing)]
    if heads_step * pl.num_programs(0) == rate_grad_ref.shape[1]:
        lanes = lax.broadcasted_iota(jnp.int32, (chunk, rate_grad_ref.shape[1]), 1)
    for n, (h, i) in enumerate(units):
        span = slice(i * chunk, (i + 1) * chunk)
        at = slice(h * width, (h + 1) * width)
        decay_grad_ref[span, at] = decays[n]
        gap = cums[h, i] - middles[h, i]
        lift, sink = jnp.exp(gap), jnp.exp(-gap)
        rate = rates[h][span]
        query, key = query_ref[span, at], key_ref[span, at]
        query_norm = lax.rsqrt(jnp.sum(query * query, axis=-1, keepdims=True) + 1e-06)
        key_norm = lax.rsqrt(jnp.sum(key * key, axis=-1, keepdims=True) + 1e-06)
        query, key = query * query_norm, key * key_norm
        query_grad = left_grads[n][chunk:] * lift
        sunk = back_grads[n] * sink
        key_grad = left_grads[n][:chunk] * lift + rate * sunk
        rate_grad = jnp.sum(sunk * key, axis=-1, keepdims=True)
        query_grad_ref[span, at] = query_norm * (
            query_grad - query * jnp.sum(query * query_grad, axis=-1, keepdims=True)
        )
        key_grad_ref[span, at] = key_norm * (
            key_grad - key * jnp.sum(key * key_grad, axis=-1, keepdims=True)
        )
        rate_grad_ref[span, :] = jnp.where(lanes == first + h, rate_grad, rate_grad_ref[span, :])


def specs_of(tokens, width, chunk, heads_step, rate_heads):
    lanes = pl.BlockSpec((tokens, heads_step * width), lambda h: (0, h))
    rate = pl.BlockSpec((tokens, rate_heads), lambda h: (0, 0))
    square = pl.BlockSpec((heads_step, tokens, chunk), lambda h: (h, 0, 0))
    state = pl.BlockSpec((heads_step, width, width), lambda h: (h, 0, 0))
    return lanes, rate, square, state


def section_maps(queries, key_input, value_input, log_decay, write_rate, out_grad):
    tokens, heads = write_rate.shape
    width = queries.shape[1] // heads
    chunk = min(128, tokens)
    heads_step = 2 if heads % 2 == 0 else 1
    lanes, rate, square, state = specs_of(tokens, width, chunk, heads_step, heads)
    shape = jax.ShapeDtypeStruct
    return pl.pallas_call(
        functools.partial(maps_kernel, chunk, width, heads_step),
        grid=(heads // heads_step,),
        in_specs=[lanes, lanes, lanes, lanes, rate, lanes],
        out_specs=[state, state, state, lanes, lanes, lanes, lanes, square, square],
        out_shape=[shape((heads, width, width), F32)] * 3
        + [shape(queries.shape, F32)]
        + [shape(queries.shape, BF)] * 3
        + [shape((heads, tokens, chunk), BF)] * 2,
        compiler_params=pltpu.CompilerParams(vmem_limit_bytes=VMEM_BYTES),
        name="section_maps",
    )(queries, key_input, value_input, log_decay, write_rate, out_grad)


def section_grads(
    queries, key_input, value_input, write_rate, out_grad, saved, entry_state, exit_grad
):
    tokens, heads = write_rate.shape
    width = queries.shape[1] // heads
    chunk = min(128, tokens)
    heads_step = 2 if heads % 2 == 0 else 1
    lanes, rate, square, state = specs_of(tokens, width, chunk, heads_step, heads)
    shape = jax.ShapeDtypeStruct
    return pl.pallas_call(
        functools.partial(grads_kernel, chunk, width, heads_step),
        grid=(heads // heads_step,),
        in_specs=[lanes, lanes, lanes, rate, lanes]
        + [lanes] * 4
        + [square] * 2
        + [state] * 2,
        out_specs=[lanes, lanes, lanes, lanes, rate, state],
        out_shape=[shape(queries.shape, F32)] * 4
        + [shape((tokens, heads), F32), shape((heads, width, width), F32)],
        compiler_params=pltpu.CompilerParams(vmem_limit_bytes=VMEM_BYTES),
        name="section_grads",
    )(queries, key_input, value_input, write_rate, out_grad, *saved, entry_state, exit_grad)


def experts_kernel(
    capacity,
    part_width,
    sources,
    place_ref,
    *refs,
):
    row_refs, grad_refs = refs[:sources], refs[sources : 2 * sources]
    rest = refs[2 * sources :]
    gate_own, gate_far, up_own, up_far, down_own, down_far, out_own, out_far = rest[:8]
    gate_s, up_s, down_s, rows_s, grads_s, pieces_s, ranks_s, weights_s = rest[8:]
    step, steps = pl.program_id(0), pl.num_programs(0)
    mine = place_ref[0]
    head_at = place_ref[1]
    first = place_ref[2]
    tokens = row_refs[0].shape[0]
    parts, padded, hidden_width = gate_s.shape
    experts = ranks_s.shape[1]
    many = rows_s.shape[0]

    def choice(source, at):
        rank = ranks_s[source, pl.ds(at, 1), :]
        slot = lax.broadcasted_iota(jnp.int32, (capacity, tokens), 0).astype(F32)
        return slot == rank

    @pl.when(step == 0)
    def dispatch():
        gate_s[...] = jnp.zeros_like(gate_s)
        up_s[...] = jnp.zeros_like(up_s)
        down_s[...] = jnp.zeros_like(down_s)
        before = (places(tokens, 0) < places(tokens, 1)).astype(BF)
        for s in range(sources):
            start = part_width // 128 * 128
            tile = row_refs[s][:, start : start + 128].astype(F32)
            offset = part_width - start
            dense = jnp.transpose(tile)[offset : offset + experts]
            named = dense > 0.0
            rank = dot(named.astype(F32), before)
            ranks_s[s] = jnp.where(named, rank, -1.0)
            weights_s[s] = dense
            picks = [choice(s, first + e).astype(F32).astype(BF) for e in range(many)]
            pick = jnp.concatenate(picks, axis=0)
            rows = dot(pick, row_refs[s][...]).astype(BF)
            grads = dot(pick, grad_refs[s][...]).astype(BF)
            for e in range(many):
                rows_s[e, s * capacity : (s + 1) * capacity] = rows[e * capacity : (e + 1) * capacity]
                grads_s[e, s * capacity : (s + 1) * capacity] = grads[e * capacity : (e + 1) * capacity]

    for ref, own, far in ((gate_s, gate_own, gate_far), (up_s, up_own, up_far)):
        ref[mine, :part_width, :] = own[0]
        ref[1 - mine, :part_width, :] = far[0]
    down_s[mine, :, :part_width] = down_own[0]
    down_s[1 - mine, :, :part_width] = down_far[0]
    at = first + step
    gate_pre = up_pre = raw_grad = 0.0
    for p in range(parts):
        rows = rows_s[step, :, p * padded : (p + 1) * padded]
        grads = grads_s[step, :, p * padded : (p + 1) * padded]
        gate_pre = gate_pre + dot(rows, gate_s[p])
        up_pre = up_pre + dot(rows, up_s[p])
        raw_grad = raw_grad + dot_t(grads, down_s[p])
    weight = jnp.concatenate(
        [
            jnp.sum(
                jnp.where(choice(s, at), weights_s[s, pl.ds(at, 1), :], 0.0), axis=1, keepdims=True
            )
            for s in range(sources)
        ],
        axis=0,
    )
    sigmoid = jax.nn.sigmoid(gate_pre)
    activated = gate_pre * sigmoid
    hidden = (activated * up_pre).astype(BF).astype(F32)
    gate_part = jnp.sum(hidden * raw_grad, axis=1, keepdims=True)
    scaled = raw_grad * weight
    gate_back = (scaled * up_pre * sigmoid * (1.0 + gate_pre * (1.0 - sigmoid))).astype(BF)
    up_back = (scaled * activated).astype(BF)
    lanes = lax.broadcasted_iota(jnp.int32, (1, padded), 1)
    for p in range(parts):
        piece = dot_t(gate_back, gate_s[p]) + dot_t(up_back, up_s[p])
        piece = piece + jnp.where(lanes == part_width + at, gate_part, 0.0)
        piece = piece.astype(BF)
        for s in range(sources):
            pieces_s[s, p, step] = piece[s * capacity : (s + 1) * capacity]

    @pl.when(step == steps - 1)
    def combine():
        for s in range(sources):
            picks = [choice(s, first + e).astype(F32).astype(BF) for e in range(many)]
            pick = jnp.concatenate(picks, axis=0)
            out = out_own if s < sources // 2 else out_far
            for p in range(parts):
                flat = pieces_s[s, p].reshape(many * capacity, padded)
                place = lax.rem(head_at + p, parts)
                out[place, s % (sources // 2)] = tdot(pick, flat).astype(BF)


def expert_work(rows, grads, weights_own, weights_far, places_here, capacity, total_experts, parts):
    sources = len(rows)
    tokens, wide = rows[0].shape
    padded = wide // parts
    many = weights_far[0].shape[0]
    part_width, hidden_width = weights_own[0].shape[1:]
    token_spec = pl.BlockSpec((tokens, wide), lambda e, p: (0, 0))
    wide_own = pl.BlockSpec((1, part_width, hidden_width), lambda e, p: (p[3] + e, 0, 0))
    wide_far = pl.BlockSpec((1, part_width, hidden_width), lambda e, p: (e, 0, 0))
    down_own = pl.BlockSpec((1, hidden_width, part_width), lambda e, p: (p[3] + e, 0, 0))
    down_far = pl.BlockSpec((1, hidden_width, part_width), lambda e, p: (e, 0, 0))
    out_shape = (parts, sources // 2, tokens, padded)
    out_spec = pl.BlockSpec(out_shape, lambda e, p: (0, 0, 0, 0))
    slots = sources * capacity
    (gate_own, up_own, down_own_w), (gate_far, up_far, down_far_w) = weights_own, weights_far
    return pl.pallas_call(
        functools.partial(experts_kernel, capacity, part_width, sources),
        grid_spec=pltpu.PrefetchScalarGridSpec(
            num_scalar_prefetch=1,
            grid=(many,),
            in_specs=[token_spec] * (2 * sources)
            + [wide_own, wide_far, wide_own, wide_far, down_own, down_far],
            out_specs=[out_spec, out_spec],
            scratch_shapes=[
                pltpu.VMEM((parts, padded, hidden_width), BF),
                pltpu.VMEM((parts, padded, hidden_width), BF),
                pltpu.VMEM((parts, hidden_width, padded), BF),
                pltpu.VMEM((many, slots, wide), BF),
                pltpu.VMEM((many, slots, wide), BF),
                pltpu.VMEM((sources, parts, many, capacity, padded), BF),
                pltpu.VMEM((sources, total_experts, tokens), F32),
                pltpu.VMEM((sources, total_experts, tokens), F32),
            ],
        ),
        out_shape=[jax.ShapeDtypeStruct(out_shape, BF)] * 2,
        compiler_params=pltpu.CompilerParams(vmem_limit_bytes=60 * 1024 * 1024),
        name="expert_work",
    )(
        places_here, *rows, *grads,
        gate_own, gate_far, up_own, up_far, down_own_w, down_far_w,
    )


def swapped(x, axis):
    return lax.ppermute(x, axis, [(0, 1), (1, 0)])


def turned(x, axis, by):
    count = lax.axis_size(axis)
    return lax.ppermute(x, axis, [(i, (i + by) % count) for i in range(count)])


def shifted(x, axis, by):
    count = lax.axis_size(axis)
    pairs = [(i, i + by) for i in range(count) if 0 <= i + by < count]
    return lax.ppermute(x, axis, pairs)


def apply_map(transfer, carried, state):
    return (
        lax.dot_general(
            transfer.astype(BF),
            state.astype(BF),
            (((2,), (1,)), ((0,), (0,))),
            preferred_element_type=F32,
        )
        + carried
    )


def split_wide(matrix, parts, padded):
    rows, wide = matrix.shape
    cut = matrix.reshape(rows, parts, wide // parts)
    cut = jnp.pad(cut, ((0, 0), (0, 0), (0, padded - wide // parts)))
    return cut.reshape(rows, parts * padded)


def per_device(
    queries,
    key_input,
    value_input,
    log_decay,
    write_rate,
    start_state,
    out_grad,
    end_grad,
    moe_input,
    moe_grad,
    expert_ids,
    gate_weights,
    gate_matrix,
    up_matrix,
    down_matrix,
):
    sections = lax.axis_size("ctx")
    position = lax.axis_index("ctx")
    parts = lax.axis_size("fsdp")
    core = lax.axis_index("fsdp")
    head_count = lax.axis_size("head")
    head_at = lax.axis_index("head")

    token_count, top_count = expert_ids.shape
    experts_here = gate_matrix.shape[0]
    many = experts_here // parts
    total_experts = experts_here * sections
    capacity = 3 * token_count // 8
    part_width = gate_matrix.shape[1]
    padded = -(-(part_width + total_experts) // 128) * 128

    far_at = (1 - core) * many
    weights_far = [
        swapped(lax.dynamic_slice_in_dim(w, far_at, many, 0), "fsdp")
        for w in (gate_matrix, up_matrix, down_matrix)
    ]

    named = expert_ids[:, :, None] == lax.iota(jnp.int32, total_experts)[None, None, :]
    dense = jnp.sum(jnp.where(named, gate_weights[:, :, None], 0.0), axis=1).astype(BF)
    spare = jnp.zeros((token_count, padded - part_width - total_experts), BF)
    rows_own = jnp.concatenate(
        [
            moe_input[:, :part_width],
            dense,
            spare,
            split_wide(moe_input[:, part_width:], parts - 1, padded),
        ],
        axis=1,
    )
    grads_own = split_wide(moe_grad.astype(BF), parts, padded)
    rows_all = [rows_own] + [turned(rows_own, "ctx", s) for s in range(1, sections)]
    grads_all = [grads_own] + [turned(grads_own, "ctx", s) for s in range(1, sections)]
    rows_all = rows_all + [swapped(r, "fsdp") for r in rows_all]
    grads_all = grads_all + [swapped(r, "fsdp") for r in grads_all]

    transfer, carried, own_grad, *saved = section_maps(
        queries, key_input, value_input, log_decay, write_rate, out_grad
    )
    entry_state, exit_grad = start_state, end_grad
    backward = jnp.swapaxes(transfer, 1, 2)
    for _ in range(sections - 1):
        leaving = apply_map(transfer, carried, entry_state).astype(BF)
        entering = apply_map(backward, own_grad, exit_grad).astype(BF)
        arrived = shifted(leaving, "ctx", 1).astype(F32)
        arrived_grad = shifted(entering, "ctx", -1).astype(F32)
        entry_state = jnp.where(position == 0, start_state, arrived)
        exit_grad = jnp.where(position == sections - 1, end_grad, arrived_grad)

    places_here = jnp.stack(
        [core, head_at, position * experts_here + core * many, core * many]
    ).astype(jnp.int32)
    out_own, out_far = expert_work(
        rows_all,
        grads_all,
        (gate_matrix, up_matrix, down_matrix),
        weights_far,
        places_here,
        capacity,
        total_experts,
        parts,
    )
    gradients = section_grads(
        queries, key_input, value_input, write_rate, out_grad, saved, entry_state, exit_grad
    )

    summed = out_own.astype(F32) + swapped(out_far, "fsdp").astype(F32)
    if head_count == parts:
        summed = summed[0] + swapped(summed[1].astype(BF), "head").astype(F32)
        pieces = summed.astype(BF)
        back = pieces[0].astype(F32)
        for s in range(1, sections):
            back = back + turned(pieces[s], "ctx", sections - s).astype(F32)
        input_grads = back[:, :part_width]
        gates = back[:, part_width : part_width + total_experts]
    else:
        order = (jnp.arange(parts) + head_at) % parts
        summed = summed[order].astype(BF)
        wide = jnp.concatenate([summed[p, :, :, :part_width] for p in range(parts)], axis=-1)
        wide = lax.psum_scatter(wide, "head", scatter_dimension=2, tiled=True)
        gates = lax.psum(summed[0, :, :, part_width : part_width + total_experts], "head")
        pieces = jnp.concatenate([wide, gates], axis=-1)
        back = pieces[0].astype(F32)
        for s in range(1, sections):
            back = back + turned(pieces[s], "ctx", sections - s).astype(F32)
        input_grads = back[:, : wide.shape[-1]]
        gates = back[:, wide.shape[-1] :]
    slots_here = top_count // head_count
    ids_here = lax.dynamic_slice_in_dim(expert_ids, head_at * slots_here, slots_here, 1)
    named = ids_here[:, :, None] == lax.iota(jnp.int32, total_experts)[None, None, :]
    gate_grads = jnp.sum(jnp.where(named, gates[:, None, :], 0.0), axis=-1)
    return (*gradients[:5], gradients[5][None], input_grads, gate_grads)


def solution(mesh):
    in_specs = (
        P(("groups", "ctx"), ("head", "fsdp")),
        P(("groups", "ctx"), ("head", "fsdp")),
        P(("groups", "ctx"), ("head", "fsdp")),
        P(("groups", "ctx"), ("head", "fsdp")),
        P(("groups", "ctx"), ("head", "fsdp")),
        P(("groups", "head", "fsdp"), None, None),
        P(("groups", "ctx"), ("head", "fsdp")),
        P(("groups", "head", "fsdp"), None, None),
        P(("groups", "ctx", "fsdp"), None),
        P(("groups", "ctx", "fsdp"), None),
        P(("groups", "ctx", "fsdp"), None),
        P(("groups", "ctx", "fsdp"), None),
        P("ctx", "fsdp", "head"),
        P("ctx", "fsdp", "head"),
        P("ctx", "head", "fsdp"),
    )
    out_specs = (
        P(("groups", "ctx"), ("head", "fsdp")),
        P(("groups", "ctx"), ("head", "fsdp")),
        P(("groups", "ctx"), ("head", "fsdp")),
        P(("groups", "ctx"), ("head", "fsdp")),
        P(("groups", "ctx"), ("head", "fsdp")),
        P(("groups", "ctx"), ("head", "fsdp"), None, None),
        P(("groups", "ctx", "fsdp"), "head"),
        P(("groups", "ctx", "fsdp"), "head"),
    )
    return jax.shard_map(
        per_device, mesh=mesh, in_specs=in_specs, out_specs=out_specs, check_vma=False
    )
```

time: 1340 us -> 194 us (0.14); the launches traced: 1320 us -> 193 us
  other arithmetic: 754 us -> 4.14 us
  matrix products: 192 us -> 5 us
  waiting for transfers between devices: 162 us -> 60.7 us
  local copies, waits for them, and re-layouts: 128 us -> 28.9 us
  Pallas kernels: 0 us -> 51 us
  starting transfers between devices: 60.5 us -> 42.4 us
  between operations: 15.5 us -> 1.06 us
    another operation x87 -> x1, other arithmetic: 711 us -> 0.61 us  [per_device(): jnp.stack([core, head_at, position * experts_here + core * many, core * m...]
    dot_general x123 -> x6, matrix products: 172 us -> 5 us  [apply_map(): lax.dot_general(transfer.astype(BF), state.astype(BF), (((2,), (1,)), ((0...]
    ppermute x6, waiting for transfers between devices: 159 us -> 6.94 us  [shifted(): return lax.ppermute(x, axis, pairs)]
    ppermute x0 -> x22, waiting for transfers between devices: none -> 53.8 us  [the longest x9 46.7 us: turned(): return lax.ppermute(x, axis, [(i, (i + by) % count) for i in range(count)])]
    pallas_call x0 -> x3, Pallas kernels: none -> 51 us  [the longest x1 25.1 us: expert_work(): pl.pallas_call(functools.partial(experts_kernel, capacity, part_width, so...]
    squeeze x36 -> x1, local copies, waits for them, and re-layouts: 26.9 us -> 0.76 us  [per_device(): back = back + turned(pieces[s], 'ctx', sections - s).astype(F32)]
    all_to_all x5 -> x0, starting transfers between devices: 25.6 us -> none  [the longest x1 6.32 us: per_device(): lax.all_to_all(send_weights.astype(jnp.bfloat16), 'ctx', split_axis=0, co...]
    ppermute x0 -> x22, starting transfers between devices: none -> 23.6 us  [the longest x9 19.4 us: turned(): return lax.ppermute(x, axis, [(i, (i + by) % count) for i in range(count)])]
  transfers between devices with their start and end apart: 15 -> 28, of which waited for: 6 -> 13; matrix products, arithmetic and copies ran while one was open for 77% -> 14% of each run, Pallas kernels for 0% -> 13%
where the time goes in v1:
time: 194 us; the launch traced here: 193 us
  waiting for transfers between devices  60.7 us (31%)
  Pallas kernels  51 us (26%)
  starting transfers between devices  42.4 us (22%)
  local copies, waits for them, and re-layouts  28.9 us (15%)
  matrix products  5 us (3%)
  other arithmetic  4.14 us (2%)
    ppermute x9, waiting for transfers between devices, turned(): return lax.ppermute(x, axis, [(i, (i + by) % count) for i in range(count)])  46.7 us
    pallas_call x1, Pallas kernels, expert_work(): pl.pallas_call(functools.partial(experts_kernel, capacity, part_width, so...  25.1 us
    ppermute x9, starting transfers between devices, turned(): return lax.ppermute(x, axis, [(i, (i + by) % count) for i in range(count)])  19.4 us
    ppermute x6, starting transfers between devices, shifted(): return lax.ppermute(x, axis, pairs)  18.7 us
    unnamed x49, local copies, waits for them, and re-layouts  16.4 us
    pallas_call x1, Pallas kernels, section_maps(): pl.pallas_call(functools.partial(maps_kernel, chunk, width, heads_step),...  13.9 us
    pallas_call x1, Pallas kernels, section_grads(): pl.pallas_call(functools.partial(grads_kernel, chunk, width, heads_step),...  12 us
    ppermute x13, waiting for transfers between devices, swapped(): return lax.ppermute(x, axis, [(0, 1), (1, 0)])  7.13 us
  transfers between devices with their start and end apart: 28, of which 13 were waited for; matrix products, arithmetic and copies ran while one was open for 14% of the time, Pallas kernels for 13%

profile of v1, /device:TPU:0, one launch (start us, length us, event | category | flops | bytes accessed | tf_op | source)
XLA Modules:
  0.0 193.2 jit_solution(12049803608246410355)
XLA Ops:
  0.7 3.4 %constant_dynamic-slice_fusion.1 = bf16[4,512,576]{1,2,0:T(8,128)(2,1)} fusion(bf16[8,512,576]{1,2,0:T(8,128)(2,1)} %param.29, s32[]{:T(128)S(6)} %select_n.55), kind=kLoop, calls=%fused_computation.44 | loop fusion | bytes 4718596 | tf_op jit(solution)/shard_map/dynamic_slice | solution.py:550
  7.2 1.6 constant_dynamic-slice_fusion.2
  9.8 2.6 %collective-permute-start.6 = (bf16[128,1280]{1,0:T(8,128)(2,1)S(1)}, bf16[128,1280]{1,0:T(8,128)(2,1)S(1)}, u32[]{:S(2)}, u32[]{:S(2)}) collective-permute-start(bf16[128,1280]{1,0:T(8,128)(2,1)S(1)} %concatenate.3.refs_0_), channel_id=1, source_target_pairs={{0,4},{4,8},{8,12},{12,0},{1,5},{5,9},{9,13},{13,1},{2,6},{6,10},{... | collective-permute-start | bytes 983048 | tf_op jit(solution)/shard_map/ppermute | solution.py:488
  12.4 2.6 %collective-permute-start.7 = (bf16[128,1280]{1,0:T(8,128)(2,1)S(1)}, bf16[128,1280]{1,0:T(8,128)(2,1)}, u32[]{:S(2)}, u32[]{:S(2)}) collective-permute-start(bf16[128,1280]{1,0:T(8,128)(2,1)S(1)} %concatenate.3.refs_0_), channel_id=1, source_target_pairs={{0,8},{4,12},{8,0},{12,4},{1,9},{5,13},{9,1},{13,5},{2,10},{6,14},... | collective-permute-start | bytes 983048 | tf_op jit(solution)/shard_map/ppermute | solution.py:488
  15.0 8.1 %collective-permute-done.6.refs_1_ = bf16[128,1280]{1,0:T(8,128)(2,1)S(1)} collective-permute-done((bf16[128,1280]{1,0:T(8,128)(2,1)S(1)}, bf16[128,1280]{1,0:T(8,128)(2,1)S(1)}, u32[]{:S(2)}, u32[]{:S(2)}) %collective-permute-start.6) | collective-permute-done | bytes 327712 | tf_op jit(solution)/shard_map/ppermute | solution.py:488
  26.9 10.1 %collective-permute-done.7.refs_2_ = bf16[128,1280]{1,0:T(8,128)(2,1)} collective-permute-done((bf16[128,1280]{1,0:T(8,128)(2,1)S(1)}, bf16[128,1280]{1,0:T(8,128)(2,1)}, u32[]{:S(2)}, u32[]{:S(2)}) %collective-permute-start.7) | collective-permute-done | bytes 327712 | tf_op jit(solution)/shard_map/ppermute | solution.py:488
  37.0 4.8 %collective-permute-done.8.refs_3_ = bf16[128,1280]{1,0:T(8,128)(2,1)} collective-permute-done((bf16[128,1280]{1,0:T(8,128)(2,1)S(1)}, bf16[128,1280]{1,0:T(8,128)(2,1)}, u32[]{:S(2)}, u32[]{:S(2)}) %collective-permute-start.8) | collective-permute-done | bytes 327712 | tf_op jit(solution)/shard_map/ppermute | solution.py:488
  41.8 2.8 %collective-permute-start.13 = (bf16[128,1280]{1,0:T(8,128)(2,1)S(1)}, bf16[128,1280]{1,0:T(8,128)(2,1)}, u32[]{:S(2)}, u32[]{:S(2)}) collective-permute-start(bf16[128,1280]{1,0:T(8,128)(2,1)S(1)} %copy.88.refs_8_), channel_id=1, source_target_pairs={{0,4},{4,8},{8,12},{12,0},{1,5},{5,9},{9,13},{13,1},{2,6},{6,10},{... | collective-permute-start | bytes 983048 | tf_op jit(solution)/shard_map/ppermute | solution.py:488
  46.2 8.2 %collective-permute-done.13.refs_9_ = bf16[128,1280]{1,0:T(8,128)(2,1)} collective-permute-done((bf16[128,1280]{1,0:T(8,128)(2,1)S(1)}, bf16[128,1280]{1,0:T(8,128)(2,1)}, u32[]{:S(2)}, u32[]{:S(2)}) %collective-permute-start.13) | collective-permute-done | bytes 327712 | tf_op jit(solution)/shard_map/ppermute | solution.py:488
  54.4 3.4 %collective-permute-start.15 = (bf16[128,1280]{1,0:T(8,128)(2,1)S(1)}, bf16[128,1280]{1,0:T(8,128)(2,1)}, u32[]{:S(2)}, u32[]{:S(2)}) collective-permute-start(bf16[128,1280]{1,0:T(8,128)(2,1)S(1)} %copy.88.refs_8_), channel_id=1, source_target_pairs={{0,12},{4,0},{8,4},{12,8},{1,13},{5,1},{9,5},{13,9},{2,14},{6,2},{... | collective-permute-start | bytes 983048 | tf_op jit(solution)/shard_map/ppermute | solution.py:488
  57.8 10.4 %collective-permute-done.14.refs_10_ = bf16[128,1280]{1,0:T(8,128)(2,1)} collective-permute-done((bf16[128,1280]{1,0:T(8,128)(2,1)S(1)}, bf16[128,1280]{1,0:T(8,128)(2,1)}, u32[]{:S(2)}, u32[]{:S(2)}) %collective-permute-start.14) | collective-permute-done | bytes 327712 | tf_op jit(solution)/shard_map/ppermute | solution.py:488
  68.2 5.0 %collective-permute-done.15.refs_11_ = bf16[128,1280]{1,0:T(8,128)(2,1)} collective-permute-done((bf16[128,1280]{1,0:T(8,128)(2,1)S(1)}, bf16[128,1280]{1,0:T(8,128)(2,1)}, u32[]{:S(2)}, u32[]{:S(2)}) %collective-permute-start.15) | collective-permute-done | bytes 327712 | tf_op jit(solution)/shard_map/ppermute | solution.py:488
  77.7 7.7 %copy.80.refs_20_ = bf16[8,512,576]{2,1,0:T(8,128)(2,1)} copy(bf16[8,512,576]{1,2,0:T(8,128)(2,1)} %param.29) | data formatting | bytes 9437184 | tf_op args[14]
  86.1 4.4 %copy.81.refs_21_ = bf16[4,512,576]{2,1,0:T(8,128)(2,1)} copy(bf16[4,512,576]{1,2,0:T(8,128)(2,1)} %collective-permute-done.22) | data formatting | bytes 4718592 | tf_op jit(solution)/shard_map/ppermute | solution.py:483
  91.9 25.1 %expert_work.1 = (bf16[2,4,128,640]{3,2,1,0:T(8,128)(2,1)}, bf16[2,4,128,640]{3,2,1,0:T(8,128)(2,1)}) custom-call(s32[4]{0:T(128)} %pad_add_fusion.place_ref, bf16[128,1280]{1,0:T(8,128)(2,1)} %copy-done.13, bf16[128,1280]{1,0:T(8,128)(2,1)} %copy-done.16, bf16[128,1280]{1,0:T(8,128)(2,1)} %collective-permute-done.7.refs_2_, ...), custom_call_target="tpu_custom_call" | custom-call | tf_op jit(solution)/shard_map/expert_work/pallas_call | solution.py:454
  117.4 13.9 %section_maps.1 = (f32[8,128,128]{2,1,0:T(8,128)S(1)}, f32[8,128,128]{2,1,0:T(8,128)S(1)}, f32[8,128,128]{2,1,0:T(8,128)S(1)}, f32[256,1024]{1,0:T(8,128)S(1)}, ...) custom-call(f32[256,1024]{1,0:T(8,128)} %query_ref.3, ...), custom_call_target="tpu_custom_call" | custom-call | tf_op jit(solution)/shard_map/section_maps/pallas_call | solution.py:304
  136.3 5.9 %collective-permute-start = (bf16[8,128,128]{2,1,0:T(8,128)(2,1)}, bf16[8,128,128]{2,1,0:T(8,128)(2,1)}, u32[]{:S(2)}, u32[]{:S(2)}) collective-permute-start(bf16[8,128,128]{2,1,0:T(8,128)(2,1)} %fusion.2), channel_id=1, source_target_pairs={{0,4},{4,8},{8,12},{1,5},{5,9},{9,13},{2,6},{6,10},{10,14},{3,7},{... | collective-permute-start | bytes 786440 | tf_op jit(solution)/shard_map/ppermute | solution.py:494
  142.2 3.6 %collective-permute-done.3 = bf16[8,128,128]{2,1,0:T(8,128)(2,1)} collective-permute-done((bf16[8,128,128]{2,1,0:T(8,128)(2,1)}, bf16[8,128,128]{2,1,0:T(8,128)(2,1)}, u32[]{:S(2)}, u32[]{:S(2)}) %collective-permute-start.3) | collective-permute-done | bytes 262176 | tf_op jit(solution)/shard_map/ppermute | solution.py:494
  149.6 4.6 %collective-permute-start.1 = (bf16[8,128,128]{2,1,0:T(8,128)(2,1)S(1)}, bf16[8,128,128]{2,1,0:T(8,128)(2,1)S(1)}, u32[]{:S(2)}, u32[]{:S(2)}) collective-permute-start(bf16[8,128,128]{2,1,0:T(8,128)(2,1)S(1)} %fusion.3), channel_id=1, source_target_pairs={{0,4},{4,8},{8,12},{1,5},{5,9},{9,13},{2,6},{6,10},{10,14},{3,7},{... | collective-permute-start | bytes 786440 | tf_op jit(solution)/shard_map/ppermute | solution.py:494
  159.7 4.4 %collective-permute-start.2 = (bf16[8,128,128]{2,1,0:T(8,128)(2,1)S(1)}, bf16[8,128,128]{2,1,0:T(8,128)(2,1)S(1)}, u32[]{:S(2)}, u32[]{:S(2)}) collective-permute-start(bf16[8,128,128]{2,1,0:T(8,128)(2,1)S(1)} %fusion.4), channel_id=1, source_target_pairs={{0,4},{4,8},{8,12},{1,5},{5,9},{9,13},{2,6},{6,10},{10,14},{3,7},{... | collective-permute-start | bytes 786440 | tf_op jit(solution)/shard_map/ppermute | solution.py:494
  164.1 3.0 %collective-permute-done.5 = bf16[8,128,128]{2,1,0:T(8,128)(2,1)S(1)} collective-permute-done((bf16[8,128,128]{2,1,0:T(8,128)(2,1)S(1)}, bf16[8,128,128]{2,1,0:T(8,128)(2,1)S(1)}, u32[]{:S(2)}, u32[]{:S(2)}) %collective-permute-start.5) | collective-permute-done | bytes 262176 | tf_op jit(solution)/shard_map/ppermute | solution.py:494
  167.3 4.9 %collective-permute-done.24 = bf16[4,128,640]{2,1,0:T(8,128)(2,1)S(1)} collective-permute-done((bf16[4,128,640]{2,1,0:T(8,128)(2,1)S(1)}, bf16[4,128,640]{2,1,0:T(8,128)(2,1)S(1)}, u32[]{:S(2)}, u32[]{:S(2)}) %collective-permute-start.24) | collective-permute-done | bytes 655392 | tf_op jit(solution)/shard_map/ppermute | solution.py:483
  173.1 1.8 collective-permute-start.25
  177.9 12.0 %section_grads.1 = (f32[256,1024]{1,0:T(8,128)}, f32[256,1024]{1,0:T(8,128)}, f32[256,1024]{1,0:T(8,128)}, f32[256,1024]{1,0:T(8,128)}, f32[256,8]{1,0:T(8,128)S(1)}, /*index=5*/f32[8,128,128]{2,1,0:T(8,128)}) custom-call(f32[256,1024]{1,0:T(8,128)S(1)} %copy-done, f32[256,1024]{1,0:T(8,128)S(1)} %copy-done.1, f32[256,1024]{1,0:T(8,128)} %value_ref.3, ...), custom_call_target="tpu_custom_call" | custom-call | tf_op jit(solution)/shard_map/section_grads/pallas_call | solution.py:327
  (115 shorter events, 37.8 us)
Async XLA Ops:
  4.1 73.3 %collective-permute-start.22 = (bf16[4,512,576]{1,2,0:T(8,128)(2,1)}, bf16[4,512,576]{1,2,0:T(8,128)(2,1)}, u32[]{:S(2)}, u32[]{:S(2)}) collective-permute-start(bf16[4,512,576]{1,2,0:T(8,128)(2,1)} %constant_dynamic-slice_fusion.1), channel_id=1, source_target_pairs={{0,1},{1,0},{2,3},{3,2},{4,5},{5,4},{6,7},{7,6},{8,9},{9,8},{10,11... | collective-permute-start | bytes 7077896 | tf_op jit(solution)/shard_map/ppermute | solution.py:483
  6.1 84.4 %collective-permute-start.20 = (bf16[4,576,512]{2,1,0:T(8,128)(2,1)}, bf16[4,576,512]{2,1,0:T(8,128)(2,1)S(1)}, u32[]{:S(2)}, u32[]{:S(2)}) collective-permute-start(bf16[4,576,512]{2,1,0:T(8,128)(2,1)} %constant_dynamic-slice_fusion.3), channel_id=1, source_target_pairs={{0,1},{1,0},{2,3},{3,2},{4,5},{5,4},{6,7},{7,6},{8,9},{9,8},{10,11... | collective-permute-start | bytes 7077896 | tf_op jit(solution)/shard_map/ppermute | solution.py:483
  8.9 81.6 %collective-permute-start.21 = (bf16[4,576,512]{2,1,0:T(8,128)(2,1)}, bf16[4,576,512]{2,1,0:T(8,128)(2,1)}, u32[]{:S(2)}, u32[]{:S(2)}) collective-permute-start(bf16[4,576,512]{2,1,0:T(8,128)(2,1)} %constant_dynamic-slice_fusion.2), channel_id=1, source_target_pairs={{0,1},{1,0},{2,3},{3,2},{4,5},{5,4},{6,7},{7,6},{8,9},{9,8},{10,11... | collective-permute-start | bytes 7077896 | tf_op jit(solution)/shard_map/ppermute | solution.py:483
  9.8 13.3 %collective-permute-start.6 = (bf16[128,1280]{1,0:T(8,128)(2,1)S(1)}, bf16[128,1280]{1,0:T(8,128)(2,1)S(1)}, u32[]{:S(2)}, u32[]{:S(2)}) collective-permute-start(bf16[128,1280]{1,0:T(8,128)(2,1)S(1)} %concatenate.3.refs_0_), channel_id=1, source_target_pairs={{0,4},{4,8},{8,12},{12,0},{1,5},{5,9},{9,13},{13,1},{2,6},{6,10},{... | collective-permute-start | bytes 983048 | tf_op jit(solution)/shard_map/ppermute | solution.py:488
  12.4 24.6 %collective-permute-start.7 = (bf16[128,1280]{1,0:T(8,128)(2,1)S(1)}, bf16[128,1280]{1,0:T(8,128)(2,1)}, u32[]{:S(2)}, u32[]{:S(2)}) collective-permute-start(bf16[128,1280]{1,0:T(8,128)(2,1)S(1)} %concatenate.3.refs_0_), channel_id=1, source_target_pairs={{0,8},{4,12},{8,0},{12,4},{1,9},{5,13},{9,1},{13,5},{2,10},{6,14},... | collective-permute-start | bytes 983048 | tf_op jit(solution)/shard_map/ppermute | solution.py:488
  23.8 18.0 %collective-permute-start.8 = (bf16[128,1280]{1,0:T(8,128)(2,1)S(1)}, bf16[128,1280]{1,0:T(8,128)(2,1)}, u32[]{:S(2)}, u32[]{:S(2)}) collective-permute-start(bf16[128,1280]{1,0:T(8,128)(2,1)S(1)} %concatenate.3.refs_0_), channel_id=1, source_target_pairs={{0,12},{4,0},{8,4},{12,8},{1,13},{5,1},{9,5},{13,9},{2,14},{6,2},{... | collective-permute-start | bytes 983048 | tf_op jit(solution)/shard_map/ppermute | solution.py:488
  37.0 7.5 %collective-permute-start.9 = (bf16[128,1280]{1,0:T(8,128)(2,1)S(1)}, bf16[128,1280]{1,0:T(8,128)(2,1)S(1)}, u32[]{:S(2)}, u32[]{:S(2)}) collective-permute-start(bf16[128,1280]{1,0:T(8,128)(2,1)S(1)} %concatenate.3.refs_0_), channel_id=1, source_target_pairs={{0,1},{1,0},{2,3},{3,2},{4,5},{5,4},{6,7},{7,6},{8,9},{9,8},{10,11... | collective-permute-start | bytes 983048 | tf_op jit(solution)/shard_map/ppermute | solution.py:483
  41.8 12.6 %collective-permute-start.13 = (bf16[128,1280]{1,0:T(8,128)(2,1)S(1)}, bf16[128,1280]{1,0:T(8,128)(2,1)}, u32[]{:S(2)}, u32[]{:S(2)}) collective-permute-start(bf16[128,1280]{1,0:T(8,128)(2,1)S(1)} %copy.88.refs_8_), channel_id=1, source_target_pairs={{0,4},{4,8},{8,12},{12,0},{1,5},{5,9},{9,13},{13,1},{2,6},{6,10},{... | collective-permute-start | bytes 983048 | tf_op jit(solution)/shard_map/ppermute | solution.py:488
  44.6 23.7 %collective-permute-start.14 = (bf16[128,1280]{1,0:T(8,128)(2,1)S(1)}, bf16[128,1280]{1,0:T(8,128)(2,1)}, u32[]{:S(2)}, u32[]{:S(2)}) collective-permute-start(bf16[128,1280]{1,0:T(8,128)(2,1)S(1)} %copy.88.refs_8_), channel_id=1, source_target_pairs={{0,8},{4,12},{8,0},{12,4},{1,9},{5,13},{9,1},{13,5},{2,10},{6,14},... | collective-permute-start | bytes 983048 | tf_op jit(solution)/shard_map/ppermute | solution.py:488
  54.4 18.9 %collective-permute-start.15 = (bf16[128,1280]{1,0:T(8,128)(2,1)S(1)}, bf16[128,1280]{1,0:T(8,128)(2,1)}, u32[]{:S(2)}, u32[]{:S(2)}) collective-permute-start(bf16[128,1280]{1,0:T(8,128)(2,1)S(1)} %copy.88.refs_8_), channel_id=1, source_target_pairs={{0,12},{4,0},{8,4},{12,8},{1,13},{5,1},{9,5},{13,9},{2,14},{6,2},{... | collective-permute-start | bytes 983048 | tf_op jit(solution)/shard_map/ppermute | solution.py:488
  76.1 14.4 %collective-permute-start.17 = (bf16[128,1280]{1,0:T(8,128)(2,1)}, bf16[128,1280]{1,0:T(8,128)(2,1)}, u32[]{:S(2)}, u32[]{:S(2)}) collective-permute-start(bf16[128,1280]{1,0:T(8,128)(2,1)} %collective-permute-done.13.refs_9_), channel_id=1, source_target_pairs={{0,1},{1,0},{2,3},{3,2},{4,5},{5,4},{6,7},{7,6},{8,9},{9,8},{10,11... | collective-permute-start | bytes 983048 | tf_op jit(solution)/shard_map/ppermute | solution.py:483
  77.2 13.3 %collective-permute-start.18 = (bf16[128,1280]{1,0:T(8,128)(2,1)}, bf16[128,1280]{1,0:T(8,128)(2,1)}, u32[]{:S(2)}, u32[]{:S(2)}) collective-permute-start(bf16[128,1280]{1,0:T(8,128)(2,1)} %collective-permute-done.14.refs_10_), channel_id=1, source_target_pairs={{0,1},{1,0},{2,3},{3,2},{4,5},{5,4},{6,7},{7,6},{8,9},{9,8},{10,11... | collective-permute-start | bytes 983048 | tf_op jit(solution)/shard_map/ppermute | solution.py:483
  77.4 13.1 %collective-permute-start.19 = (bf16[128,1280]{1,0:T(8,128)(2,1)}, bf16[128,1280]{1,0:T(8,128)(2,1)}, u32[]{:S(2)}, u32[]{:S(2)}) collective-permute-start(bf16[128,1280]{1,0:T(8,128)(2,1)} %collective-permute-done.15.refs_11_), channel_id=1, source_target_pairs={{0,1},{1,0},{2,3},{3,2},{4,5},{5,4},{6,7},{7,6},{8,9},{9,8},{10,11... | collective-permute-start | bytes 983048 | tf_op jit(solution)/shard_map/ppermute | solution.py:483
  117.0 37.2 %collective-permute-start.23 = (bf16[2,4,128,640]{3,2,1,0:T(8,128)(2,1)}, bf16[2,4,128,640]{3,2,1,0:T(8,128)(2,1)}, u32[]{:S(2)}, u32[]{:S(2)}) collective-permute-start(bf16[2,4,128,640]{3,2,1,0:T(8,128)(2,1)} %get-tuple-element.41), channel_id=1, source_target_pairs={{0,1},{1,0},{2,3},{3,2},{4,5},{5,4},{6,7},{7,6},{8,9},{9,8},{10,11... | collective-permute-start | bytes 3932168 | tf_op jit(solution)/shard_map/ppermute | solution.py:483
  134.0 11.7 %collective-permute-start.3 = (bf16[8,128,128]{2,1,0:T(8,128)(2,1)}, bf16[8,128,128]{2,1,0:T(8,128)(2,1)}, u32[]{:S(2)}, u32[]{:S(2)}) collective-permute-start(bf16[8,128,128]{2,1,0:T(8,128)(2,1)} %fusion.5), channel_id=1, source_target_pairs={{4,0},{8,4},{12,8},{5,1},{9,5},{13,9},{6,2},{10,6},{14,10},{7,3},{... | collective-permute-start | bytes 786440 | tf_op jit(solution)/shard_map/ppermute | solution.py:494
  136.3 12.0 %collective-permute-start = (bf16[8,128,128]{2,1,0:T(8,128)(2,1)}, bf16[8,128,128]{2,1,0:T(8,128)(2,1)}, u32[]{:S(2)}, u32[]{:S(2)}) collective-permute-start(bf16[8,128,128]{2,1,0:T(8,128)(2,1)} %fusion.2), channel_id=1, source_target_pairs={{0,4},{4,8},{8,12},{1,5},{5,9},{9,13},{2,6},{6,10},{10,14},{3,7},{... | collective-permute-start | bytes 786440 | tf_op jit(solution)/shard_map/ppermute | solution.py:494
  147.0 10.6 %collective-permute-start.4 = (bf16[8,128,128]{2,1,0:T(8,128)(2,1)S(1)}, bf16[8,128,128]{2,1,0:T(8,128)(2,1)S(1)}, u32[]{:S(2)}, u32[]{:S(2)}) collective-permute-start(bf16[8,128,128]{2,1,0:T(8,128)(2,1)S(1)} %fusion.6), channel_id=1, source_target_pairs={{4,0},{8,4},{12,8},{5,1},{9,5},{13,9},{6,2},{10,6},{14,10},{7,3},{... | collective-permute-start | bytes 786440 | tf_op jit(solution)/shard_map/ppermute | solution.py:494
  149.6 9.9 %collective-permute-start.1 = (bf16[8,128,128]{2,1,0:T(8,128)(2,1)S(1)}, bf16[8,128,128]{2,1,0:T(8,128)(2,1)S(1)}, u32[]{:S(2)}, u32[]{:S(2)}) collective-permute-start(bf16[8,128,128]{2,1,0:T(8,128)(2,1)S(1)} %fusion.3), channel_id=1, source_target_pairs={{0,4},{4,8},{8,12},{1,5},{5,9},{9,13},{2,6},{6,10},{10,14},{3,7},{... | collective-permute-start | bytes 786440 | tf_op jit(solution)/shard_map/ppermute | solution.py:494
  156.0 16.2 %collective-permute-start.24 = (bf16[4,128,640]{2,1,0:T(8,128)(2,1)S(1)}, bf16[4,128,640]{2,1,0:T(8,128)(2,1)S(1)}, u32[]{:S(2)}, u32[]{:S(2)}) collective-permute-start(bf16[4,128,640]{2,1,0:T(8,128)(2,1)S(1)} %fusion.8), channel_id=1, source_target_pairs={{0,2},{2,0},{1,3},{3,1},{4,6},{6,4},{5,7},{7,5},{8,10},{10,8},{9,1... | collective-permute-start | bytes 1966088 | tf_op jit(solution)/shard_map/ppermute | solution.py:483
  157.8 9.3 %collective-permute-start.5 = (bf16[8,128,128]{2,1,0:T(8,128)(2,1)S(1)}, bf16[8,128,128]{2,1,0:T(8,128)(2,1)S(1)}, u32[]{:S(2)}, u32[]{:S(2)}) collective-permute-start(bf16[8,128,128]{2,1,0:T(8,128)(2,1)S(1)} %fusion.7), channel_id=1, source_target_pairs={{4,0},{8,4},{12,8},{5,1},{9,5},{13,9},{6,2},{10,6},{14,10},{7,3},{... | collective-permute-start | bytes 786440 | tf_op jit(solution)/shard_map/ppermute | solution.py:494
  159.7 18.1 %collective-permute-start.2 = (bf16[8,128,128]{2,1,0:T(8,128)(2,1)S(1)}, bf16[8,128,128]{2,1,0:T(8,128)(2,1)S(1)}, u32[]{:S(2)}, u32[]{:S(2)}) collective-permute-start(bf16[8,128,128]{2,1,0:T(8,128)(2,1)S(1)} %fusion.4), channel_id=1, source_target_pairs={{0,4},{4,8},{8,12},{1,5},{5,9},{9,13},{2,6},{6,10},{10,14},{3,7},{... | collective-permute-start | bytes 786440 | tf_op jit(solution)/shard_map/ppermute | solution.py:494
  173.1 17.5 %collective-permute-start.25 = (bf16[128,640]{1,0:T(8,128)(2,1)}, bf16[128,640]{1,0:T(8,128)(2,1)S(1)}, u32[]{:S(2)}, u32[]{:S(2)}) collective-permute-start(bf16[128,640]{1,0:T(8,128)(2,1)} %get-tuple-element.82), channel_id=1, source_target_pairs={{0,12},{4,0},{8,4},{12,8},{1,13},{5,1},{9,5},{13,9},{2,14},{6,2},{... | collective-permute-start | bytes 491528 | tf_op jit(solution)/shard_map/ppermute | solution.py:488
  174.9 15.7 %collective-permute-start.26 = (bf16[128,640]{1,0:T(8,128)(2,1)}, bf16[128,640]{1,0:T(8,128)(2,1)S(1)}, u32[]{:S(2)}, u32[]{:S(2)}) collective-permute-start(bf16[128,640]{1,0:T(8,128)(2,1)} %get-tuple-element.84), channel_id=1, source_target_pairs={{0,8},{4,12},{8,0},{12,4},{1,9},{5,13},{9,1},{13,5},{2,10},{6,14},... | collective-permute-start | bytes 491528 | tf_op jit(solution)/shard_map/ppermute | solution.py:488
  176.3 14.3 %collective-permute-start.27 = (bf16[128,640]{1,0:T(8,128)(2,1)S(1)}, bf16[128,640]{1,0:T(8,128)(2,1)}, u32[]{:S(2)}, u32[]{:S(2)}) collective-permute-start(bf16[128,640]{1,0:T(8,128)(2,1)S(1)} %get-tuple-element.83), channel_id=1, source_target_pairs={{0,4},{4,8},{8,12},{12,0},{1,5},{5,9},{9,13},{13,1},{2,6},{6,10},{... | collective-permute-start | bytes 491528 | tf_op jit(solution)/shard_map/ppermute | solution.py:488
  (26 other events, 303.7 us)

commit v2 on v1

v2 whole, which is shorter than its diff:
```python
import functools

import jax
import jax.numpy as jnp
from jax import lax
from jax.experimental import pallas as pl
from jax.experimental.pallas import tpu as pltpu
from jax.sharding import PartitionSpec as P

BF = jnp.bfloat16
F32 = jnp.float32
VMEM_BYTES = 62 * 1024 * 1024


def dot(a, b):
    return lax.dot_general(
        a.astype(BF), b.astype(BF), (((1,), (0,)), ((), ())), preferred_element_type=F32
    )


def dot_t(a, b):
    return lax.dot_general(
        a.astype(BF), b.astype(BF), (((1,), (1,)), ((), ())), preferred_element_type=F32
    )


def tdot(a, b):
    return lax.dot_general(
        a.astype(BF), b.astype(BF), (((0,), (0,)), ((), ())), preferred_element_type=F32
    )


def halves(x, axis):
    high = x.astype(BF)
    return jnp.concatenate([high, (x - high.astype(F32)).astype(BF)], axis=axis)


def places(size, axis):
    return lax.broadcasted_iota(jnp.int32, (size, size), axis)


def column(matrix, at):
    lanes = lax.broadcasted_iota(jnp.int32, matrix.shape, 1)
    return jnp.sum(jnp.where(lanes == at, matrix, 0.0), axis=1, keepdims=True)


def to_column(row):
    size = row.shape[1]
    spread = jnp.broadcast_to(row, (size, size))
    return jnp.sum(jnp.where(places(size, 0) == places(size, 1), spread, 0.0), axis=1, keepdims=True)


def inverse_less_one(scores):
    size = scores[0].shape[0]
    rows, cols = places(size, 0), places(size, 1)
    eye = (rows == cols).astype(F32)
    span, off = 1, None
    while span < size:
        joins = (rows // (2 * span) == cols // (2 * span)) & (rows // span != cols // span)
        parts = [jnp.where(joins, a, 0.0).astype(BF) for a in scores]
        if off is None:
            off = [-p.astype(F32) for p in parts]
        else:
            full = [(o + eye).astype(BF) for o in off]
            half = [dot(p, f) for p, f in zip(parts, full)]
            off = [o - dot(f, h) for o, f, h in zip(off, full, half)]
        span *= 2
    return off


def maps_kernel(
    chunk,
    width,
    heads_step,
    first,
    given,
    query_ref,
    key_ref,
    value_ref,
    decay_ref,
    rate_ref,
    grad_ref,
    *refs,
):
    (
        transfer_ref,
        carried_ref,
        own_ref,
        cum_ref,
        query_l_ref,
        key_l_ref,
        back_ref,
        lower_ref,
        score_ref,
    ) = refs[given:]
    tokens = query_ref.shape[0]
    chunks = tokens // chunk
    rows, cols = places(chunk, 0), places(chunk, 1)
    tri = (rows >= cols).astype(BF)
    tri = jnp.concatenate([tri, tri], axis=1)
    units = [(h, i) for h in range(heads_step) for i in range(chunks)]
    first = first + pl.program_id(0) * heads_step
    rate_cols = jnp.transpose(rate_ref[...])
    rates = [column(rate_cols, first + h) for h in range(heads_step)]

    def part(ref, unit):
        h, i = unit
        return ref[i * chunk : (i + 1) * chunk, h * width : (h + 1) * width]

    def unit_rows(x):
        return x * lax.rsqrt(jnp.sum(x * x, axis=-1, keepdims=True) + 1e-06)

    cums = [dot(tri, halves(part(decay_ref, u), 0)) for u in units]
    queries = [unit_rows(part(query_ref, u)) for u in units]
    keys = [unit_rows(part(key_ref, u)) for u in units]
    values = [part(value_ref, u) for u in units]
    middles = [0.5 * c[chunk - 1 : chunk, :] for c in cums]
    lifts = [jnp.exp(c - m) for c, m in zip(cums, middles)]
    sinks = [jnp.exp(m - c) for c, m in zip(cums, middles)]
    key_l = [(k * e).astype(BF) for k, e in zip(keys, lifts)]
    query_l = [(q * e).astype(BF) for q, e in zip(queries, lifts)]
    back = [
        (k * e * rates[h][i * chunk : (i + 1) * chunk]).astype(BF)
        for k, e, (h, i) in zip(keys, sinks, units)
    ]
    both = [dot_t(jnp.concatenate([k, q], axis=0), b) for k, q, b in zip(key_l, query_l, back)]
    key_scores = [jnp.where(rows > cols, s[:chunk], 0.0) for s in both]
    scores = [jnp.where(rows >= cols, s[chunk:], 0.0).astype(BF) for s in both]
    lower = [o.astype(BF) for o in inverse_less_one(key_scores)]
    wide = [jnp.concatenate([k, v.astype(BF)], axis=1) for k, v in zip(key_l, values)]
    solved = [
        dot(o, w) + jnp.concatenate([k.astype(F32), v], axis=1)
        for o, w, k, v in zip(lower, wide, key_l, values)
    ]
    solved = [s.astype(BF) for s in solved]
    stepped = [tdot(b, s) for b, s in zip(back, solved)]
    reads = [q.astype(F32) - dot(p, s[:, :width]) for q, p, s in zip(query_l, scores, solved)]
    mids = [to_column(jnp.exp(m)) for m in middles]
    owns = [m * tdot(r, part(grad_ref, u)) for m, r, u in zip(mids, reads, units)]
    for n, u in enumerate(units):
        h, i = u
        span = slice(i * chunk, (i + 1) * chunk)
        lanes = slice(h * width, (h + 1) * width)
        cum_ref[span, lanes] = cums[n]
        query_l_ref[span, lanes] = query_l[n]
        key_l_ref[span, lanes] = key_l[n]
        back_ref[span, lanes] = back[n]
        lower_ref[h, span, :] = lower[n]
        score_ref[h, span, :] = scores[n]
    eye = (places(width, 0) == places(width, 1)).astype(F32)
    for h in range(heads_step):
        state = None
        for i in range(chunks):
            n = h * chunks + i
            mid, step = mids[n], stepped[n][:, :width]
            entering = jnp.concatenate([eye, jnp.zeros_like(eye)], axis=1) if i == 0 else state
            scaled = mid * entering
            moved = scaled - dot(step, scaled)
            carried = jnp.concatenate([jnp.zeros_like(eye), stepped[n][:, width:]], axis=1)
            state = mid * (moved + carried)
        transfer_ref[h] = state[:, :width].astype(BF)
        carried_ref[h] = state[:, width:].astype(BF)
        total = owns[h * chunks + chunks - 1]
        for i in range(chunks - 2, -1, -1):
            n = h * chunks + i
            scaled = mids[n] * total
            total = owns[n] + mids[n] * (scaled - tdot(stepped[n][:, :width], scaled))
        own_ref[h] = total.astype(BF)


def grads_kernel(
    chunk,
    width,
    heads_step,
    place_ref,
    query_ref,
    key_ref,
    value_ref,
    rate_ref,
    grad_ref,
    cum_ref,
    query_l_ref,
    key_l_ref,
    back_ref,
    lower_ref,
    score_ref,
    start_ref,
    end_ref,
    *refs,
):
    arrived_refs, refs, rate_s = refs[:-7], refs[-7:-1], refs[-1]
    (
        query_grad_ref,
        key_grad_ref,
        value_grad_ref,
        decay_grad_ref,
        rate_grad_ref,
        state_grad_ref,
    ) = refs
    position, last = place_ref[0], len(arrived_refs)

    def arrived(own_ref, h, turn):
        state = own_ref[h]
        for r, ref in enumerate(arrived_refs):
            state = jnp.where(position == turn(r + 1), ref[h].astype(F32), state)
        return state

    tokens = query_ref.shape[0]
    chunks = tokens // chunk
    rows, cols = places(chunk, 0), places(chunk, 1)
    tri = (rows <= cols).astype(BF)
    tri = jnp.concatenate([tri, tri], axis=1)
    first = pl.program_id(0) * heads_step
    heads = range(heads_step)
    rate_cols = jnp.transpose(rate_ref[...])
    rates = [column(rate_cols, first + h) for h in heads]

    def part(ref, h, i):
        return ref[i * chunk : (i + 1) * chunk, h * width : (h + 1) * width]

    def mat(ref, h, i):
        return ref[h, i * chunk : (i + 1) * chunk, :]

    cums = {(h, i): part(cum_ref, h, i) for i in range(chunks) for h in heads}
    middles = {u: 0.5 * c[chunk - 1 : chunk, :] for u, c in cums.items()}
    mids = {u: to_column(jnp.exp(m)) for u, m in middles.items()}
    states = {(h, 0): arrived(start_ref, h, lambda r: r) for h in heads}
    scaled, updates = {}, {}
    for i in range(chunks):
        for h in heads:
            u = (h, i)
            scaled[u] = mids[u] * states[u]
        rests = [part(value_ref, h, i) - dot(part(key_l_ref, h, i), scaled[h, i]) for h in heads]
        for h in heads:
            updates[h, i] = (rests[h] + dot(mat(lower_ref, h, i), rests[h])).astype(BF)
        for h in heads:
            moved = scaled[h, i] + tdot(part(back_ref, h, i), updates[h, i])
            states[h, i + 1] = mids[h, i] * moved
    out = {(h, chunks): arrived(end_ref, h, lambda r: last - r) for h in heads}
    rest_grads, lifted, out_grads = {}, {}, {}
    for i in range(chunks - 1, -1, -1):
        update_grads = []
        for h in heads:
            lifted[h, i] = mids[h, i] * out[h, i + 1]
            out_grads[h, i] = part(grad_ref, h, i).astype(BF)
            got = tdot(mat(score_ref, h, i), out_grads[h, i])
            update_grads.append(got + dot(part(back_ref, h, i), lifted[h, i]))
        for h in heads:
            rest = update_grads[h] + tdot(mat(lower_ref, h, i), update_grads[h])
            value_grad_ref[i * chunk : (i + 1) * chunk, h * width : (h + 1) * width] = rest
            rest_grads[h, i] = rest.astype(BF)
        for h in heads:
            left = jnp.concatenate([part(query_l_ref, h, i), part(key_l_ref, h, i)], axis=0)
            right = jnp.concatenate([out_grads[h, i], -rest_grads[h, i]], axis=0)
            out[h, i] = mids[h, i] * (lifted[h, i] + tdot(left, right))
    for h in heads:
        state_grad_ref[h] = out[h, 0]
    units = [(h, i) for i in range(chunks) for h in heads]
    joint = [jnp.concatenate([-rest_grads[u], out_grads[u]], axis=0) for u in units]
    pairs = [dot_t(j, updates[u]) for j, u in zip(joint, units)]
    key_pairs = [jnp.where(rows > cols, p[:chunk], 0.0).astype(BF) for p in pairs]
    query_pairs = [jnp.where(rows >= cols, p[chunk:], 0.0).astype(BF) for p in pairs]
    pairs = [jnp.concatenate([k, q], axis=0) for k, q in zip(key_pairs, query_pairs)]
    left_grads = [
        dot(p, part(back_ref, *u)) + dot_t(j, scaled[u]) for p, j, u in zip(pairs, joint, units)
    ]
    back_grads = [
        tdot(p, jnp.concatenate([part(key_l_ref, *u), part(query_l_ref, *u)], axis=0))
        + dot_t(updates[u], lifted[u])
        for p, u in zip(pairs, units)
    ]
    ones = jnp.ones((8, 2 * width), BF)
    crossing = [
        dot_t(ones, halves(out[h, i + 1] * states[h, i + 1], 1))[:1] for h, i in units
    ]
    slopes = [
        part(key_l_ref, *u).astype(F32) * l[:chunk]
        + part(query_l_ref, *u).astype(F32) * l[chunk:]
        - part(back_ref, *u).astype(F32) * b
        for u, l, b in zip(units, left_grads, back_grads)
    ]
    decays = [dot(tri, halves(s, 0)) + c for s, c in zip(slopes, crossing)]
    lanes = lax.broadcasted_iota(jnp.int32, (chunk, rate_s.shape[1]), 1)
    for n, (h, i) in enumerate(units):
        span = slice(i * chunk, (i + 1) * chunk)
        at = slice(h * width, (h + 1) * width)
        decay_grad_ref[span, at] = decays[n]
        gap = cums[h, i] - middles[h, i]
        lift, sink = jnp.exp(gap), jnp.exp(-gap)
        rate = rates[h][span]
        query, key = query_ref[span, at], key_ref[span, at]
        query_norm = lax.rsqrt(jnp.sum(query * query, axis=-1, keepdims=True) + 1e-06)
        key_norm = lax.rsqrt(jnp.sum(key * key, axis=-1, keepdims=True) + 1e-06)
        query, key = query * query_norm, key * key_norm
        query_grad = left_grads[n][chunk:] * lift
        sunk = back_grads[n] * sink
        key_grad = left_grads[n][:chunk] * lift + rate * sunk
        rate_grad = jnp.sum(sunk * key, axis=-1, keepdims=True)
        query_grad_ref[span, at] = query_norm * (
            query_grad - query * jnp.sum(query * query_grad, axis=-1, keepdims=True)
        )
        key_grad_ref[span, at] = key_norm * (
            key_grad - key * jnp.sum(key * key_grad, axis=-1, keepdims=True)
        )
        rate_s[span, :] = jnp.where(lanes == first + h, rate_grad, rate_s[span, :])

    @pl.when(pl.program_id(0) == pl.num_programs(0) - 1)
    def finish():
        rate_grad_ref[...] = jnp.transpose(rate_s[...])[: rate_grad_ref.shape[0]]


def specs_of(tokens, width, chunk, heads_step, rate_heads, skip=0):
    lanes = pl.BlockSpec((tokens, heads_step * width), lambda h, *p: (0, skip + h))
    rate = pl.BlockSpec((rate_heads, tokens), lambda h, *p: (0, 0))
    square = pl.BlockSpec((heads_step, tokens, chunk), lambda h, *p: (skip + h, 0, 0))
    state = pl.BlockSpec((heads_step, width, width), lambda h, *p: (skip + h, 0, 0))
    return lanes, rate, square, state


def section_maps(
    queries, key_input, value_input, log_decay, write_rate, out_grad, first, heads, into=()
):
    heads_all, tokens = write_rate.shape
    width = queries.shape[1] // heads_all
    chunk = min(128, tokens)
    heads_step = 2 if heads % 2 == 0 and first % 2 == 0 else 1
    lanes, rate, square, state = specs_of(
        tokens, width, chunk, heads_step, heads_all, first // heads_step
    )
    shape = jax.ShapeDtypeStruct
    return pl.pallas_call(
        functools.partial(maps_kernel, chunk, width, heads_step, first, len(into)),
        grid=(heads // heads_step,),
        in_specs=[lanes, lanes, lanes, lanes, rate, lanes]
        + [pl.BlockSpec(memory_space=pl.ANY)] * len(into),
        out_specs=[state, state, state, lanes, lanes, lanes, lanes, square, square],
        out_shape=[shape((heads_all, width, width), BF)] * 3
        + [shape(queries.shape, F32)]
        + [shape(queries.shape, BF)] * 3
        + [shape((heads_all, tokens, chunk), BF)] * 2,
        input_output_aliases={6 + n: n for n in range(len(into))},
        compiler_params=pltpu.CompilerParams(vmem_limit_bytes=VMEM_BYTES),
        cost_estimate=pl.CostEstimate(flops=10**8, bytes_accessed=10**7, transcendentals=0),
        name="section_maps",
    )(queries, key_input, value_input, log_decay, write_rate, out_grad, *into)


def section_grads(
    place, queries, key_input, value_input, write_rate, out_grad, saved, ends, arrivals
):
    heads, tokens = write_rate.shape
    width = queries.shape[1] // heads
    chunk = min(128, tokens)
    heads_step = 2 if heads % 2 == 0 else 1
    lanes, rate, square, state = specs_of(tokens, width, chunk, heads_step, heads)
    shape = jax.ShapeDtypeStruct
    return pl.pallas_call(
        functools.partial(grads_kernel, chunk, width, heads_step),
        grid_spec=pltpu.PrefetchScalarGridSpec(
            num_scalar_prefetch=1,
            grid=(heads // heads_step,),
            in_specs=[lanes, lanes, lanes, rate, lanes]
            + [lanes] * 4
            + [square] * 2
            + [state] * (2 + len(arrivals)),
            out_specs=[lanes, lanes, lanes, lanes, rate, state],
            scratch_shapes=[pltpu.VMEM((tokens, 128), F32)],
        ),
        out_shape=[shape(queries.shape, F32)] * 4
        + [shape((heads, tokens), F32), shape((heads, width, width), F32)],
        compiler_params=pltpu.CompilerParams(vmem_limit_bytes=VMEM_BYTES),
        cost_estimate=pl.CostEstimate(flops=10**8, bytes_accessed=10**7, transcendentals=0),
        name="section_grads",
    )(place, queries, key_input, value_input, write_rate, out_grad, *saved, *ends, *arrivals)


def hop_kernel(backward_at, place_ref, transfer_ref, carried_ref, own_ref, state_ref, out_ref):
    heads = transfer_ref.shape[0]

    @pl.when(place_ref[0] == backward_at)
    def backward():
        for h in range(heads):
            out_ref[h] = (tdot(transfer_ref[h], state_ref[h]) + own_ref[h]).astype(BF)

    @pl.when(place_ref[0] != backward_at)
    def forward():
        for h in range(heads):
            out_ref[h] = (dot(transfer_ref[h], state_ref[h]) + carried_ref[h]).astype(BF)


def hop(place, transfer, carried, own_grad, state, turn, sections):
    spec = pl.BlockSpec(state.shape, lambda i, p: (0, 0, 0))
    leaving = pl.pallas_call(
        functools.partial(hop_kernel, sections - turn),
        grid_spec=pltpu.PrefetchScalarGridSpec(
            num_scalar_prefetch=1, grid=(1,), in_specs=[spec] * 4, out_specs=spec
        ),
        out_shape=jax.ShapeDtypeStruct(state.shape, BF),
        compiler_params=pltpu.CompilerParams(vmem_limit_bytes=VMEM_BYTES),
        cost_estimate=pl.CostEstimate(flops=10**8, bytes_accessed=10**6, transcendentals=0),
        name="hop",
    )(place, transfer, carried, own_grad, state)
    pairs = [(turn - 1, turn), (sections - turn, sections - turn - 1)]
    return lax.ppermute(leaving, "ctx", pairs)


def experts_kernel(capacity, part_width, order, place_ref, *refs):
    sources = len(order)
    own_ref, came_refs, other_refs = refs[0], refs[1:sources], refs[sources : 2 * sources - 1]
    weight_refs, refs = refs[2 * sources - 1 : 2 * sources + 5], refs[2 * sources + 5 :]
    keep_ref, send_refs, scratch = refs[0], refs[1:3], refs[3:]
    weights_s, tokens_s, pieces_s, ranks_s, gates_s, sems = scratch
    step, steps = pl.program_id(0), pl.num_programs(0)
    mine, head_at, first, came_is = place_ref[0], place_ref[1], place_ref[2], place_ref[3]
    tokens = own_ref.shape[0]
    wide, hidden_width = weights_s.shape[2:]
    padded = wide // 2
    experts = ranks_s.shape[1]
    many = tokens_s.shape[1]

    def weight_copies(expert, slot):
        for m in range(3):
            for far in range(2):
                part = mine if far == 0 else 1 - mine
                at = pl.multiple_of(part * padded, 128)
                yield pltpu.make_async_copy(
                    weight_refs[2 * m + far].at[expert],
                    weights_s.at[slot, m, pl.ds(at, part_width)],
                    sems.at[slot, 2 * m + far],
                )

    def choice(source, at):
        rank = ranks_s[source, pl.ds(at, 1), :]
        slot = lax.broadcasted_iota(jnp.int32, (capacity, tokens), 0).astype(F32)
        return slot == rank

    def choices(source):
        picks = [choice(source, first + e).astype(F32).astype(BF) for e in range(many)]
        return jnp.concatenate(picks, axis=0)

    slot = lax.rem(step, 2)

    @pl.when(step == 0)
    def dispatch():
        for copy in weight_copies(0, 0):
            copy.start()
        blank = jnp.zeros((padded - part_width, hidden_width), BF)
        for n in range(2):
            for m in range(3):
                weights_s[n, m, part_width:padded] = blank
                weights_s[n, m, padded + part_width :] = blank
        before = (places(tokens, 0) < places(tokens, 1)).astype(BF)
        for s, turn in enumerate(order):
            if turn == 0:
                came, other, kind = own_ref.at[:, :wide], own_ref.at[:, wide:], 0
            else:
                came, other, kind = came_refs[turn - 1], other_refs[turn - 1], came_is
            start = part_width // 128 * 128
            offset = part_width - start
            dense = jnp.transpose(came[:, start : start + 128].astype(F32))
            dense = dense[offset : offset + experts]
            named = dense > 0.0
            rank = dot(named.astype(F32), before)
            ranks_s[s] = jnp.where(named, rank, -1.0)
            gates_s[s] = dense
            pick = choices(s)
            for which, ref in ((kind, came), (1 - kind, other)):
                picked = dot(pick, ref[...]).astype(BF)
                for e in range(many):
                    span = slice(s * capacity, (s + 1) * capacity)
                    tokens_s[which, e, span] = picked[e * capacity : (e + 1) * capacity]

    @pl.when(step + 1 < steps)
    def prefetch():
        for copy in weight_copies(step + 1, 1 - slot):
            copy.start()

    for copy in weight_copies(step, slot):
        copy.wait()
    at = first + step
    gate_pre = dot(tokens_s[0, step], weights_s[slot, 0])
    up_pre = dot(tokens_s[0, step], weights_s[slot, 1])
    raw_grad = dot(tokens_s[1, step], weights_s[slot, 2])
    weight = jnp.concatenate(
        [
            jnp.sum(
                jnp.where(choice(s, at), gates_s[s, pl.ds(at, 1), :], 0.0), axis=1, keepdims=True
            )
            for s in range(sources)
        ],
        axis=0,
    )
    sigmoid = jax.nn.sigmoid(gate_pre)
    activated = gate_pre * sigmoid
    hidden = (activated * up_pre).astype(BF).astype(F32)
    gate_part = jnp.sum(hidden * raw_grad, axis=1, keepdims=True)
    scaled = raw_grad * weight
    gate_back = (scaled * up_pre * sigmoid * (1.0 + gate_pre * (1.0 - sigmoid))).astype(BF)
    up_back = (scaled * activated).astype(BF)
    piece = dot_t(gate_back, weights_s[slot, 0]) + dot_t(up_back, weights_s[slot, 1])
    lanes = lax.broadcasted_iota(jnp.int32, (1, wide), 1)
    here = (lanes == part_width + at) | (lanes == padded + part_width + at)
    piece = (piece + jnp.where(here, gate_part, 0.0)).astype(BF)
    for s in range(sources):
        pieces_s[s, step] = piece[s * capacity : (s + 1) * capacity]

    @pl.when(step == steps - 1)
    def combine():
        per = send_refs[0].shape[0]
        for s in range(sources):
            flat = pieces_s[s].reshape(many * capacity, wide)
            total = tdot(choices(s), flat).astype(BF)
            left, right = total[:, :padded], total[:, padded:]
            keep_ref[s] = jnp.where(head_at == 0, left, right)
            send_refs[s // per][s % per] = jnp.where(head_at == 0, right, left)


def expert_work(place, own, came, other, weights, capacity, total_experts, order):
    tokens, wide = came[0].shape
    many, part_width, hidden_width = weights[0].shape
    sources = len(order)
    padded = wide // 2
    whole = lambda x: pl.BlockSpec(x.shape, lambda e, p: (0,) * len(x.shape))
    shape = jax.ShapeDtypeStruct
    outs = [shape((n, tokens, padded), BF) for n in (sources, sources // 2, sources // 2)]
    token_args = (own, *came, *other)
    return pl.pallas_call(
        functools.partial(experts_kernel, capacity, part_width, order),
        grid_spec=pltpu.PrefetchScalarGridSpec(
            num_scalar_prefetch=1,
            grid=(many,),
            in_specs=[whole(x) for x in token_args]
            + [pl.BlockSpec(memory_space=pl.ANY)] * len(weights),
            out_specs=[whole(x) for x in outs],
            scratch_shapes=[
                pltpu.VMEM((2, 3, wide, hidden_width), BF),
                pltpu.VMEM((2, many, sources * capacity, wide), BF),
                pltpu.VMEM((sources, many, capacity, wide), BF),
                pltpu.VMEM((sources, total_experts, tokens), F32),
                pltpu.VMEM((sources, total_experts, tokens), F32),
                pltpu.SemaphoreType.DMA((2, 6)),
            ],
        ),
        out_shape=outs,
        compiler_params=pltpu.CompilerParams(vmem_limit_bytes=VMEM_BYTES),
        name="expert_work",
    )(place, *token_args, *weights)


def plain_call(kernel, name, out_shape, *args):
    return pl.pallas_call(
        kernel,
        out_shape=out_shape,
        compiler_params=pltpu.CompilerParams(vmem_limit_bytes=VMEM_BYTES),
        name=name,
    )(*args)


def head_sum_kernel(first, keep, got, *outs):
    for k, out in enumerate(outs):
        out[...] = (keep[first + k].astype(F32) + got[k].astype(F32)).astype(BF)


def home_kernel(part_width, experts, at_ref, ids_ref, *refs):
    pieces, (input_ref, gate_ref) = refs[:-2], refs[-2:]
    total = pieces[0][...].astype(F32)
    for piece in pieces[1:]:
        total = total + piece[...].astype(F32)
    total = jnp.transpose(total)
    input_ref[...] = total[:part_width]
    gates = total[part_width : part_width + experts]
    slots = gate_ref.shape[0]
    names = lax.broadcasted_iota(jnp.int32, gates.shape, 0)
    for j in range(slots):
        ids = ids_ref[pl.ds(at_ref[0] * slots + j, 1), :]
        gate_ref[j : j + 1, :] = jnp.sum(jnp.where(names == ids, gates, 0.0), axis=0, keepdims=True)


def swapped(x, axis):
    return lax.ppermute(x, axis, [(0, 1), (1, 0)])


def turned(x, axis, by):
    count = lax.axis_size(axis)
    return lax.ppermute(x, axis, [(i, (i + by) % count) for i in range(count)])


def pack_kernel(
    part_width, padded, which_ref, rows_ref, grads_ref, ids_ref, gates_ref, own_ref, sent_ref
):
    top, tokens = ids_ref.shape
    start = part_width // 128 * 128
    experts = lax.broadcasted_iota(jnp.int32, (128, tokens), 0) + (start - part_width)
    dense = jnp.zeros((128, tokens), F32)
    for j in range(top):
        named = experts == ids_ref[j : j + 1, :]
        dense = dense + jnp.where(named, gates_ref[j : j + 1, :], 0.0)
    dense = jnp.transpose(dense)
    lanes = lax.broadcasted_iota(jnp.int32, (tokens, 128), 1) + start
    wide = 2 * padded
    for n, ref in enumerate((rows_ref, grads_ref)):
        x = ref[...].astype(F32)
        x = jnp.concatenate([x, jnp.zeros((tokens, wide - x.shape[1]), F32)], axis=1)
        moved = pltpu.roll(x, padded - part_width, 1)
        tile = jnp.where(lanes < part_width, x[:, start : start + 128], dense)
        blank = jnp.zeros((tokens, padded - start - 128), F32)
        pieces = [x[:, :start], tile] + [blank] * (start + 128 < padded) + [moved[:, padded:]]
        packed = jnp.concatenate(pieces, axis=1).astype(BF)
        own_ref[:, n * wide : (n + 1) * wide] = packed

        @pl.when(which_ref[0] == n)
        def keep(packed=packed):
            sent_ref[...] = packed


def packed_tokens(first_is, rows, grads, ids, gates, part_width, padded):
    tokens = rows.shape[0]
    whole = lambda x: pl.BlockSpec(x.shape, lambda i, p: (0, 0))
    shapes = [jax.ShapeDtypeStruct((tokens, n * padded), BF) for n in (4, 2)]
    return pl.pallas_call(
        functools.partial(pack_kernel, part_width, padded),
        grid_spec=pltpu.PrefetchScalarGridSpec(
            num_scalar_prefetch=1,
            grid=(1,),
            in_specs=[whole(x) for x in (rows, grads, ids, gates)],
            out_specs=[whole(x) for x in shapes],
        ),
        out_shape=shapes,
        compiler_params=pltpu.CompilerParams(vmem_limit_bytes=VMEM_BYTES),
        name="packed_tokens",
    )(first_is, rows, grads, ids, gates)


def per_device(
    queries,
    key_input,
    value_input,
    log_decay,
    write_rate,
    start_state,
    out_grad,
    end_grad,
    moe_input,
    moe_grad,
    expert_ids,
    gate_weights,
    gate_matrix,
    up_matrix,
    down_matrix,
):
    sections = lax.axis_size("ctx")
    position = lax.axis_index("ctx")
    parts = lax.axis_size("fsdp")
    core = lax.axis_index("fsdp")
    head_count = lax.axis_size("head")
    head_at = lax.axis_index("head")

    token_count, top_count = expert_ids.shape
    experts_here = gate_matrix.shape[0]
    total_experts = experts_here * sections
    capacity = 3 * token_count // 8
    part_width = gate_matrix.shape[1]
    padded = -(-(part_width + total_experts) // 128) * 128

    turns = range(1, sections)
    near = [s for s in turns if s in (1, sections - 1)]
    far = [s for s in turns if s not in near]
    order = far + near + [0]
    came_is = head_at if head_count == 2 else 0 * head_at
    came_is = came_is.astype(jnp.int32)
    place = jnp.reshape(position, (1,)).astype(jnp.int32)
    recurrent = (queries, key_input, value_input, log_decay, write_rate.T, out_grad)
    heads_here = write_rate.shape[1]
    weights_own = [gate_matrix, up_matrix, jnp.swapaxes(down_matrix, 1, 2)]
    came, other, weights_far = {}, {}, [None] * 3

    def fetch_other(s):
        if head_count == 2:
            other[s] = swapped(came[s], "head")
        else:
            other[s] = turned(own[:, own.shape[1] // 2 :], "ctx", s)

    own, sent = packed_tokens(
        came_is.reshape(1), moe_input, moe_grad, expert_ids.T, gate_weights.T, part_width, padded
    )
    sent, recurrent, weights_own = lax.optimization_barrier((sent, recurrent, weights_own))
    for s in near:
        came[s] = turned(sent, "ctx", s)
    weights_far[0] = swapped(weights_own[0], "fsdp")
    first_maps = section_maps(*recurrent, 0, heads_here // 2)
    came, weights_far[0], first_maps, recurrent, sent, weights_own = lax.optimization_barrier(
        (came, weights_far[0], first_maps, recurrent, sent, weights_own)
    )
    for s in far:
        came[s] = turned(sent, "ctx", s)
    for s in near:
        fetch_other(s)
    weights_far[1] = swapped(weights_own[1], "fsdp")
    last_maps = section_maps(
        *recurrent, heads_here // 2, heads_here - heads_here // 2, into=first_maps
    )
    came, other, weights_far[1], last_maps, weights_own = lax.optimization_barrier(
        (came, other, weights_far[1], last_maps, weights_own)
    )
    for s in far:
        fetch_other(s)
    weights_far[2] = swapped(weights_own[2], "fsdp")
    transfer, carried, own_grad, *saved = last_maps
    state = jnp.where(position == 0, start_state, end_grad).astype(BF)
    state = hop(place, transfer, carried, own_grad, state, 1, sections)
    arrivals = [state]
    if sections > 2:
        other, state = lax.optimization_barrier((other, state))
        state = hop(place, transfer, carried, own_grad, state, 2, sections)
        arrivals.append(state)
    expert_place = jnp.stack([core, head_at, position * experts_here, came_is]).astype(jnp.int32)
    weights = [w for pair in zip(weights_own, weights_far) for w in pair]
    keep, *sends = expert_work(
        expert_place,
        own,
        [came[s] for s in turns],
        [other[s] for s in turns],
        weights,
        capacity,
        total_experts,
        order,
    )
    for turn in range(3, sections):
        state = hop(place, transfer, carried, own_grad, state, turn, sections)
        arrivals.append(state)
    gradients = section_grads(
        place,
        queries,
        key_input,
        value_input,
        write_rate.T,
        out_grad,
        saved,
        (start_state, end_grad),
        arrivals,
    )

    if head_count == 2:
        shape = jax.ShapeDtypeStruct
        per = len(order) // 2
        block = (token_count, padded)
        pieces = []
        for n, send in enumerate(sends):
            sums = plain_call(
                functools.partial(head_sum_kernel, n * per),
                "head_sum",
                [shape(block, BF)] * per,
                keep, swapped(send, "head"),
            )
            for turn, piece in zip(order[n * per : (n + 1) * per], sums):
                pieces.append(turned(piece, "ctx", sections - turn) if turn else piece)
        whole = lambda x: pl.BlockSpec(x.shape, lambda i, p: (0, 0))
        outs = [shape((part_width, token_count), F32), shape((top_count // 2, token_count), F32)]
        home_args = (expert_ids.T, *pieces)
        input_grads, gate_grads = pl.pallas_call(
            functools.partial(home_kernel, part_width, total_experts),
            grid_spec=pltpu.PrefetchScalarGridSpec(
                num_scalar_prefetch=1,
                grid=(1,),
                in_specs=[whole(x) for x in home_args],
                out_specs=[whole(x) for x in outs],
            ),
            out_shape=outs,
            compiler_params=pltpu.CompilerParams(vmem_limit_bytes=VMEM_BYTES),
            name="home",
        )(head_at.astype(jnp.int32).reshape(1), *home_args)
        input_grads, gate_grads = input_grads.T, gate_grads.T
    else:
        sent_back = jnp.concatenate(sends, axis=0)
        halves_in = [jnp.where(head_at == 0, keep, sent_back), jnp.where(head_at == 0, sent_back, keep)]
        wide = jnp.concatenate([x[:, :, :part_width] for x in halves_in], axis=-1)
        wide = lax.psum_scatter(wide, "head", scatter_dimension=2, tiled=True)
        gates = lax.psum(keep[:, :, part_width : part_width + total_experts], "head")
        pieces = jnp.concatenate([wide, gates], axis=-1)
        back = 0.0
        for piece, turn in zip(pieces, order):
            back = back + (turned(piece, "ctx", sections - turn) if turn else piece).astype(F32)
        input_grads, gates = back[:, : wide.shape[-1]], back[:, wide.shape[-1] :]
        slots_here = top_count // head_count
        ids_here = lax.dynamic_slice_in_dim(expert_ids, head_at * slots_here, slots_here, 1)
        named = ids_here[:, :, None] == lax.iota(jnp.int32, total_experts)[None, None, :]
        gate_grads = jnp.sum(jnp.where(named, gates[:, None, :], 0.0), axis=-1)
    return (*gradients[:4], gradients[4].T, gradients[5][None], input_grads, gate_grads)


def solution(mesh):
    in_specs = (
        P(("groups", "ctx"), ("head", "fsdp")),
        P(("groups", "ctx"), ("head", "fsdp")),
        P(("groups", "ctx"), ("head", "fsdp")),
        P(("groups", "ctx"), ("head", "fsdp")),
        P(("groups", "ctx"), ("head", "fsdp")),
        P(("groups", "head", "fsdp"), None, None),
        P(("groups", "ctx"), ("head", "fsdp")),
        P(("groups", "head", "fsdp"), None, None),
        P(("groups", "ctx", "fsdp"), None),
        P(("groups", "ctx", "fsdp"), None),
        P(("groups", "ctx", "fsdp"), None),
        P(("groups", "ctx", "fsdp"), None),
        P("ctx", "fsdp", "head"),
        P("ctx", "fsdp", "head"),
        P("ctx", "head", "fsdp"),
    )
    out_specs = (
        P(("groups", "ctx"), ("head", "fsdp")),
        P(("groups", "ctx"), ("head", "fsdp")),
        P(("groups", "ctx"), ("head", "fsdp")),
        P(("groups", "ctx"), ("head", "fsdp")),
        P(("groups", "ctx"), ("head", "fsdp")),
        P(("groups", "ctx"), ("head", "fsdp"), None, None),
        P(("groups", "ctx", "fsdp"), "head"),
        P(("groups", "ctx", "fsdp"), "head"),
    )
    return jax.shard_map(
        per_device, mesh=mesh, in_specs=in_specs, out_specs=out_specs, check_vma=False
    )
```

time: 194 us -> 126 us (0.65)
  waiting for transfers between devices: 60.7 us -> 24.4 us
  local copies, waits for them, and re-layouts: 28.9 us -> 4.32 us
  Pallas kernels: 51 us -> 68.1 us
  starting transfers between devices: 42.4 us -> 26.6 us
  matrix products: 5 us -> 0 us
  other arithmetic: 4.14 us -> 1.44 us
    ppermute x9 -> x6, waiting for transfers between devices: 46.7 us -> 13.5 us  [turned(): return lax.ppermute(x, axis, [(i, (i + by) % count) for i in range(count)])]
    pallas_call x2 -> x10, Pallas kernels: 39 us -> 55.6 us  [the longest x1 24.4 us: expert_work(): pl.pallas_call(functools.partial(experts_kernel, capacity, part_width, or...]
    ppermute x6 -> x3, starting transfers between devices: 18.7 us -> 5.29 us  [hop(): return lax.ppermute(leaving, 'ctx', pairs)]
    unnamed x49 -> x28, local copies, waits for them, and re-layouts: 16.4 us -> 4.32 us
    dynamic_slice x4 -> x0, local copies, waits for them, and re-layouts: 6.58 us -> none  [the longest x3 6.58 us: per_device(): lax.dynamic_slice_in_dim(w, far_at, many, 0)]
    dot_general x6 -> x0, matrix products: 5 us -> none  [apply_map(): lax.dot_general(transfer.astype(BF), state.astype(BF), (((2,), (1,)), ((0...]
    ppermute x1 -> x0, local copies, waits for them, and re-layouts: 4.4 us -> none  [swapped(): return lax.ppermute(x, axis, [(0, 1), (1, 0)])]
    ppermute x9 -> x6, starting transfers between devices: 19.4 us -> 15.1 us  [turned(): return lax.ppermute(x, axis, [(i, (i + by) % count) for i in range(count)])]
  transfers between devices with their start and end apart: 28 -> 17, of which waited for: 13 -> 5; matrix products, arithmetic and copies ran while one was open for 14% -> 1% of each run, Pallas kernels for 13% -> 51%
where the time goes in v2:
time: 126 us
  Pallas kernels  68.1 us (54%)
  starting transfers between devices  26.6 us (21%)
  waiting for transfers between devices  24.4 us (19%)
  local copies, waits for them, and re-layouts  4.32 us (3%)
  other arithmetic  1.44 us (1%)
    pallas_call x1, Pallas kernels, expert_work(): pl.pallas_call(functools.partial(experts_kernel, capacity, part_width, or...  24.4 us
    pallas_call x2, Pallas kernels, section_maps(): pl.pallas_call(functools.partial(maps_kernel, chunk, width, heads_step, f...  16.4 us
    ppermute x6, starting transfers between devices, turned(): return lax.ppermute(x, axis, [(i, (i + by) % count) for i in range(count)])  15.1 us
    ppermute x6, waiting for transfers between devices, turned(): return lax.ppermute(x, axis, [(i, (i + by) % count) for i in range(count)])  13.5 us
    pallas_call x1, Pallas kernels, section_grads(): pl.pallas_call(functools.partial(grads_kernel, chunk, width, heads_step),...  12.6 us
    pallas_call x3, Pallas kernels, hop(): pl.pallas_call(functools.partial(hop_kernel, sections - turn), grid_spec=...  6.44 us
    ppermute x8, starting transfers between devices, swapped(): return lax.ppermute(x, axis, [(0, 1), (1, 0)])  6.25 us
    ppermute x3, waiting for transfers between devices, hop(): return lax.ppermute(leaving, 'ctx', pairs)  6.24 us
  transfers between devices with their start and end apart: 17, of which 5 were waited for; matrix products, arithmetic and copies ran while one was open for 1% of the time, Pallas kernels for 51%

profile of v2, /device:TPU:0, one launch (start us, length us, event | category | flops | bytes accessed | tf_op | source)
XLA Modules:
  0.0 125.8 jit_solution(6409125707125066110)
XLA Ops:
  0.6 2.4 %packed_tokens.1 = (bf16[128,2560]{1,0:T(8,128)(2,1)}, bf16[128,1280]{1,0:T(8,128)(2,1)}) custom-call(s32[1]{0:T(128)} %bitcast.2.which_ref.at_ref, bf16[128,1152]{1,0:T(8,128)(2,1)} %rows_ref.1, f32[128,1152]{1,0:T(8,128)} %grads_ref.1, s32[8,128]{1,0:T(8,128)} %bitcast.17, f32[8,128]{1,0:T(8,128)} %bitcast.19), custom_call_target="tpu_custom_call" | custom-call | tf_op jit(solution)/shard_map/packed_tokens/pallas_call | solution.py:620
  3.5 2.6 %collective-permute-start = (bf16[128,1280]{1,0:T(8,128)(2,1)}, bf16[128,1280]{1,0:T(8,128)(2,1)S(1)}, u32[]{:S(2)}, u32[]{:S(2)}) collective-permute-start(bf16[128,1280]{1,0:T(8,128)(2,1)} %get-tuple-element.118), channel_id=1, source_target_pairs={{0,4},{4,8},{8,12},{12,0},{1,5},{5,9},{9,13},{13,1},{2,6},{6,10},{... | collective-permute-start | bytes 983048 | tf_op jit(solution)/shard_map/ppermute | solution.py:585
  6.1 2.1 %collective-permute-start.1 = (bf16[128,1280]{1,0:T(8,128)(2,1)}, bf16[128,1280]{1,0:T(8,128)(2,1)S(1)}, u32[]{:S(2)}, u32[]{:S(2)}) collective-permute-start(bf16[128,1280]{1,0:T(8,128)(2,1)} %get-tuple-element.118), channel_id=1, source_target_pairs={{0,12},{4,0},{8,4},{12,8},{1,13},{5,1},{9,5},{13,9},{2,14},{6,2},{... | collective-permute-start | bytes 983048 | tf_op jit(solution)/shard_map/ppermute | solution.py:585
  8.2 8.2 %section_maps.2 = (bf16[8,128,128]{2,1,0:T(8,128)(2,1)}, bf16[8,128,128]{2,1,0:T(8,128)(2,1)}, bf16[8,128,128]{2,1,0:T(8,128)(2,1)}, f32[256,1024]{1,0:T(8,128)}...) custom-call(f32[256,1024]{1,0:T(8,128)} %query_ref.3, ...), custom_call_target="tpu_custom_call" | custom-call | flops 100000000 | bytes 10000000 | tf_op jit(solution)/shard_map/section_maps/pallas_call | solution.py:331
  16.9 6.2 %collective-permute-done.1.refs_3_ = bf16[128,1280]{1,0:T(8,128)(2,1)S(1)} collective-permute-done((bf16[128,1280]{1,0:T(8,128)(2,1)}, bf16[128,1280]{1,0:T(8,128)(2,1)S(1)}, u32[]{:S(2)}, u32[]{:S(2)}) %collective-permute-start.1) | collective-permute-done | bytes 327712 | tf_op jit(solution)/shard_map/ppermute | solution.py:585
  24.6 1.5 %collective-permute-start.4 = (bf16[128,1280]{1,0:T(8,128)(2,1)S(1)}, bf16[128,1280]{1,0:T(8,128)(2,1)}, u32[]{:S(2)}, u32[]{:S(2)}) collective-permute-start(bf16[128,1280]{1,0:T(8,128)(2,1)S(1)} %collective-permute-done.refs_1_), channel_id=1, source_target_pairs={{0,2},{2,0},{1,3},{3,1},{4,6},{6,4},{5,7},{7,5},{8,10},{10,8},{9,1... | collective-permute-start | bytes 983048 | tf_op jit(solution)/shard_map/ppermute | solution.py:580
  26.7 8.2 %section_maps.3 = (bf16[8,128,128]{2,1,0:T(8,128)(2,1)}, bf16[8,128,128]{2,1,0:T(8,128)(2,1)}, bf16[8,128,128]{2,1,0:T(8,128)(2,1)}, f32[256,1024]{1,0:T(8,128)}...) custom-call(f32[256,1024]{1,0:T(8,128)} %query_ref.3, ...), custom_call_target="tpu_custom_call", output_to_operand_aliasing={{0}: (6, {}), {1}: (7, {}), {2}: (8, {}), {3}: (9, {}), {4}... | custom-call | flops 100000000 | bytes 10000000 | tf_op jit(solution)/shard_map/section_maps/pallas_call | solution.py:331
  34.9 6.6 %collective-permute-done.3.refs_2_ = bf16[128,1280]{1,0:T(8,128)(2,1)S(1)} collective-permute-done((bf16[128,1280]{1,0:T(8,128)(2,1)}, bf16[128,1280]{1,0:T(8,128)(2,1)S(1)}, u32[]{:S(2)}, u32[]{:S(2)}) %collective-permute-start.3) | collective-permute-done | bytes 327712 | tf_op jit(solution)/shard_map/ppermute | solution.py:585
  41.6 1.5 %collective-permute-start.8 = (bf16[128,1280]{1,0:T(8,128)(2,1)S(1)}, bf16[128,1280]{1,0:T(8,128)(2,1)S(1)}, u32[]{:S(2)}, u32[]{:S(2)}) collective-permute-start(bf16[128,1280]{1,0:T(8,128)(2,1)S(1)} %collective-permute-done.3.refs_2_), channel_id=1, source_target_pairs={{0,2},{2,0},{1,3},{3,1},{4,6},{6,4},{5,7},{7,5},{8,10},{10,8},{9,1... | collective-permute-start | bytes 983048 | tf_op jit(solution)/shard_map/ppermute | solution.py:580
  43.9 2.1 %hop.3 = bf16[8,128,128]{2,1,0:T(8,128)(2,1)} custom-call(s32[1]{0:T(128)} %bitcast.place_ref, bf16[8,128,128]{2,1,0:T(8,128)(2,1)} %get-tuple-element.153.transfer_ref, bf16[8,128,128]{2,1,0:T(8,128)(2,1)} %get-tuple-element.154.carried_ref, bf16[8,128,128]{2,1,0:T(8,128)(2,1)} %get-tuple-element.155.own_ref, bf16[8,128,128]{2,1,0:T(8,128)(2,1)} %select_convert_fusion.state_ref), custom_call_target="tpu_custom_call" | custom-call | flops 100000000 | bytes 1000000 | tf_op jit(solution)/shard_map/hop/pallas_call | solution.py:393
  46.0 3.3 %collective-permute-start.7 = (bf16[8,128,128]{2,1,0:T(8,128)(2,1)}, bf16[8,128,128]{2,1,0:T(8,128)(2,1)S(1)}, u32[]{:S(2)}, u32[]{:S(2)}) collective-permute-start(bf16[8,128,128]{2,1,0:T(8,128)(2,1)} %hop.3), channel_id=1, source_target_pairs={{0,4},{12,8},{1,5},{13,9},{2,6},{14,10},{3,7},{15,11},{16,20},{28,... | collective-permute-start | bytes 786440 | tf_op jit(solution)/shard_map/ppermute | solution.py:404
  49.4 6.2 %collective-permute-done.7.state_ref.refs_0_ = bf16[8,128,128]{2,1,0:T(8,128)(2,1)S(1)} collective-permute-done((bf16[8,128,128]{2,1,0:T(8,128)(2,1)}, bf16[8,128,128]{2,1,0:T(8,128)(2,1)S(1)}, u32[]{:S(2)}, u32[]{:S(2)}) %collective-permute-start.7) | collective-permute-done | bytes 262176 | tf_op jit(solution)/shard_map/ppermute | solution.py:404
  56.3 2.2 %hop.4 = bf16[8,128,128]{2,1,0:T(8,128)(2,1)} custom-call(s32[1]{0:T(128)} %bitcast.place_ref, bf16[8,128,128]{2,1,0:T(8,128)(2,1)} %get-tuple-element.153.transfer_ref, bf16[8,128,128]{2,1,0:T(8,128)(2,1)} %get-tuple-element.154.carried_ref, bf16[8,128,128]{2,1,0:T(8,128)(2,1)} %get-tuple-element.155.own_ref, bf16[8,128,128]{2,1,0:T(8,128)(2,1)} %copy-done.2), custom_call_target="tpu_custom_call" | custom-call | flops 100000000 | bytes 1000000 | tf_op jit(solution)/shard_map/hop/pallas_call | solution.py:393
  59.9 24.4 %expert_work.1 = (bf16[4,128,640]{2,1,0:T(8,128)(2,1)}, bf16[2,128,640]{2,1,0:T(8,128)(2,1)}, bf16[2,128,640]{2,1,0:T(8,128)(2,1)}) custom-call(s32[4]{0:T(128)} %pad_add_fusion.place_ref, bf16[128,2560]{1,0:T(8,128)(2,1)} %get-tuple-element.166.refs_0_, bf16[128,1280]{1,0:T(8,128)(2,1)} %copy-done.4, bf16[128,1280]{1,0:T(8,128)(2,1)} %copy-done.6, ...), custom_call_target="tpu_custom_call" | custom-call | tf_op jit(solution)/shard_map/expert_work/pallas_call | solution.py:527
  85.0 1.5 %collective-permute-start.12 = (bf16[2,128,640]{2,1,0:T(8,128)(2,1)}, bf16[2,128,640]{2,1,0:T(8,128)(2,1)S(1)}, u32[]{:S(2)}, u32[]{:S(2)}) collective-permute-start(bf16[2,128,640]{2,1,0:T(8,128)(2,1)} %get-tuple-element.178), channel_id=1, source_target_pairs={{0,2},{2,0},{1,3},{3,1},{4,6},{6,4},{5,7},{7,5},{8,10},{10,8},{9,1... | collective-permute-start | bytes 983048 | tf_op jit(solution)/shard_map/ppermute | solution.py:580
  87.2 2.1 %hop.5 = bf16[8,128,128]{2,1,0:T(8,128)(2,1)} custom-call(s32[1]{0:T(128)} %bitcast.place_ref, bf16[8,128,128]{2,1,0:T(8,128)(2,1)} %get-tuple-element.153.transfer_ref, bf16[8,128,128]{2,1,0:T(8,128)(2,1)} %get-tuple-element.154.carried_ref, bf16[8,128,128]{2,1,0:T(8,128)(2,1)} %get-tuple-element.155.own_ref, bf16[8,128,128]{2,1,0:T(8,128)(2,1)} %copy-done.3), custom_call_target="tpu_custom_call" | custom-call | flops 100000000 | bytes 1000000 | tf_op jit(solution)/shard_map/hop/pallas_call | solution.py:393
  90.6 4.7 %collective-permute-done.15.got = bf16[2,128,640]{2,1,0:T(8,128)(2,1)S(1)} collective-permute-done((bf16[2,128,640]{2,1,0:T(8,128)(2,1)}, bf16[2,128,640]{2,1,0:T(8,128)(2,1)S(1)}, u32[]{:S(2)}, u32[]{:S(2)}) %collective-permute-start.15) | collective-permute-done | bytes 327712 | tf_op jit(solution)/shard_map/ppermute | solution.py:580
  96.0 1.9 %head_sum.3 = (bf16[128,640]{1,0:T(8,128)(2,1)}, bf16[128,640]{1,0:T(8,128)(2,1)}) custom-call(bf16[4,128,640]{2,1,0:T(8,128)(2,1)} %get-tuple-element.177.keep, bf16[2,128,640]{2,1,0:T(8,128)(2,1)} %copy-done.9), custom_call_target="tpu_custom_call" | custom-call | tf_op jit(solution)/shard_map/head_sum/pallas_call | solution.py:551
  98.0 4.2 %collective-permute-start.16 = (bf16[128,640]{1,0:T(8,128)(2,1)}, bf16[128,640]{1,0:T(8,128)(2,1)S(1)}, u32[]{:S(2)}, u32[]{:S(2)}) collective-permute-start(bf16[128,640]{1,0:T(8,128)(2,1)} %get-tuple-element.182), channel_id=1, source_target_pairs={{0,4},{4,8},{8,12},{12,0},{1,5},{5,9},{9,13},{13,1},{2,6},{6,10},{... | collective-permute-start | bytes 491528 | tf_op jit(solution)/shard_map/ppermute | solution.py:585
  102.9 1.9 %head_sum.2 = (bf16[128,640]{1,0:T(8,128)(2,1)}, bf16[128,640]{1,0:T(8,128)(2,1)}) custom-call(bf16[4,128,640]{2,1,0:T(8,128)(2,1)} %get-tuple-element.177.keep, bf16[2,128,640]{2,1,0:T(8,128)(2,1)} %copy-done.8), custom_call_target="tpu_custom_call" | custom-call | tf_op jit(solution)/shard_map/head_sum/pallas_call | solution.py:551
  104.9 3.3 %collective-permute-start.13 = (bf16[128,640]{1,0:T(8,128)(2,1)}, bf16[128,640]{1,0:T(8,128)(2,1)S(1)}, u32[]{:S(2)}, u32[]{:S(2)}) collective-permute-start(bf16[128,640]{1,0:T(8,128)(2,1)} %get-tuple-element.179), channel_id=1, source_target_pairs={{0,8},{4,12},{8,0},{12,4},{1,9},{5,13},{9,1},{13,5},{2,10},{6,14},... | collective-permute-start | bytes 491528 | tf_op jit(solution)/shard_map/ppermute | solution.py:585
  108.1 1.5 %collective-permute-start.14 = (bf16[128,640]{1,0:T(8,128)(2,1)}, bf16[128,640]{1,0:T(8,128)(2,1)S(1)}, u32[]{:S(2)}, u32[]{:S(2)}) collective-permute-start(bf16[128,640]{1,0:T(8,128)(2,1)} %get-tuple-element.180), channel_id=1, source_target_pairs={{0,12},{4,0},{8,4},{12,8},{1,13},{5,1},{9,5},{13,9},{2,14},{6,2},{... | collective-permute-start | bytes 491528 | tf_op jit(solution)/shard_map/ppermute | solution.py:585
  110.4 12.6 %section_grads.1 = (f32[256,1024]{1,0:T(8,128)}, f32[256,1024]{1,0:T(8,128)}, f32[256,1024]{1,0:T(8,128)}, f32[256,1024]{1,0:T(8,128)}, f32[8,256]{1,0:T(8,128)}, /*index=5*/f32[8,128,128]{2,1,0:T(8,128)}) custom-call(s32[1]{0:T(128)} %bitcast.place_ref, f32[256,1024]{1,0:T(8,128)} %query_ref.3, f32[256,1024]{1,0:T(8,128)} %key_ref.3, ...), custom_call_target="tpu_custom_call" | custom-call | flops 100000000 | bytes 10000000 | tf_op jit(solution)/shard_map/section_grads/pallas_call | solution.py:357
  123.7 2.1 %home.1 = (f32[576,128]{1,0:T(8,128)}, f32[4,128]{1,0:T(4,128)}) custom-call(s32[1]{0:T(128)} %bitcast.2.which_ref.at_ref, s32[8,128]{1,0:T(8,128)} %bitcast.18, bf16[128,640]{1,0:T(8,128)(2,1)} %copy-done.12, bf16[128,640]{1,0:T(8,128)(2,1)} %copy-done.13, bf16[128,640]{1,0:T(8,128)(2,1)} %copy-done.11, bf16[128,640]{1,0:T(8,128)(2,1)} %get-tuple-element.183.refs_3_), custom_call_target="tpu_custom_call" | custom-call | tf_op jit(solution)/shard_map/home/pallas_call | solution.py:760
  (51 shorter events, 11.5 us)
Async XLA Ops:
  3.0 20.1 %collective-permute-start.2 = (bf16[8,576,512]{2,1,0:T(8,128)(2,1)}, bf16[8,576,512]{2,1,0:T(8,128)(2,1)}, u32[]{:S(2)}, u32[]{:S(2)}) collective-permute-start(bf16[8,576,512]{2,1,0:T(8,128)(2,1)} %refs_7_), channel_id=1, source_target_pairs={{0,1},{1,0},{2,3},{3,2},{4,5},{5,4},{6,7},{7,6},{8,9},{9,8},{10,11... | collective-permute-start | bytes 14155784 | tf_op jit(solution)/shard_map/ppermute | solution.py:580
  3.5 13.4 %collective-permute-start = (bf16[128,1280]{1,0:T(8,128)(2,1)}, bf16[128,1280]{1,0:T(8,128)(2,1)S(1)}, u32[]{:S(2)}, u32[]{:S(2)}) collective-permute-start(bf16[128,1280]{1,0:T(8,128)(2,1)} %get-tuple-element.118), channel_id=1, source_target_pairs={{0,4},{4,8},{8,12},{12,0},{1,5},{5,9},{9,13},{13,1},{2,6},{6,10},{... | collective-permute-start | bytes 983048 | tf_op jit(solution)/shard_map/ppermute | solution.py:585
  6.1 17.1 %collective-permute-start.1 = (bf16[128,1280]{1,0:T(8,128)(2,1)}, bf16[128,1280]{1,0:T(8,128)(2,1)S(1)}, u32[]{:S(2)}, u32[]{:S(2)}) collective-permute-start(bf16[128,1280]{1,0:T(8,128)(2,1)} %get-tuple-element.118), channel_id=1, source_target_pairs={{0,12},{4,0},{8,4},{12,8},{1,13},{5,1},{9,5},{13,9},{2,14},{6,2},{... | collective-permute-start | bytes 983048 | tf_op jit(solution)/shard_map/ppermute | solution.py:585
  16.9 17.9 %copy-start.4 = (bf16[128,1280]{1,0:T(8,128)(2,1)}, bf16[128,1280]{1,0:T(8,128)(2,1)S(1)}, u32[]{:S(2)}) copy-start(bf16[128,1280]{1,0:T(8,128)(2,1)S(1)} %collective-permute-done.refs_1_) | copy-start | bytes 983044
  23.1 11.7 %copy-start.5 = (bf16[128,1280]{1,0:T(8,128)(2,1)}, bf16[128,1280]{1,0:T(8,128)(2,1)S(1)}, u32[]{:S(2)}) copy-start(bf16[128,1280]{1,0:T(8,128)(2,1)S(1)} %collective-permute-done.1.refs_3_) | copy-start | bytes 983044
  23.2 20.0 %copy-start = (f32[8,128,128]{2,1,0:T(8,128)S(1)}, f32[8,128,128]{2,1,0:T(8,128)}, u32[]{:S(2)}) copy-start(f32[8,128,128]{2,1,0:T(8,128)} %start_ref.1) | copy-start | bytes 1572868
  23.2 20.0 %copy-start.1 = (f32[8,128,128]{2,1,0:T(8,128)S(1)}, f32[8,128,128]{2,1,0:T(8,128)}, u32[]{:S(2)}) copy-start(f32[8,128,128]{2,1,0:T(8,128)} %end_ref.1) | copy-start | bytes 1572868
  23.2 18.4 %collective-permute-start.6 = (bf16[8,576,512]{2,1,0:T(8,128)(2,1)}, bf16[8,576,512]{2,1,0:T(8,128)(2,1)}, u32[]{:S(2)}, u32[]{:S(2)}) collective-permute-start(bf16[8,576,512]{2,1,0:T(8,128)(2,1)} %refs_9_), channel_id=1, source_target_pairs={{0,1},{1,0},{2,3},{3,2},{4,5},{5,4},{6,7},{7,6},{8,9},{9,8},{10,11... | collective-permute-start | bytes 14155784 | tf_op jit(solution)/shard_map/ppermute | solution.py:580
  23.2 18.3 %collective-permute-start.3 = (bf16[128,1280]{1,0:T(8,128)(2,1)}, bf16[128,1280]{1,0:T(8,128)(2,1)S(1)}, u32[]{:S(2)}, u32[]{:S(2)}) collective-permute-start(bf16[128,1280]{1,0:T(8,128)(2,1)} %get-tuple-element.118), channel_id=1, source_target_pairs={{0,8},{4,12},{8,0},{12,4},{1,9},{5,13},{9,1},{13,5},{2,10},{6,14},... | collective-permute-start | bytes 983048 | tf_op jit(solution)/shard_map/ppermute | solution.py:585
  24.6 16.9 %collective-permute-start.4 = (bf16[128,1280]{1,0:T(8,128)(2,1)S(1)}, bf16[128,1280]{1,0:T(8,128)(2,1)}, u32[]{:S(2)}, u32[]{:S(2)}) collective-permute-start(bf16[128,1280]{1,0:T(8,128)(2,1)S(1)} %collective-permute-done.refs_1_), channel_id=1, source_target_pairs={{0,2},{2,0},{1,3},{3,1},{4,6},{6,4},{5,7},{7,5},{8,10},{10,8},{9,1... | collective-permute-start | bytes 983048 | tf_op jit(solution)/shard_map/ppermute | solution.py:580
  26.1 15.4 %collective-permute-start.5 = (bf16[128,1280]{1,0:T(8,128)(2,1)S(1)}, bf16[128,1280]{1,0:T(8,128)(2,1)}, u32[]{:S(2)}, u32[]{:S(2)}) collective-permute-start(bf16[128,1280]{1,0:T(8,128)(2,1)S(1)} %collective-permute-done.1.refs_3_), channel_id=1, source_target_pairs={{0,2},{2,0},{1,3},{3,1},{4,6},{6,4},{5,7},{7,5},{8,10},{10,8},{9,1... | collective-permute-start | bytes 983048 | tf_op jit(solution)/shard_map/ppermute | solution.py:580
  41.5 18.4 %copy-start.6 = (bf16[128,1280]{1,0:T(8,128)(2,1)}, bf16[128,1280]{1,0:T(8,128)(2,1)S(1)}, u32[]{:S(2)}) copy-start(bf16[128,1280]{1,0:T(8,128)(2,1)S(1)} %collective-permute-done.3.refs_2_) | copy-start | bytes 983044
  41.5 18.4 %collective-permute-start.11 = (bf16[8,576,512]{2,1,0:T(8,128)(2,1)}, bf16[8,576,512]{2,1,0:T(8,128)(2,1)}, u32[]{:S(2)}, u32[]{:S(2)}) collective-permute-start(bf16[8,576,512]{2,1,0:T(8,128)(2,1)} %bitcast.12), channel_id=1, source_target_pairs={{0,1},{1,0},{2,3},{3,2},{4,5},{5,4},{6,7},{7,6},{8,9},{9,8},{10,11... | collective-permute-start | bytes 14155784 | tf_op jit(solution)/shard_map/ppermute | solution.py:580
  41.6 14.0 %collective-permute-start.8 = (bf16[128,1280]{1,0:T(8,128)(2,1)S(1)}, bf16[128,1280]{1,0:T(8,128)(2,1)S(1)}, u32[]{:S(2)}, u32[]{:S(2)}) collective-permute-start(bf16[128,1280]{1,0:T(8,128)(2,1)S(1)} %collective-permute-done.3.refs_2_), channel_id=1, source_target_pairs={{0,2},{2,0},{1,3},{3,1},{4,6},{6,4},{5,7},{7,5},{8,10},{10,8},{9,1... | collective-permute-start | bytes 983048 | tf_op jit(solution)/shard_map/ppermute | solution.py:580
  46.0 9.6 %collective-permute-start.7 = (bf16[8,128,128]{2,1,0:T(8,128)(2,1)}, bf16[8,128,128]{2,1,0:T(8,128)(2,1)S(1)}, u32[]{:S(2)}, u32[]{:S(2)}) collective-permute-start(bf16[8,128,128]{2,1,0:T(8,128)(2,1)} %hop.3), channel_id=1, source_target_pairs={{0,4},{12,8},{1,5},{13,9},{2,6},{14,10},{3,7},{15,11},{16,20},{28,... | collective-permute-start | bytes 786440 | tf_op jit(solution)/shard_map/ppermute | solution.py:404
  56.3 3.6 %copy-start.7 = (bf16[128,1280]{1,0:T(8,128)(2,1)}, bf16[128,1280]{1,0:T(8,128)(2,1)S(1)}, u32[]{:S(2)}) copy-start(bf16[128,1280]{1,0:T(8,128)(2,1)S(1)} %collective-permute-done.8.refs_5_) | copy-start | bytes 983044
  58.6 27.9 %collective-permute-start.9 = (bf16[8,128,128]{2,1,0:T(8,128)(2,1)}, bf16[8,128,128]{2,1,0:T(8,128)(2,1)S(1)}, u32[]{:S(2)}, u32[]{:S(2)}) collective-permute-start(bf16[8,128,128]{2,1,0:T(8,128)(2,1)} %hop.4), channel_id=1, source_target_pairs={{4,8},{8,4},{5,9},{9,5},{6,10},{10,6},{7,11},{11,7},{20,24},{24,20... | collective-permute-start | bytes 786440 | tf_op jit(solution)/shard_map/ppermute | solution.py:404
  84.4 10.9 %collective-permute-start.15 = (bf16[2,128,640]{2,1,0:T(8,128)(2,1)}, bf16[2,128,640]{2,1,0:T(8,128)(2,1)S(1)}, u32[]{:S(2)}, u32[]{:S(2)}) collective-permute-start(bf16[2,128,640]{2,1,0:T(8,128)(2,1)} %get-tuple-element.181), channel_id=1, source_target_pairs={{0,2},{2,0},{1,3},{3,1},{4,6},{6,4},{5,7},{7,5},{8,10},{10,8},{9,1... | collective-permute-start | bytes 983048 | tf_op jit(solution)/shard_map/ppermute | solution.py:580
  85.0 17.2 %collective-permute-start.12 = (bf16[2,128,640]{2,1,0:T(8,128)(2,1)}, bf16[2,128,640]{2,1,0:T(8,128)(2,1)S(1)}, u32[]{:S(2)}, u32[]{:S(2)}) collective-permute-start(bf16[2,128,640]{2,1,0:T(8,128)(2,1)} %get-tuple-element.178), channel_id=1, source_target_pairs={{0,2},{2,0},{1,3},{3,1},{4,6},{6,4},{5,7},{7,5},{8,10},{10,8},{9,1... | collective-permute-start | bytes 983048 | tf_op jit(solution)/shard_map/ppermute | solution.py:580
  89.3 20.4 %collective-permute-start.10 = (bf16[8,128,128]{2,1,0:T(8,128)(2,1)}, bf16[8,128,128]{2,1,0:T(8,128)(2,1)S(1)}, u32[]{:S(2)}, u32[]{:S(2)}) collective-permute-start(bf16[8,128,128]{2,1,0:T(8,128)(2,1)} %hop.5), channel_id=1, source_target_pairs={{8,12},{4,0},{9,13},{5,1},{10,14},{6,2},{11,15},{7,3},{24,28},{20,... | collective-permute-start | bytes 786440 | tf_op jit(solution)/shard_map/ppermute | solution.py:404
  98.0 25.0 %collective-permute-start.16 = (bf16[128,640]{1,0:T(8,128)(2,1)}, bf16[128,640]{1,0:T(8,128)(2,1)S(1)}, u32[]{:S(2)}, u32[]{:S(2)}) collective-permute-start(bf16[128,640]{1,0:T(8,128)(2,1)} %get-tuple-element.182), channel_id=1, source_target_pairs={{0,4},{4,8},{8,12},{12,0},{1,5},{5,9},{9,13},{13,1},{2,6},{6,10},{... | collective-permute-start | bytes 491528 | tf_op jit(solution)/shard_map/ppermute | solution.py:585
  104.9 18.1 %collective-permute-start.13 = (bf16[128,640]{1,0:T(8,128)(2,1)}, bf16[128,640]{1,0:T(8,128)(2,1)S(1)}, u32[]{:S(2)}, u32[]{:S(2)}) collective-permute-start(bf16[128,640]{1,0:T(8,128)(2,1)} %get-tuple-element.179), channel_id=1, source_target_pairs={{0,8},{4,12},{8,0},{12,4},{1,9},{5,13},{9,1},{13,5},{2,10},{6,14},... | collective-permute-start | bytes 491528 | tf_op jit(solution)/shard_map/ppermute | solution.py:585
  108.1 14.9 %collective-permute-start.14 = (bf16[128,640]{1,0:T(8,128)(2,1)}, bf16[128,640]{1,0:T(8,128)(2,1)S(1)}, u32[]{:S(2)}, u32[]{:S(2)}) collective-permute-start(bf16[128,640]{1,0:T(8,128)(2,1)} %get-tuple-element.180), channel_id=1, source_target_pairs={{0,12},{4,0},{8,4},{12,8},{1,13},{5,1},{9,5},{13,9},{2,14},{6,2},{... | collective-permute-start | bytes 491528 | tf_op jit(solution)/shard_map/ppermute | solution.py:585
  123.0 0.7 copy-start.13
  (7 other events, 4.9 us)

commit v3 on v2

--- a/solution.py
+++ b/solution.py
@@ -10,6 +10,9 @@
 BF = jnp.bfloat16
 F32 = jnp.float32
 VMEM_BYTES = 62 * 1024 * 1024
+WEIGHT_SLOTS = 3
+HEADS_STEPS = (4, 2, 1)
+SMALL_BYTES = 12 * 1024 * 1024
 
 
 def dot(a, b):
@@ -172,6 +175,10 @@
     chunk,
     width,
     heads_step,
+    first,
+    heads_done,
+    arrivals,
+    given,
     place_ref,
     query_ref,
     key_ref,
@@ -188,14 +195,16 @@
     end_ref,
     *refs,
 ):
-    arrived_refs, refs, rate_s = refs[:-7], refs[-7:-1], refs[-1]
+    first_head = first
+    arrived_refs, before_refs, refs = refs[:arrivals], refs[arrivals : arrivals + given], refs[arrivals + given :]
     (
         query_grad_ref,
         key_grad_ref,
         value_grad_ref,
         decay_grad_ref,
+        state_grad_ref,
         rate_grad_ref,
-        state_grad_ref,
+        rate_s,
     ) = refs
     position, last = place_ref[0], len(arrived_refs)
 
@@ -210,7 +219,7 @@
     rows, cols = places(chunk, 0), places(chunk, 1)
     tri = (rows <= cols).astype(BF)
     tri = jnp.concatenate([tri, tri], axis=1)
-    first = pl.program_id(0) * heads_step
+    first = first_head + pl.program_id(0) * heads_step
     heads = range(heads_step)
     rate_cols = jnp.transpose(rate_ref[...])
     rates = [column(rate_cols, first + h) for h in heads]
@@ -306,7 +315,16 @@
 
     @pl.when(pl.program_id(0) == pl.num_programs(0) - 1)
     def finish():
-        rate_grad_ref[...] = jnp.transpose(rate_s[...])[: rate_grad_ref.shape[0]]
+        rates_now = jnp.transpose(rate_s[...])[: rate_grad_ref.shape[0]]
+        if given:
+            rows_at = lax.broadcasted_iota(jnp.int32, rates_now.shape, 0)
+            fresh = (rows_at >= first_head) & (rows_at < first_head + heads_done)
+            rates_now = jnp.where(fresh, rates_now, before_refs[-1][...])
+        rate_grad_ref[...] = rates_now
+
+
+def heads_of_step(first, heads):
+    return next(n for n in HEADS_STEPS if heads % n == 0 and first % n == 0)
 
 
 def specs_of(tokens, width, chunk, heads_step, rate_heads, skip=0):
@@ -323,7 +341,7 @@
     heads_all, tokens = write_rate.shape
     width = queries.shape[1] // heads_all
     chunk = min(128, tokens)
-    heads_step = 2 if heads % 2 == 0 and first % 2 == 0 else 1
+    heads_step = heads_of_step(first, heads)
     lanes, rate, square, state = specs_of(
         tokens, width, chunk, heads_step, heads_all, first // heads_step
     )
@@ -346,60 +364,78 @@
 
 
 def section_grads(
-    place, queries, key_input, value_input, write_rate, out_grad, saved, ends, arrivals
+    place,
+    queries,
+    key_input,
+    value_input,
+    write_rate,
+    out_grad,
+    saved,
+    ends,
+    arrivals,
+    first,
+    heads,
+    into=(),
 ):
-    heads, tokens = write_rate.shape
-    width = queries.shape[1] // heads
+    heads_all, tokens = write_rate.shape
+    width = queries.shape[1] // heads_all
     chunk = min(128, tokens)
-    heads_step = 2 if heads % 2 == 0 else 1
-    lanes, rate, square, state = specs_of(tokens, width, chunk, heads_step, heads)
+    heads_step = heads_of_step(first, heads)
+    lanes, rate, square, state = specs_of(
+        tokens, width, chunk, heads_step, heads_all, first // heads_step
+    )
     shape = jax.ShapeDtypeStruct
+    args = (queries, key_input, value_input, write_rate, out_grad, *saved, *ends, *arrivals)
+    kept = [pl.BlockSpec(memory_space=pl.ANY)] * 5 + [rate]
     return pl.pallas_call(
-        functools.partial(grads_kernel, chunk, width, heads_step),
+        functools.partial(
+            grads_kernel, chunk, width, heads_step, first, heads, len(arrivals), len(into)
+        ),
         grid_spec=pltpu.PrefetchScalarGridSpec(
             num_scalar_prefetch=1,
             grid=(heads // heads_step,),
             in_specs=[lanes, lanes, lanes, rate, lanes]
             + [lanes] * 4
             + [square] * 2
-            + [state] * (2 + len(arrivals)),
-            out_specs=[lanes, lanes, lanes, lanes, rate, state],
+            + [state] * (2 + len(arrivals))
+            + kept[: len(into)],
+            out_specs=[lanes, lanes, lanes, lanes, state, rate],
             scratch_shapes=[pltpu.VMEM((tokens, 128), F32)],
         ),
         out_shape=[shape(queries.shape, F32)] * 4
-        + [shape((heads, tokens), F32), shape((heads, width, width), F32)],
+        + [shape((heads_all, width, width), F32), shape((heads_all, tokens), F32)],
+        input_output_aliases={1 + len(args) + n: n for n in range(len(into[:5]))},
         compiler_params=pltpu.CompilerParams(vmem_limit_bytes=VMEM_BYTES),
-        cost_estimate=pl.CostEstimate(flops=10**8, bytes_accessed=10**7, transcendentals=0),
         name="section_grads",
-    )(place, queries, key_input, value_input, write_rate, out_grad, *saved, *ends, *arrivals)
-
-
-def hop_kernel(backward_at, place_ref, transfer_ref, carried_ref, own_ref, state_ref, out_ref):
+    )(place, *args, *into)
+
+
+def hop_kernel(backward_at, place_ref, transfer_ref, carried_ref, own_ref, *refs):
     heads = transfer_ref.shape[0]
+    forward_state, backward_state, out_ref = refs[0], refs[-2], refs[-1]
 
     @pl.when(place_ref[0] == backward_at)
     def backward():
         for h in range(heads):
-            out_ref[h] = (tdot(transfer_ref[h], state_ref[h]) + own_ref[h]).astype(BF)
+            out_ref[h] = (tdot(transfer_ref[h], backward_state[h]) + own_ref[h]).astype(BF)
 
     @pl.when(place_ref[0] != backward_at)
     def forward():
         for h in range(heads):
-            out_ref[h] = (dot(transfer_ref[h], state_ref[h]) + carried_ref[h]).astype(BF)
-
-
-def hop(place, transfer, carried, own_grad, state, turn, sections):
-    spec = pl.BlockSpec(state.shape, lambda i, p: (0, 0, 0))
+            out_ref[h] = (dot(transfer_ref[h], forward_state[h]) + carried_ref[h]).astype(BF)
+
+
+def hop(place, transfer, carried, own_grad, states, turn, sections):
+    spec = pl.BlockSpec(transfer.shape, lambda i, p: (0, 0, 0))
     leaving = pl.pallas_call(
         functools.partial(hop_kernel, sections - turn),
         grid_spec=pltpu.PrefetchScalarGridSpec(
-            num_scalar_prefetch=1, grid=(1,), in_specs=[spec] * 4, out_specs=spec
+            num_scalar_prefetch=1, grid=(1,), in_specs=[spec] * (3 + len(states)), out_specs=spec
         ),
-        out_shape=jax.ShapeDtypeStruct(state.shape, BF),
-        compiler_params=pltpu.CompilerParams(vmem_limit_bytes=VMEM_BYTES),
-        cost_estimate=pl.CostEstimate(flops=10**8, bytes_accessed=10**6, transcendentals=0),
+        out_shape=jax.ShapeDtypeStruct(transfer.shape, BF),
+        compiler_params=pltpu.CompilerParams(vmem_limit_bytes=SMALL_BYTES),
         name="hop",
-    )(place, transfer, carried, own_grad, state)
+    )(place, transfer, carried, own_grad, *states)
     pairs = [(turn - 1, turn), (sections - turn, sections - turn - 1)]
     return lax.ppermute(leaving, "ctx", pairs)
 
@@ -409,11 +445,11 @@
     own_ref, came_refs, other_refs = refs[0], refs[1:sources], refs[sources : 2 * sources - 1]
     weight_refs, refs = refs[2 * sources - 1 : 2 * sources + 5], refs[2 * sources + 5 :]
     keep_ref, send_refs, scratch = refs[0], refs[1:3], refs[3:]
-    weights_s, tokens_s, pieces_s, ranks_s, gates_s, sems = scratch
+    weights_s, down_s, tokens_s, pieces_s, ranks_s, gates_s, sems = scratch
     step, steps = pl.program_id(0), pl.num_programs(0)
     mine, head_at, first, came_is = place_ref[0], place_ref[1], place_ref[2], place_ref[3]
     tokens = own_ref.shape[0]
-    wide, hidden_width = weights_s.shape[2:]
+    wide, hidden_width = down_s.shape[1:]
     padded = wide // 2
     experts = ranks_s.shape[1]
     many = tokens_s.shape[1]
@@ -422,10 +458,11 @@
         for m in range(3):
             for far in range(2):
                 part = mine if far == 0 else 1 - mine
-                at = pl.multiple_of(part * padded, 128)
+                rows = pl.ds(pl.multiple_of(part * padded, 128), part_width)
+                lanes = slice(m * hidden_width, (m + 1) * hidden_width)
                 yield pltpu.make_async_copy(
                     weight_refs[2 * m + far].at[expert],
-                    weights_s.at[slot, m, pl.ds(at, part_width)],
+                    weights_s.at[slot, rows, lanes] if m < 2 else down_s.at[slot, rows],
                     sems.at[slot, 2 * m + far],
                 )
 
@@ -438,17 +475,19 @@
         picks = [choice(source, first + e).astype(F32).astype(BF) for e in range(many)]
         return jnp.concatenate(picks, axis=0)
 
-    slot = lax.rem(step, 2)
+    slots = weights_s.shape[0]
+    slot = lax.rem(step, slots)
 
     @pl.when(step == 0)
     def dispatch():
-        for copy in weight_copies(0, 0):
-            copy.start()
-        blank = jnp.zeros((padded - part_width, hidden_width), BF)
-        for n in range(2):
-            for m in range(3):
-                weights_s[n, m, part_width:padded] = blank
-                weights_s[n, m, padded + part_width :] = blank
+        for e in range(slots - 1):
+            for copy in weight_copies(e, e):
+                copy.start()
+        for n in range(slots):
+            for ref in (weights_s, down_s):
+                blank = jnp.zeros((padded - part_width, ref.shape[2]), BF)
+                ref[n, part_width:padded] = blank
+                ref[n, padded + part_width :] = blank
         before = (places(tokens, 0) < places(tokens, 1)).astype(BF)
         for s, turn in enumerate(order):
             if turn == 0:
@@ -470,17 +509,14 @@
                     span = slice(s * capacity, (s + 1) * capacity)
                     tokens_s[which, e, span] = picked[e * capacity : (e + 1) * capacity]
 
-    @pl.when(step + 1 < steps)
+    @pl.when(step + slots - 1 < steps)
     def prefetch():
-        for copy in weight_copies(step + 1, 1 - slot):
+        for copy in weight_copies(step + slots - 1, lax.rem(step + slots - 1, slots)):
             copy.start()
 
     for copy in weight_copies(step, slot):
         copy.wait()
     at = first + step
-    gate_pre = dot(tokens_s[0, step], weights_s[slot, 0])
-    up_pre = dot(tokens_s[0, step], weights_s[slot, 1])
-    raw_grad = dot(tokens_s[1, step], weights_s[slot, 2])
     weight = jnp.concatenate(
         [
             jnp.sum(
@@ -490,14 +526,21 @@
         ],
         axis=0,
     )
-    sigmoid = jax.nn.sigmoid(gate_pre)
-    activated = gate_pre * sigmoid
-    hidden = (activated * up_pre).astype(BF).astype(F32)
-    gate_part = jnp.sum(hidden * raw_grad, axis=1, keepdims=True)
-    scaled = raw_grad * weight
-    gate_back = (scaled * up_pre * sigmoid * (1.0 + gate_pre * (1.0 - sigmoid))).astype(BF)
-    up_back = (scaled * activated).astype(BF)
-    piece = dot_t(gate_back, weights_s[slot, 0]) + dot_t(up_back, weights_s[slot, 1])
+    cut = hidden_width // (2 if hidden_width % 512 == 0 else 1)
+    gate_part, gate_backs, up_backs = 0.0, [], []
+    for f in range(0, hidden_width, cut):
+        gate_pre = dot(tokens_s[0, step], weights_s[slot, :, f : f + cut])
+        up_pre = dot(tokens_s[0, step], weights_s[slot, :, hidden_width + f : hidden_width + f + cut])
+        raw_grad = dot(tokens_s[1, step], down_s[slot, :, f : f + cut])
+        sigmoid = jax.nn.sigmoid(gate_pre)
+        activated = gate_pre * sigmoid
+        hidden = (activated * up_pre).astype(BF).astype(F32)
+        gate_part = gate_part + jnp.sum(hidden * raw_grad, axis=1, keepdims=True)
+        scaled = raw_grad * weight
+        slope = sigmoid + activated * (1.0 - sigmoid)
+        gate_backs.append((scaled * up_pre * slope).astype(BF))
+        up_backs.append((scaled * activated).astype(BF))
+    piece = dot_t(jnp.concatenate(gate_backs + up_backs, axis=1), weights_s[slot])
     lanes = lax.broadcasted_iota(jnp.int32, (1, wide), 1)
     here = (lanes == part_width + at) | (lanes == padded + part_width + at)
     piece = (piece + jnp.where(here, gate_part, 0.0)).astype(BF)
@@ -520,6 +563,7 @@
     many, part_width, hidden_width = weights[0].shape
     sources = len(order)
     padded = wide // 2
+    slots = min(WEIGHT_SLOTS, many)
     whole = lambda x: pl.BlockSpec(x.shape, lambda e, p: (0,) * len(x.shape))
     shape = jax.ShapeDtypeStruct
     outs = [shape((n, tokens, padded), BF) for n in (sources, sources // 2, sources // 2)]
@@ -533,12 +577,13 @@
             + [pl.BlockSpec(memory_space=pl.ANY)] * len(weights),
             out_specs=[whole(x) for x in outs],
             scratch_shapes=[
-                pltpu.VMEM((2, 3, wide, hidden_width), BF),
+                pltpu.VMEM((slots, wide, 2 * hidden_width), BF),
+                pltpu.VMEM((slots, wide, hidden_width), BF),
                 pltpu.VMEM((2, many, sources * capacity, wide), BF),
                 pltpu.VMEM((sources, many, capacity, wide), BF),
                 pltpu.VMEM((sources, total_experts, tokens), F32),
                 pltpu.VMEM((sources, total_experts, tokens), F32),
-                pltpu.SemaphoreType.DMA((2, 6)),
+                pltpu.SemaphoreType.DMA((slots, 6)),
             ],
         ),
         out_shape=outs,
@@ -551,7 +596,7 @@
     return pl.pallas_call(
         kernel,
         out_shape=out_shape,
-        compiler_params=pltpu.CompilerParams(vmem_limit_bytes=VMEM_BYTES),
+        compiler_params=pltpu.CompilerParams(vmem_limit_bytes=SMALL_BYTES),
         name=name,
     )(*args)
 
@@ -686,35 +731,30 @@
     sent, recurrent, weights_own = lax.optimization_barrier((sent, recurrent, weights_own))
     for s in near:
         came[s] = turned(sent, "ctx", s)
-    weights_far[0] = swapped(weights_own[0], "fsdp")
-    first_maps = section_maps(*recurrent, 0, heads_here // 2)
-    came, weights_far[0], first_maps, recurrent, sent, weights_own = lax.optimization_barrier(
-        (came, weights_far[0], first_maps, recurrent, sent, weights_own)
+    for m in range(2):
+        weights_far[m] = swapped(weights_own[m], "fsdp")
+    transfer, carried, own_grad, *saved = section_maps(*recurrent, 0, heads_here)
+    came, weights_far[:2], transfer, sent, weights_own = lax.optimization_barrier(
+        (came, weights_far[:2], transfer, sent, weights_own)
     )
     for s in far:
         came[s] = turned(sent, "ctx", s)
     for s in near:
         fetch_other(s)
-    weights_far[1] = swapped(weights_own[1], "fsdp")
-    last_maps = section_maps(
-        *recurrent, heads_here // 2, heads_here - heads_here // 2, into=first_maps
-    )
-    came, other, weights_far[1], last_maps, weights_own = lax.optimization_barrier(
-        (came, other, weights_far[1], last_maps, weights_own)
-    )
+    weights_far[2] = swapped(weights_own[2], "fsdp")
+    maps = (transfer, carried, own_grad)
+    arrivals = [hop(place, *maps, (start_state, end_grad), 1, sections)]
+    came, other, arrivals = lax.optimization_barrier((came, other, arrivals))
     for s in far:
         fetch_other(s)
-    weights_far[2] = swapped(weights_own[2], "fsdp")
-    transfer, carried, own_grad, *saved = last_maps
-    state = jnp.where(position == 0, start_state, end_grad).astype(BF)
-    state = hop(place, transfer, carried, own_grad, state, 1, sections)
-    arrivals = [state]
     if sections > 2:
-        other, state = lax.optimization_barrier((other, state))
-        state = hop(place, transfer, carried, own_grad, state, 2, sections)
-        arrivals.append(state)
+        arrivals.append(hop(place, *maps, arrivals[-1:], 2, sections))
+    other, arrivals = lax.optimization_barrier((other, arrivals))
     expert_place = jnp.stack([core, head_at, position * experts_here, came_is]).astype(jnp.int32)
     weights = [w for pair in zip(weights_own, weights_far) for w in pair]
+    late = []
+    for turn in range(3, sections):
+        late.append(hop(place, *maps, (arrivals + late)[-1:], turn, sections))
     keep, *sends = expert_work(
         expert_place,
         own,
@@ -725,35 +765,43 @@
         total_experts,
         order,
     )
-    for turn in range(3, sections):
-        state = hop(place, transfer, carried, own_grad, state, turn, sections)
-        arrivals.append(state)
-    gradients = section_grads(
+    keep, sends, late = lax.optimization_barrier((keep, sends, late))
+    arrivals = arrivals + late
+    grad_args = (
         place,
-        queries,
-        key_input,
-        value_input,
-        write_rate.T,
-        out_grad,
+        *(queries, key_input, value_input, write_rate.T, out_grad),
         saved,
         (start_state, end_grad),
         arrivals,
     )
-
+    half = heads_here // 2
+    rest = half + (heads_here - half) // 2
+    gradients = section_grads(*grad_args, 0, half)
+    if head_count == 2:
+        others_sums = [swapped(send, "head") for send in sends]
+        others_sums[0], gradients = lax.optimization_barrier((others_sums[0], gradients))
     if head_count == 2:
         shape = jax.ShapeDtypeStruct
         per = len(order) // 2
         block = (token_count, padded)
         pieces = []
-        for n, send in enumerate(sends):
+        for n, (low, high) in enumerate(((half, rest), (rest, heads_here))):
             sums = plain_call(
                 functools.partial(head_sum_kernel, n * per),
                 "head_sum",
                 [shape(block, BF)] * per,
-                keep, swapped(send, "head"),
+                keep, others_sums[n],
             )
-            for turn, piece in zip(order[n * per : (n + 1) * per], sums):
-                pieces.append(turned(piece, "ctx", sections - turn) if turn else piece)
+            sums, gradients, grad_args = lax.optimization_barrier((sums, gradients, grad_args))
+            pieces += [
+                turned(piece, "ctx", sections - turn) if turn else piece
+                for turn, piece in zip(order[n * per : (n + 1) * per], sums)
+            ]
+            if high > low:
+                gradients = section_grads(*grad_args, low, high - low, into=gradients)
+            if n == 0:
+                others_sums[1], gradients = lax.optimization_barrier((others_sums[1], gradients))
+        pieces, gradients = lax.optimization_barrier((pieces, gradients))
         whole = lambda x: pl.BlockSpec(x.shape, lambda i, p: (0, 0))
         outs = [shape((part_width, token_count), F32), shape((top_count // 2, token_count), F32)]
         home_args = (expert_ids.T, *pieces)
@@ -766,11 +814,13 @@
                 out_specs=[whole(x) for x in outs],
             ),
             out_shape=outs,
-            compiler_params=pltpu.CompilerParams(vmem_limit_bytes=VMEM_BYTES),
+            compiler_params=pltpu.CompilerParams(vmem_limit_bytes=SMALL_BYTES),
             name="home",
         )(head_at.astype(jnp.int32).reshape(1), *home_args)
         input_grads, gate_grads = input_grads.T, gate_grads.T
     else:
+        if heads_here > half:
+            gradients = section_grads(*grad_args, half, heads_here - half, into=gradients)
         sent_back = jnp.concatenate(sends, axis=0)
         halves_in = [jnp.where(head_at == 0, keep, sent_back), jnp.where(head_at == 0, sent_back, keep)]
         wide = jnp.concatenate([x[:, :, :part_width] for x in halves_in], axis=-1)
@@ -785,7 +835,7 @@
         ids_here = lax.dynamic_slice_in_dim(expert_ids, head_at * slots_here, slots_here, 1)
         named = ids_here[:, :, None] == lax.iota(jnp.int32, total_experts)[None, None, :]
         gate_grads = jnp.sum(jnp.where(named, gates[:, None, :], 0.0), axis=-1)
-    return (*gradients[:4], gradients[4].T, gradients[5][None], input_grads, gate_grads)
+    return (*gradients[:4], gradients[5].T, gradients[4][None], input_grads, gate_grads)
 
 
 def solution(mesh):

time: 126 us -> 108 us (0.86)
  Pallas kernels: 68.1 us -> 55.5 us
  starting transfers between devices: 26.6 us -> 23.5 us
  local copies, waits for them, and re-layouts: 4.32 us -> 2.91 us
    pallas_call x3, Pallas kernels: 6.44 us -> 0.65 us  [hop(): pl.pallas_call(functools.partial(hop_kernel, sections - turn), grid_spec=...]
    pallas_call x2 -> x1, Pallas kernels: 16.4 us -> 10.6 us  [section_maps(): pl.pallas_call(functools.partial(maps_kernel, chunk, width, heads_step, f...]
    pallas_call x1 -> x3, Pallas kernels: 12.6 us -> 16.8 us  [section_grads(): pl.pallas_call(functools.partial(grads_kernel, chunk, width, heads_step,...]
    ppermute x8, waiting for transfers between devices: 4.75 us -> 8.83 us  [swapped(): return lax.ppermute(x, axis, [(0, 1), (1, 0)])]
    ppermute x6, waiting for transfers between devices: 13.5 us -> 9.57 us  [turned(): return lax.ppermute(x, axis, [(i, (i + by) % count) for i in range(count)])]
    pallas_call x2, Pallas kernels: 3.88 us -> 0.16 us  [plain_call(): pl.pallas_call(kernel, out_shape=out_shape, compiler_params=pltpu.Compile...]
    ppermute x6, starting transfers between devices: 15.1 us -> 11.6 us  [turned(): return lax.ppermute(x, axis, [(i, (i + by) % count) for i in range(count)])]
    unnamed x28 -> x32, local copies, waits for them, and re-layouts: 4.32 us -> 2.91 us
  transfers between devices with their start and end apart: 17 -> 17, of which waited for: 5 -> 6; matrix products, arithmetic and copies ran while one was open for 1% -> 1% of each run, Pallas kernels for 51% -> 49%
where the time goes in v3:
time: 108 us; the launch traced here: 107 us
  Pallas kernels  55.5 us (51%)
  waiting for transfers between devices  23.7 us (22%)
  starting transfers between devices  23.5 us (22%)
  local copies, waits for them, and re-layouts  2.91 us (3%)
    pallas_call x1, Pallas kernels, expert_work(): pl.pallas_call(functools.partial(experts_kernel, capacity, part_width, or...  23.9 us
    pallas_call x3, Pallas kernels, section_grads(): pl.pallas_call(functools.partial(grads_kernel, chunk, width, heads_step,...  16.8 us
    ppermute x6, starting transfers between devices, turned(): return lax.ppermute(x, axis, [(i, (i + by) % count) for i in range(count)])  11.6 us
    pallas_call x1, Pallas kernels, section_maps(): pl.pallas_call(functools.partial(maps_kernel, chunk, width, heads_step, f...  10.6 us
    ppermute x6, waiting for transfers between devices, turned(): return lax.ppermute(x, axis, [(i, (i + by) % count) for i in range(count)])  9.57 us
    ppermute x8, waiting for transfers between devices, swapped(): return lax.ppermute(x, axis, [(0, 1), (1, 0)])  8.83 us
    ppermute x8, starting transfers between devices, swapped(): return lax.ppermute(x, axis, [(0, 1), (1, 0)])  6.25 us
    ppermute x3, starting transfers between devices, hop(): return lax.ppermute(leaving, 'ctx', pairs)  5.65 us
  transfers between devices with their start and end apart: 17, of which 6 were waited for; matrix products, arithmetic and copies ran while one was open for 1% of the time, Pallas kernels for 49%

profile of v3, /device:TPU:0, one launch (start us, length us, event | category | flops | bytes accessed | tf_op | source)
XLA Modules:
  0.0 107.1 jit_solution(15520515328209028077)
XLA Ops:
  0.7 2.5 %packed_tokens.1 = (bf16[128,2560]{1,0:T(8,128)(2,1)}, bf16[128,1280]{1,0:T(8,128)(2,1)}) custom-call(s32[1]{0:T(128)} %bitcast.1.which_ref.at_ref, bf16[128,1152]{1,0:T(8,128)(2,1)} %rows_ref.1, f32[128,1152]{1,0:T(8,128)} %grads_ref.1, s32[8,128]{1,0:T(8,128)} %bitcast.12, f32[8,128]{1,0:T(8,128)} %bitcast.21), custom_call_target="tpu_custom_call" | custom-call | tf_op jit(solution)/shard_map/packed_tokens/pallas_call | solution.py:665
  3.7 5.0 %collective-permute-start.1 = (bf16[128,1280]{1,0:T(8,128)(2,1)}, bf16[128,1280]{1,0:T(8,128)(2,1)S(1)}, u32[]{:S(2)}, u32[]{:S(2)}) collective-permute-start(bf16[128,1280]{1,0:T(8,128)(2,1)} %get-tuple-element.168), channel_id=1, source_target_pairs={{0,12},{4,0},{8,4},{12,8},{1,13},{5,1},{9,5},{13,9},{2,14},{6,2},{... | collective-permute-start | bytes 983048 | tf_op jit(solution)/shard_map/ppermute | solution.py:630
  8.7 10.6 %section_maps.1 = (bf16[8,128,128]{2,1,0:T(8,128)(2,1)}, bf16[8,128,128]{2,1,0:T(8,128)(2,1)}, bf16[8,128,128]{2,1,0:T(8,128)(2,1)}, f32[256,1024]{1,0:T(8,128)}...) custom-call(f32[256,1024]{1,0:T(8,128)} %query_ref.4, ...), custom_call_target="tpu_custom_call" | custom-call | flops 100000000 | bytes 10000000 | tf_op jit(solution)/shard_map/section_maps/pallas_call | solution.py:349
  19.3 4.7 %collective-permute-done.refs_1_ = bf16[128,1280]{1,0:T(8,128)(2,1)S(1)} collective-permute-done((bf16[128,1280]{1,0:T(8,128)(2,1)}, bf16[128,1280]{1,0:T(8,128)(2,1)S(1)}, u32[]{:S(2)}, u32[]{:S(2)}) %collective-permute-start) | collective-permute-done | bytes 327712 | tf_op jit(solution)/shard_map/ppermute | solution.py:630
  24.9 1.5 %collective-permute-start.5 = (bf16[128,1280]{1,0:T(8,128)(2,1)S(1)}, bf16[128,1280]{1,0:T(8,128)(2,1)S(1)}, u32[]{:S(2)}, u32[]{:S(2)}) collective-permute-start(bf16[128,1280]{1,0:T(8,128)(2,1)S(1)} %collective-permute-done.refs_1_), channel_id=1, source_target_pairs={{0,2},{2,0},{1,3},{3,1},{4,6},{6,4},{5,7},{7,5},{8,10},{10,8},{9,1... | collective-permute-start | bytes 983048 | tf_op jit(solution)/shard_map/ppermute | solution.py:625
  27.0 0.9 copy-done.5
  27.9 0.9 copy-done.6
  28.9 0.9 copy-done.7
  30.0 3.5 %collective-permute-start.7 = (bf16[8,128,128]{2,1,0:T(8,128)(2,1)S(1)}, bf16[8,128,128]{2,1,0:T(8,128)(2,1)S(1)}, u32[]{:S(2)}, u32[]{:S(2)}) collective-permute-start(bf16[8,128,128]{2,1,0:T(8,128)(2,1)S(1)} %hop.3), channel_id=1, source_target_pairs={{0,4},{12,8},{1,5},{13,9},{2,6},{14,10},{3,7},{15,11},{16,20},{28,... | collective-permute-start | bytes 786440 | tf_op jit(solution)/shard_map/ppermute | solution.py:440
  33.5 5.3 %collective-permute-done.7.refs_0_ = bf16[8,128,128]{2,1,0:T(8,128)(2,1)S(1)} collective-permute-done((bf16[8,128,128]{2,1,0:T(8,128)(2,1)S(1)}, bf16[8,128,128]{2,1,0:T(8,128)(2,1)S(1)}, u32[]{:S(2)}, u32[]{:S(2)}) %collective-permute-start.7) | collective-permute-done | bytes 262176 | tf_op jit(solution)/shard_map/ppermute | solution.py:440
  38.8 3.3 %collective-permute-done.4.refs_2_ = bf16[128,1280]{1,0:T(8,128)(2,1)S(1)} collective-permute-done((bf16[128,1280]{1,0:T(8,128)(2,1)S(1)}, bf16[128,1280]{1,0:T(8,128)(2,1)S(1)}, u32[]{:S(2)}, u32[]{:S(2)}) %collective-permute-start.4) | collective-permute-done | bytes 327712 | tf_op jit(solution)/shard_map/ppermute | solution.py:630
  42.2 1.5 %collective-permute-start.8 = (bf16[128,1280]{1,0:T(8,128)(2,1)S(1)}, bf16[128,1280]{1,0:T(8,128)(2,1)}, u32[]{:S(2)}, u32[]{:S(2)}) collective-permute-start(bf16[128,1280]{1,0:T(8,128)(2,1)S(1)} %collective-permute-done.4.refs_2_), channel_id=1, source_target_pairs={{0,2},{2,0},{1,3},{3,1},{4,6},{6,4},{5,7},{7,5},{8,10},{10,8},{9,1... | collective-permute-start | bytes 983048 | tf_op jit(solution)/shard_map/ppermute | solution.py:625
  44.7 7.0 %collective-permute-done.8.refs_5_ = bf16[128,1280]{1,0:T(8,128)(2,1)} collective-permute-done((bf16[128,1280]{1,0:T(8,128)(2,1)S(1)}, bf16[128,1280]{1,0:T(8,128)(2,1)}, u32[]{:S(2)}, u32[]{:S(2)}) %collective-permute-start.8) | collective-permute-done | bytes 327712 | tf_op jit(solution)/shard_map/ppermute | solution.py:625
  51.8 1.5 %collective-permute-start.11 = (bf16[8,128,128]{2,1,0:T(8,128)(2,1)S(1)}, bf16[8,128,128]{2,1,0:T(8,128)(2,1)S(1)}, u32[]{:S(2)}, u32[]{:S(2)}) collective-permute-start(bf16[8,128,128]{2,1,0:T(8,128)(2,1)S(1)} %hop.5), channel_id=1, source_target_pairs={{8,12},{4,0},{9,13},{5,1},{10,14},{6,2},{11,15},{7,3},{24,28},{20,... | collective-permute-start | bytes 786440 | tf_op jit(solution)/shard_map/ppermute | solution.py:440
  54.0 23.9 %expert_work.1 = (bf16[4,128,640]{2,1,0:T(8,128)(2,1)}, bf16[2,128,640]{2,1,0:T(8,128)(2,1)}, bf16[2,128,640]{2,1,0:T(8,128)(2,1)}) custom-call(s32[4]{0:T(128)} %pad_add_fusion.place_ref, bf16[128,2560]{1,0:T(8,128)(2,1)} %get-tuple-element.154.refs_0_, bf16[128,1280]{1,0:T(8,128)(2,1)} %copy-done.11, bf16[128,1280]{1,0:T(8,128)(2,1)} %copy-done.12, ...), custom_call_target="tpu_custom_call" | custom-call | tf_op jit(solution)/shard_map/expert_work/pallas_call | solution.py:571
  78.0 1.5 %collective-permute-start.12 = (bf16[2,128,640]{2,1,0:T(8,128)(2,1)}, bf16[2,128,640]{2,1,0:T(8,128)(2,1)S(1)}, u32[]{:S(2)}, u32[]{:S(2)}) collective-permute-start(bf16[2,128,640]{2,1,0:T(8,128)(2,1)} %get-tuple-element.192), channel_id=1, source_target_pairs={{0,2},{2,0},{1,3},{3,1},{4,6},{6,4},{5,7},{7,5},{8,10},{10,8},{9,1... | collective-permute-start | bytes 983048 | tf_op jit(solution)/shard_map/ppermute | solution.py:625
  80.1 7.0 %section_grads.3 = (f32[256,1024]{1,0:T(8,128)}, f32[256,1024]{1,0:T(8,128)}, f32[256,1024]{1,0:T(8,128)}, f32[256,1024]{1,0:T(8,128)}, f32[8,128,128]{2,1,0:T(8,128)}, /*index=5*/f32[8,256]{1,0:T(8,128)}) custom-call(s32[1]{0:T(128)} %bitcast.7.place_ref, f32[256,1024]{1,0:T(8,128)} %query_ref.4, f32[256,1024]{1,0:T(8,128)} %key_ref.4, ...), custom_call_target="tpu_custom_call" | custom-call | tf_op jit(solution)/shard_map/section_grads/pallas_call | solution.py:390
  87.0 1.9 %collective-permute-done.12.got = bf16[2,128,640]{2,1,0:T(8,128)(2,1)S(1)} collective-permute-done((bf16[2,128,640]{2,1,0:T(8,128)(2,1)}, bf16[2,128,640]{2,1,0:T(8,128)(2,1)S(1)}, u32[]{:S(2)}, u32[]{:S(2)}) %collective-permute-start.12) | collective-permute-done | bytes 327712 | tf_op jit(solution)/shard_map/ppermute | solution.py:625
  89.0 3.7 %collective-permute-start.13 = (bf16[128,640]{1,0:T(8,128)(2,1)S(1)}, bf16[128,640]{1,0:T(8,128)(2,1)S(1)}, u32[]{:S(2)}, u32[]{:S(2)}) collective-permute-start(bf16[128,640]{1,0:T(8,128)(2,1)S(1)} %get-tuple-element.216), channel_id=1, source_target_pairs={{0,8},{4,12},{8,0},{12,4},{1,9},{5,13},{9,1},{13,5},{2,10},{6,14},... | collective-permute-start | bytes 491528 | tf_op jit(solution)/shard_map/ppermute | solution.py:630
  92.7 1.4 %collective-permute-start.14 = (bf16[128,640]{1,0:T(8,128)(2,1)S(1)}, bf16[128,640]{1,0:T(8,128)(2,1)S(1)}, u32[]{:S(2)}, u32[]{:S(2)}) collective-permute-start(bf16[128,640]{1,0:T(8,128)(2,1)S(1)} %get-tuple-element.217), channel_id=1, source_target_pairs={{0,12},{4,0},{8,4},{12,8},{1,13},{5,1},{9,5},{13,9},{2,14},{6,2},{... | collective-permute-start | bytes 491528 | tf_op jit(solution)/shard_map/ppermute | solution.py:630
  94.0 4.9 %section_grads.4 = (f32[256,1024]{1,0:T(8,128)}, f32[256,1024]{1,0:T(8,128)}, f32[256,1024]{1,0:T(8,128)}, f32[256,1024]{1,0:T(8,128)}, f32[8,128,128]{2,1,0:T(8,128)}, /*index=5*/f32[8,256]{1,0:T(8,128)}) custom-call(s32[1]{0:T(128)} %bitcast.7.place_ref, ...), custom_call_target="tpu_custom_call", output_to_operand_aliasing={{0}: (17, {}), {1}: (18, {}), {2}: (19, {}), {3}: (20, {}),... | custom-call | tf_op jit(solution)/shard_map/section_grads/pallas_call | solution.py:390
  99.7 4.9 %section_grads.5 = (f32[256,1024]{1,0:T(8,128)}, f32[256,1024]{1,0:T(8,128)}, f32[256,1024]{1,0:T(8,128)}, f32[256,1024]{1,0:T(8,128)}, f32[8,128,128]{2,1,0:T(8,128)}, /*index=5*/f32[8,256]{1,0:T(8,128)}) custom-call(s32[1]{0:T(128)} %bitcast.7.place_ref, ...), custom_call_target="tpu_custom_call", output_to_operand_aliasing={{0}: (17, {}), {1}: (18, {}), {2}: (19, {}), {3}: (20, {}),... | custom-call | tf_op jit(solution)/shard_map/section_grads/pallas_call | solution.py:390
  104.7 1.5 %collective-permute-done.16.refs_2_ = bf16[128,640]{1,0:T(8,128)(2,1)S(1)} collective-permute-done((bf16[128,640]{1,0:T(8,128)(2,1)S(1)}, bf16[128,640]{1,0:T(8,128)(2,1)S(1)}, u32[]{:S(2)}, u32[]{:S(2)}) %collective-permute-start.16) | collective-permute-done | bytes 163872 | tf_op jit(solution)/shard_map/ppermute | solution.py:630
  106.2 0.9 home.1
  (55 shorter events, 5.4 us)
Async XLA Ops:
  0.6 26.3 %copy-start.1 = (f32[8,128,128]{2,1,0:T(8,128)S(1)}, f32[8,128,128]{2,1,0:T(8,128)}, u32[]{:S(2)}) copy-start(f32[8,128,128]{2,1,0:T(8,128)} %end_ref.3) | copy-start | bytes 1572868
  0.6 26.3 %copy-start = (f32[8,128,128]{2,1,0:T(8,128)S(1)}, f32[8,128,128]{2,1,0:T(8,128)}, u32[]{:S(2)}) copy-start(f32[8,128,128]{2,1,0:T(8,128)} %start_ref.3) | copy-start | bytes 1572868
  3.2 21.0 %copy-start.15 = (bf16[128,1280]{1,0:T(8,128)(2,1)S(1)}, bf16[128,1280]{1,0:T(8,128)(2,1)}, u32[]{:S(2)}) copy-start(bf16[128,1280]{1,0:T(8,128)(2,1)} %get-tuple-element.168) | copy-start | bytes 983044
  3.2 20.9 %collective-permute-start.2 = (bf16[8,576,512]{2,1,0:T(8,128)(2,1)}, bf16[8,576,512]{2,1,0:T(8,128)(2,1)}, u32[]{:S(2)}, u32[]{:S(2)}) collective-permute-start(bf16[8,576,512]{2,1,0:T(8,128)(2,1)} %refs_7_), channel_id=1, source_target_pairs={{0,1},{1,0},{2,3},{3,2},{4,5},{5,4},{6,7},{7,6},{8,9},{9,8},{10,11... | collective-permute-start | bytes 14155784 | tf_op jit(solution)/shard_map/ppermute | solution.py:625
  3.6 20.4 %collective-permute-start.3 = (bf16[8,576,512]{2,1,0:T(8,128)(2,1)}, bf16[8,576,512]{2,1,0:T(8,128)(2,1)}, u32[]{:S(2)}, u32[]{:S(2)}) collective-permute-start(bf16[8,576,512]{2,1,0:T(8,128)(2,1)} %refs_9_), channel_id=1, source_target_pairs={{0,1},{1,0},{2,3},{3,2},{4,5},{5,4},{6,7},{7,6},{8,9},{9,8},{10,11... | collective-permute-start | bytes 14155784 | tf_op jit(solution)/shard_map/ppermute | solution.py:625
  3.7 15.6 %collective-permute-start.1 = (bf16[128,1280]{1,0:T(8,128)(2,1)}, bf16[128,1280]{1,0:T(8,128)(2,1)S(1)}, u32[]{:S(2)}, u32[]{:S(2)}) collective-permute-start(bf16[128,1280]{1,0:T(8,128)(2,1)} %get-tuple-element.168), channel_id=1, source_target_pairs={{0,12},{4,0},{8,4},{12,8},{1,13},{5,1},{9,5},{13,9},{2,14},{6,2},{... | collective-permute-start | bytes 983048 | tf_op jit(solution)/shard_map/ppermute | solution.py:630
  8.7 15.3 %collective-permute-start = (bf16[128,1280]{1,0:T(8,128)(2,1)}, bf16[128,1280]{1,0:T(8,128)(2,1)S(1)}, u32[]{:S(2)}, u32[]{:S(2)}) collective-permute-start(bf16[128,1280]{1,0:T(8,128)(2,1)} %get-tuple-element.168), channel_id=1, source_target_pairs={{0,4},{4,8},{8,12},{12,0},{1,5},{5,9},{9,13},{13,1},{2,6},{6,10},{... | collective-permute-start | bytes 983048 | tf_op jit(solution)/shard_map/ppermute | solution.py:630
  19.3 34.7 %copy-start.10 = (bf16[128,1280]{1,0:T(8,128)(2,1)}, bf16[128,1280]{1,0:T(8,128)(2,1)S(1)}, u32[]{:S(2)}) copy-start(bf16[128,1280]{1,0:T(8,128)(2,1)S(1)} %collective-permute-done.1.refs_3_) | copy-start | bytes 983044
  24.0 27.6 %copy-start.11 = (bf16[128,1280]{1,0:T(8,128)(2,1)}, bf16[128,1280]{1,0:T(8,128)(2,1)S(1)}, u32[]{:S(2)}) copy-start(bf16[128,1280]{1,0:T(8,128)(2,1)S(1)} %collective-permute-done.refs_1_) | copy-start | bytes 983044
  24.0 29.9 %collective-permute-start.10 = (bf16[8,576,512]{2,1,0:T(8,128)(2,1)}, bf16[8,576,512]{2,1,0:T(8,128)(2,1)}, u32[]{:S(2)}, u32[]{:S(2)}) collective-permute-start(bf16[8,576,512]{2,1,0:T(8,128)(2,1)} %bitcast.14), channel_id=1, source_target_pairs={{0,1},{1,0},{2,3},{3,2},{4,5},{5,4},{6,7},{7,6},{8,9},{9,8},{10,11... | collective-permute-start | bytes 14155784 | tf_op jit(solution)/shard_map/ppermute | solution.py:625
  24.1 18.0 %collective-permute-start.4 = (bf16[128,1280]{1,0:T(8,128)(2,1)S(1)}, bf16[128,1280]{1,0:T(8,128)(2,1)S(1)}, u32[]{:S(2)}, u32[]{:S(2)}) collective-permute-start(bf16[128,1280]{1,0:T(8,128)(2,1)S(1)} %copy-done.15), channel_id=1, source_target_pairs={{0,8},{4,12},{8,0},{12,4},{1,9},{5,13},{9,1},{13,5},{2,10},{6,14},... | collective-permute-start | bytes 983048 | tf_op jit(solution)/shard_map/ppermute | solution.py:630
  24.9 17.2 %collective-permute-start.5 = (bf16[128,1280]{1,0:T(8,128)(2,1)S(1)}, bf16[128,1280]{1,0:T(8,128)(2,1)S(1)}, u32[]{:S(2)}, u32[]{:S(2)}) collective-permute-start(bf16[128,1280]{1,0:T(8,128)(2,1)S(1)} %collective-permute-done.refs_1_), channel_id=1, source_target_pairs={{0,2},{2,0},{1,3},{3,1},{4,6},{6,4},{5,7},{7,5},{8,10},{10,8},{9,1... | collective-permute-start | bytes 983048 | tf_op jit(solution)/shard_map/ppermute | solution.py:625
  26.4 15.8 %collective-permute-start.6 = (bf16[128,1280]{1,0:T(8,128)(2,1)S(1)}, bf16[128,1280]{1,0:T(8,128)(2,1)S(1)}, u32[]{:S(2)}, u32[]{:S(2)}) collective-permute-start(bf16[128,1280]{1,0:T(8,128)(2,1)S(1)} %collective-permute-done.1.refs_3_), channel_id=1, source_target_pairs={{0,2},{2,0},{1,3},{3,1},{4,6},{6,4},{5,7},{7,5},{8,10},{10,8},{9,1... | collective-permute-start | bytes 983048 | tf_op jit(solution)/shard_map/ppermute | solution.py:625
  30.0 8.8 %collective-permute-start.7 = (bf16[8,128,128]{2,1,0:T(8,128)(2,1)S(1)}, bf16[8,128,128]{2,1,0:T(8,128)(2,1)S(1)}, u32[]{:S(2)}, u32[]{:S(2)}) collective-permute-start(bf16[8,128,128]{2,1,0:T(8,128)(2,1)S(1)} %hop.3), channel_id=1, source_target_pairs={{0,4},{12,8},{1,5},{13,9},{2,6},{14,10},{3,7},{15,11},{16,20},{28,... | collective-permute-start | bytes 786440 | tf_op jit(solution)/shard_map/ppermute | solution.py:440
  38.8 39.1 %copy-start.2 = (bf16[8,128,128]{2,1,0:T(8,128)(2,1)}, bf16[8,128,128]{2,1,0:T(8,128)(2,1)S(1)}, u32[]{:S(2)}) copy-start(bf16[8,128,128]{2,1,0:T(8,128)(2,1)S(1)} %collective-permute-done.7.refs_0_) | copy-start | bytes 786436
  42.2 9.4 %collective-permute-start.8 = (bf16[128,1280]{1,0:T(8,128)(2,1)S(1)}, bf16[128,1280]{1,0:T(8,128)(2,1)}, u32[]{:S(2)}, u32[]{:S(2)}) collective-permute-start(bf16[128,1280]{1,0:T(8,128)(2,1)S(1)} %collective-permute-done.4.refs_2_), channel_id=1, source_target_pairs={{0,2},{2,0},{1,3},{3,1},{4,6},{6,4},{5,7},{7,5},{8,10},{10,8},{9,1... | collective-permute-start | bytes 983048 | tf_op jit(solution)/shard_map/ppermute | solution.py:625
  44.0 0.7 collective-permute-start.9
  44.7 33.3 %copy-start.3 = (bf16[8,128,128]{2,1,0:T(8,128)(2,1)}, bf16[8,128,128]{2,1,0:T(8,128)(2,1)S(1)}, u32[]{:S(2)}) copy-start(bf16[8,128,128]{2,1,0:T(8,128)(2,1)S(1)} %collective-permute-done.9.refs_0_.refs_1_) | copy-start | bytes 786436
  51.8 26.1 %collective-permute-start.11 = (bf16[8,128,128]{2,1,0:T(8,128)(2,1)S(1)}, bf16[8,128,128]{2,1,0:T(8,128)(2,1)S(1)}, u32[]{:S(2)}, u32[]{:S(2)}) collective-permute-start(bf16[8,128,128]{2,1,0:T(8,128)(2,1)S(1)} %hop.5), channel_id=1, source_target_pairs={{8,12},{4,0},{9,13},{5,1},{10,14},{6,2},{11,15},{7,3},{24,28},{20,... | collective-permute-start | bytes 786440 | tf_op jit(solution)/shard_map/ppermute | solution.py:440
  78.0 10.9 %collective-permute-start.12 = (bf16[2,128,640]{2,1,0:T(8,128)(2,1)}, bf16[2,128,640]{2,1,0:T(8,128)(2,1)S(1)}, u32[]{:S(2)}, u32[]{:S(2)}) collective-permute-start(bf16[2,128,640]{2,1,0:T(8,128)(2,1)} %get-tuple-element.192), channel_id=1, source_target_pairs={{0,2},{2,0},{1,3},{3,1},{4,6},{6,4},{5,7},{7,5},{8,10},{10,8},{9,1... | collective-permute-start | bytes 983048 | tf_op jit(solution)/shard_map/ppermute | solution.py:625
  79.5 19.4 %collective-permute-start.15 = (bf16[2,128,640]{2,1,0:T(8,128)(2,1)}, bf16[2,128,640]{2,1,0:T(8,128)(2,1)S(1)}, u32[]{:S(2)}, u32[]{:S(2)}) collective-permute-start(bf16[2,128,640]{2,1,0:T(8,128)(2,1)} %get-tuple-element.218), channel_id=1, source_target_pairs={{0,2},{2,0},{1,3},{3,1},{4,6},{6,4},{5,7},{7,5},{8,10},{10,8},{9,1... | collective-permute-start | bytes 983048 | tf_op jit(solution)/shard_map/ppermute | solution.py:625
  89.0 15.7 %collective-permute-start.13 = (bf16[128,640]{1,0:T(8,128)(2,1)S(1)}, bf16[128,640]{1,0:T(8,128)(2,1)S(1)}, u32[]{:S(2)}, u32[]{:S(2)}) collective-permute-start(bf16[128,640]{1,0:T(8,128)(2,1)S(1)} %get-tuple-element.216), channel_id=1, source_target_pairs={{0,8},{4,12},{8,0},{12,4},{1,9},{5,13},{9,1},{13,5},{2,10},{6,14},... | collective-permute-start | bytes 491528 | tf_op jit(solution)/shard_map/ppermute | solution.py:630
  92.7 12.0 %collective-permute-start.14 = (bf16[128,640]{1,0:T(8,128)(2,1)S(1)}, bf16[128,640]{1,0:T(8,128)(2,1)S(1)}, u32[]{:S(2)}, u32[]{:S(2)}) collective-permute-start(bf16[128,640]{1,0:T(8,128)(2,1)S(1)} %get-tuple-element.217), channel_id=1, source_target_pairs={{0,12},{4,0},{8,4},{12,8},{1,13},{5,1},{9,5},{13,9},{2,14},{6,2},{... | collective-permute-start | bytes 491528 | tf_op jit(solution)/shard_map/ppermute | solution.py:630
  99.0 7.2 %collective-permute-start.16 = (bf16[128,640]{1,0:T(8,128)(2,1)S(1)}, bf16[128,640]{1,0:T(8,128)(2,1)S(1)}, u32[]{:S(2)}, u32[]{:S(2)}) collective-permute-start(bf16[128,640]{1,0:T(8,128)(2,1)S(1)} %get-tuple-element.257), channel_id=1, source_target_pairs={{0,4},{4,8},{8,12},{12,0},{1,5},{5,9},{9,13},{13,1},{2,6},{6,10},{... | collective-permute-start | bytes 491528 | tf_op jit(solution)/shard_map/ppermute | solution.py:630
  (9 other events, 54.5 us)

commit v4 on v3

--- a/solution.py
+++ b/solution.py
@@ -440,10 +440,71 @@
     return lax.ppermute(leaving, "ctx", pairs)
 
 
-def experts_kernel(capacity, part_width, order, place_ref, *refs):
+def choice(ranks_s, source, at, capacity):
+    rank = ranks_s[source, pl.ds(at, 1), :]
+    slot = lax.broadcasted_iota(jnp.int32, (capacity, ranks_s.shape[2]), 0).astype(F32)
+    return slot == rank
+
+
+def choices(ranks_s, source, first, many, capacity):
+    picks = [choice(ranks_s, source, first + e, capacity) for e in range(many)]
+    return jnp.concatenate([pick.astype(F32).astype(BF) for pick in picks], axis=0)
+
+
+def rank_tokens(tokens_ref, part_width, experts):
+    tokens = tokens_ref.shape[0]
+    start = part_width // 128 * 128
+    dense = jnp.transpose(tokens_ref[:, start : start + 128].astype(F32))
+    dense = dense[part_width - start : part_width - start + experts]
+    named = dense > 0.0
+    before = (places(tokens, 0) < places(tokens, 1)).astype(BF)
+    return dense, jnp.where(named, dot(named.astype(F32), before), -1.0)
+
+
+def dispatch_kernel(capacity, part_width, sources, place_ref, own_ref, *refs):
+    came_refs, other_refs, out_ref, ranks_s = refs[: sources - 1], refs[sources - 1 : -2], refs[-2], refs[-1]
+    first, came_is = place_ref[2], place_ref[3]
+    many, wide = out_ref.shape[1], out_ref.shape[3]
+    for s in range(sources):
+        if s == sources - 1:
+            came, other, kind = own_ref.at[:, :wide], own_ref.at[:, wide:], 0
+        else:
+            came, other, kind = came_refs[s], other_refs[s], came_is
+        ranks_s[s] = rank_tokens(came, part_width, ranks_s.shape[1])[1]
+        pick = choices(ranks_s, s, first, many, capacity)
+        for which, ref in ((kind, came), (1 - kind, other)):
+            picked = dot(pick, ref[...]).astype(BF)
+            for e in range(many):
+                span = slice(s * capacity, (s + 1) * capacity)
+                out_ref[which, e, span] = picked[e * capacity : (e + 1) * capacity]
+
+
+def dispatched(place, own, came, other, part_width, many, capacity, total_experts):
+    tokens, wide = own.shape[0], own.shape[1] // 2
+    sources = len(came) + 1
+    whole = lambda x: pl.BlockSpec(x.shape, lambda i, p: (0,) * len(x.shape))
+    out = jax.ShapeDtypeStruct((2, many, sources * capacity, wide), BF)
+    args = (own, *came, *other)
+    return pl.pallas_call(
+        functools.partial(dispatch_kernel, capacity, part_width, sources),
+        grid_spec=pltpu.PrefetchScalarGridSpec(
+            num_scalar_prefetch=1,
+            grid=(1,),
+            in_specs=[whole(x) for x in args],
+            out_specs=whole(out),
+            scratch_shapes=[pltpu.VMEM((sources, total_experts, tokens), F32)],
+        ),
+        out_shape=out,
+        compiler_params=pltpu.CompilerParams(vmem_limit_bytes=VMEM_BYTES),
+        name="dispatched",
+    )(place, *args)
+
+
+def experts_kernel(capacity, part_width, order, late, place_ref, *refs):
     sources = len(order)
-    own_ref, came_refs, other_refs = refs[0], refs[1:sources], refs[sources : 2 * sources - 1]
-    weight_refs, refs = refs[2 * sources - 1 : 2 * sources + 5], refs[2 * sources + 5 :]
+    own_ref, came_refs, other_refs = refs[0], refs[1:sources], refs[sources : sources + late]
+    early_ref, refs = refs[sources + late], refs[sources + late + 1 :]
+    weight_refs, refs = refs[:6], refs[6:]
     keep_ref, send_refs, scratch = refs[0], refs[1:3], refs[3:]
     weights_s, down_s, tokens_s, pieces_s, ranks_s, gates_s, sems = scratch
     step, steps = pl.program_id(0), pl.num_programs(0)
@@ -465,15 +526,12 @@
                     weights_s.at[slot, rows, lanes] if m < 2 else down_s.at[slot, rows],
                     sems.at[slot, 2 * m + far],
                 )
-
-    def choice(source, at):
-        rank = ranks_s[source, pl.ds(at, 1), :]
-        slot = lax.broadcasted_iota(jnp.int32, (capacity, tokens), 0).astype(F32)
-        return slot == rank
-
-    def choices(source):
-        picks = [choice(source, first + e).astype(F32).astype(BF) for e in range(many)]
-        return jnp.concatenate(picks, axis=0)
+        for which in range(2):
+            yield pltpu.make_async_copy(
+                early_ref.at[which, expert],
+                tokens_s.at[which, expert, late * capacity :],
+                sems.at[slot, 6 + which],
+            )
 
     slots = weights_s.shape[0]
     slot = lax.rem(step, slots)
@@ -488,22 +546,12 @@
                 blank = jnp.zeros((padded - part_width, ref.shape[2]), BF)
                 ref[n, part_width:padded] = blank
                 ref[n, padded + part_width :] = blank
-        before = (places(tokens, 0) < places(tokens, 1)).astype(BF)
         for s, turn in enumerate(order):
-            if turn == 0:
-                came, other, kind = own_ref.at[:, :wide], own_ref.at[:, wide:], 0
-            else:
-                came, other, kind = came_refs[turn - 1], other_refs[turn - 1], came_is
-            start = part_width // 128 * 128
-            offset = part_width - start
-            dense = jnp.transpose(came[:, start : start + 128].astype(F32))
-            dense = dense[offset : offset + experts]
-            named = dense > 0.0
-            rank = dot(named.astype(F32), before)
-            ranks_s[s] = jnp.where(named, rank, -1.0)
-            gates_s[s] = dense
-            pick = choices(s)
-            for which, ref in ((kind, came), (1 - kind, other)):
+            came = came_refs[turn - 1] if turn else own_ref
+            gates_s[s], ranks_s[s] = rank_tokens(came, part_width, experts)
+        for s, turn in enumerate(order[:late]):
+            pick = choices(ranks_s, s, first, many, capacity)
+            for which, ref in ((came_is, came_refs[turn - 1]), (1 - came_is, other_refs[s])):
                 picked = dot(pick, ref[...]).astype(BF)
                 for e in range(many):
                     span = slice(s * capacity, (s + 1) * capacity)
@@ -520,7 +568,7 @@
     weight = jnp.concatenate(
         [
             jnp.sum(
-                jnp.where(choice(s, at), gates_s[s, pl.ds(at, 1), :], 0.0), axis=1, keepdims=True
+                jnp.where(choice(ranks_s, s, at, capacity), gates_s[s, pl.ds(at, 1), :], 0.0), axis=1, keepdims=True
             )
             for s in range(sources)
         ],
@@ -552,13 +600,13 @@
         per = send_refs[0].shape[0]
         for s in range(sources):
             flat = pieces_s[s].reshape(many * capacity, wide)
-            total = tdot(choices(s), flat).astype(BF)
+            total = tdot(choices(ranks_s, s, first, many, capacity), flat).astype(BF)
             left, right = total[:, :padded], total[:, padded:]
             keep_ref[s] = jnp.where(head_at == 0, left, right)
             send_refs[s // per][s % per] = jnp.where(head_at == 0, right, left)
 
 
-def expert_work(place, own, came, other, weights, capacity, total_experts, order):
+def expert_work(place, own, came, other, early, weights, capacity, total_experts, order):
     tokens, wide = came[0].shape
     many, part_width, hidden_width = weights[0].shape
     sources = len(order)
@@ -569,12 +617,12 @@
     outs = [shape((n, tokens, padded), BF) for n in (sources, sources // 2, sources // 2)]
     token_args = (own, *came, *other)
     return pl.pallas_call(
-        functools.partial(experts_kernel, capacity, part_width, order),
+        functools.partial(experts_kernel, capacity, part_width, order, len(other)),
         grid_spec=pltpu.PrefetchScalarGridSpec(
             num_scalar_prefetch=1,
             grid=(many,),
             in_specs=[whole(x) for x in token_args]
-            + [pl.BlockSpec(memory_space=pl.ANY)] * len(weights),
+            + [pl.BlockSpec(memory_space=pl.ANY)] * (1 + len(weights)),
             out_specs=[whole(x) for x in outs],
             scratch_shapes=[
                 pltpu.VMEM((slots, wide, 2 * hidden_width), BF),
@@ -583,13 +631,13 @@
                 pltpu.VMEM((sources, many, capacity, wide), BF),
                 pltpu.VMEM((sources, total_experts, tokens), F32),
                 pltpu.VMEM((sources, total_experts, tokens), F32),
-                pltpu.SemaphoreType.DMA((slots, 6)),
+                pltpu.SemaphoreType.DMA((slots, 8)),
             ],
         ),
         out_shape=outs,
         compiler_params=pltpu.CompilerParams(vmem_limit_bytes=VMEM_BYTES),
         name="expert_work",
-    )(place, *token_args, *weights)
+    )(place, *token_args, early, *weights)
 
 
 def plain_call(kernel, name, out_shape, *args):
@@ -728,7 +776,10 @@
     own, sent = packed_tokens(
         came_is.reshape(1), moe_input, moe_grad, expert_ids.T, gate_weights.T, part_width, padded
     )
-    sent, recurrent, weights_own = lax.optimization_barrier((sent, recurrent, weights_own))
+    expert_place = jnp.stack([core, head_at, position * experts_here, came_is]).astype(jnp.int32)
+    sent, recurrent, weights_own, expert_place = lax.optimization_barrier(
+        (sent, recurrent, weights_own, expert_place)
+    )
     for s in near:
         came[s] = turned(sent, "ctx", s)
     for m in range(2):
@@ -749,8 +800,17 @@
         fetch_other(s)
     if sections > 2:
         arrivals.append(hop(place, *maps, arrivals[-1:], 2, sections))
-    other, arrivals = lax.optimization_barrier((other, arrivals))
-    expert_place = jnp.stack([core, head_at, position * experts_here, came_is]).astype(jnp.int32)
+    early = dispatched(
+        expert_place,
+        own,
+        [came[s] for s in near],
+        [other[s] for s in near],
+        part_width,
+        experts_here,
+        capacity,
+        total_experts,
+    )
+    other, arrivals, early = lax.optimization_barrier((other, arrivals, early))
     weights = [w for pair in zip(weights_own, weights_far) for w in pair]
     late = []
     for turn in range(3, sections):
@@ -759,7 +819,8 @@
         expert_place,
         own,
         [came[s] for s in turns],
-        [other[s] for s in turns],
+        [other[s] for s in far],
+        early,
         weights,
         capacity,
         total_experts,

time: 108 us -> 106 us (0.981)
  waiting for transfers between devices: 23.7 us -> 17.8 us
  Pallas kernels: 55.5 us -> 60.4 us
    pallas_call x0 -> x1, Pallas kernels: none -> 6.83 us  [dispatched(): pl.pallas_call(functools.partial(dispatch_kernel, capacity, part_width, s...]
    ppermute x8, waiting for transfers between devices: 8.83 us -> 2.2 us  [swapped(): return lax.ppermute(x, axis, [(0, 1), (1, 0)])]
    pallas_call x1, Pallas kernels: 23.9 us -> 22.1 us  [expert_work(): pl.pallas_call(functools.partial(experts_kernel, capacity, part_width, or...]
    unnamed x32 -> x34, local copies, waits for them, and re-layouts: 2.91 us -> 2.92 us
  transfers between devices with their start and end apart: 17 -> 17, of which waited for: 6 -> 6; matrix products, arithmetic and copies ran while one was open for 1% -> 0% of each run, Pallas kernels for 49% -> 54%
where the time goes in v4:
time: 106 us
  Pallas kernels  60.4 us (57%)
  starting transfers between devices  23.3 us (22%)
  waiting for transfers between devices  17.8 us (17%)
  local copies, waits for them, and re-layouts  2.92 us (3%)
    pallas_call x1, Pallas kernels, expert_work(): pl.pallas_call(functools.partial(experts_kernel, capacity, part_width, or...  22.1 us
    pallas_call x3, Pallas kernels, section_grads(): pl.pallas_call(functools.partial(grads_kernel, chunk, width, heads_step,...  16.8 us
    ppermute x6, starting transfers between devices, turned(): return lax.ppermute(x, axis, [(i, (i + by) % count) for i in range(count)])  11.3 us
    pallas_call x1, Pallas kernels, section_maps(): pl.pallas_call(functools.partial(maps_kernel, chunk, width, heads_step, f...  10.6 us
    ppermute x6, waiting for transfers between devices, turned(): return lax.ppermute(x, axis, [(i, (i + by) % count) for i in range(count)])  10.3 us
    pallas_call x1, Pallas kernels, dispatched(): pl.pallas_call(functools.partial(dispatch_kernel, capacity, part_width, s...  6.83 us
    ppermute x8, starting transfers between devices, swapped(): return lax.ppermute(x, axis, [(0, 1), (1, 0)])  6.25 us
    ppermute x3, starting transfers between devices, hop(): return lax.ppermute(leaving, 'ctx', pairs)  5.78 us
  transfers between devices with their start and end apart: 17, of which 6 were waited for; matrix products, arithmetic and copies ran while one was open for 0% of the time, Pallas kernels for 54%

profile of v4, /device:TPU:0, one launch (start us, length us, event | category | flops | bytes accessed | tf_op | source)
XLA Modules:
  0.0 106.0 jit_solution(2973189309842600118)
XLA Ops:
  1.3 2.4 %packed_tokens.1 = (bf16[128,2560]{1,0:T(8,128)(2,1)}, bf16[128,1280]{1,0:T(8,128)(2,1)}) custom-call(s32[1]{0:T(128)} %bitcast.which_ref.at_ref, bf16[128,1152]{1,0:T(8,128)(2,1)} %rows_ref.1, f32[128,1152]{1,0:T(8,128)} %grads_ref.1, s32[8,128]{1,0:T(8,128)} %bitcast.12, f32[8,128]{1,0:T(8,128)} %bitcast.21), custom_call_target="tpu_custom_call" | custom-call | tf_op jit(solution)/shard_map/packed_tokens/pallas_call | solution.py:713
  4.2 5.0 %collective-permute-start.1 = (bf16[128,1280]{1,0:T(8,128)(2,1)}, bf16[128,1280]{1,0:T(8,128)(2,1)S(1)}, u32[]{:S(2)}, u32[]{:S(2)}) collective-permute-start(bf16[128,1280]{1,0:T(8,128)(2,1)} %get-tuple-element.169), channel_id=1, source_target_pairs={{0,12},{4,0},{8,4},{12,8},{1,13},{5,1},{9,5},{13,9},{2,14},{6,2},{... | collective-permute-start | bytes 983048 | tf_op jit(solution)/shard_map/ppermute | solution.py:678
  9.3 10.6 %section_maps.1 = (bf16[8,128,128]{2,1,0:T(8,128)(2,1)}, bf16[8,128,128]{2,1,0:T(8,128)(2,1)}, bf16[8,128,128]{2,1,0:T(8,128)(2,1)}, f32[256,1024]{1,0:T(8,128)}...) custom-call(f32[256,1024]{1,0:T(8,128)} %query_ref.4, ...), custom_call_target="tpu_custom_call" | custom-call | flops 100000000 | bytes 10000000 | tf_op jit(solution)/shard_map/section_maps/pallas_call | solution.py:349
  19.9 4.7 %collective-permute-done.refs_0_.refs_1_ = bf16[128,1280]{1,0:T(8,128)(2,1)S(1)} collective-permute-done((bf16[128,1280]{1,0:T(8,128)(2,1)}, bf16[128,1280]{1,0:T(8,128)(2,1)S(1)}, u32[]{:S(2)}, u32[]{:S(2)}) %collective-permute-start) | collective-permute-done | bytes 327712 | tf_op jit(solution)/shard_map/ppermute | solution.py:678
  25.4 1.5 %collective-permute-start.5 = (bf16[128,1280]{1,0:T(8,128)(2,1)S(1)}, bf16[128,1280]{1,0:T(8,128)(2,1)S(1)}, u32[]{:S(2)}, u32[]{:S(2)}) collective-permute-start(bf16[128,1280]{1,0:T(8,128)(2,1)S(1)} %collective-permute-done.refs_0_.refs_1_), channel_id=1, source_target_pairs={{0,2},{2,0},{1,3},{3,1},{4,6},{6,4},{5,7},{7,5},{8,10},{10,8},{9,1... | collective-permute-start | bytes 983048 | tf_op jit(solution)/shard_map/ppermute | solution.py:673
  27.5 0.9 copy-done.5
  28.4 0.9 copy-done.7
  29.4 0.9 copy-done.9
  30.6 3.6 %collective-permute-start.7 = (bf16[8,128,128]{2,1,0:T(8,128)(2,1)S(1)}, bf16[8,128,128]{2,1,0:T(8,128)(2,1)S(1)}, u32[]{:S(2)}, u32[]{:S(2)}) collective-permute-start(bf16[8,128,128]{2,1,0:T(8,128)(2,1)S(1)} %hop.3), channel_id=1, source_target_pairs={{0,4},{12,8},{1,5},{13,9},{2,6},{14,10},{3,7},{15,11},{16,20},{28,... | collective-permute-start | bytes 786440 | tf_op jit(solution)/shard_map/ppermute | solution.py:440
  34.2 5.3 %collective-permute-done.7.refs_0_ = bf16[8,128,128]{2,1,0:T(8,128)(2,1)S(1)} collective-permute-done((bf16[8,128,128]{2,1,0:T(8,128)(2,1)S(1)}, bf16[8,128,128]{2,1,0:T(8,128)(2,1)S(1)}, u32[]{:S(2)}, u32[]{:S(2)}) %collective-permute-start.7) | collective-permute-done | bytes 262176 | tf_op jit(solution)/shard_map/ppermute | solution.py:440
  39.5 3.5 %collective-permute-done.4.refs_2_ = bf16[128,1280]{1,0:T(8,128)(2,1)} collective-permute-done((bf16[128,1280]{1,0:T(8,128)(2,1)}, bf16[128,1280]{1,0:T(8,128)(2,1)}, u32[]{:S(2)}, u32[]{:S(2)}) %collective-permute-start.4) | collective-permute-done | bytes 327712 | tf_op jit(solution)/shard_map/ppermute | solution.py:678
  43.0 1.5 %collective-permute-start.8 = (bf16[128,1280]{1,0:T(8,128)(2,1)}, bf16[128,1280]{1,0:T(8,128)(2,1)}, u32[]{:S(2)}, u32[]{:S(2)}) collective-permute-start(bf16[128,1280]{1,0:T(8,128)(2,1)} %collective-permute-done.4.refs_2_), channel_id=1, source_target_pairs={{0,2},{2,0},{1,3},{3,1},{4,6},{6,4},{5,7},{7,5},{8,10},{10,8},{9,1... | collective-permute-start | bytes 983048 | tf_op jit(solution)/shard_map/ppermute | solution.py:673
  45.5 6.8 %dispatched.1.refs_5_ = bf16[2,8,144,1280]{3,2,1,0:T(8,128)(2,1)} custom-call(s32[4]{0:T(128)} %pad_add_fusion.place_ref, bf16[128,2560]{1,0:T(8,128)(2,1)} %get-tuple-element.156.own_ref.refs_0_, bf16[128,1280]{1,0:T(8,128)(2,1)} %copy-done.14, bf16[128,1280]{1,0:T(8,128)(2,1)} %copy-done.13, bf16[128,1280]{1,0:T(8,128)(2,1)} %copy-done.15, ...), custom_call_target="tpu_custom_call" | custom-call | tf_op jit(solution)/shard_map/dispatched/pallas_call | solution.py:488
  52.9 1.5 %collective-permute-start.11 = (bf16[8,128,128]{2,1,0:T(8,128)(2,1)S(1)}, bf16[8,128,128]{2,1,0:T(8,128)(2,1)S(1)}, u32[]{:S(2)}, u32[]{:S(2)}) collective-permute-start(bf16[8,128,128]{2,1,0:T(8,128)(2,1)S(1)} %hop.5), channel_id=1, source_target_pairs={{8,12},{4,0},{9,13},{5,1},{10,14},{6,2},{11,15},{7,3},{24,28},{20,... | collective-permute-start | bytes 786440 | tf_op jit(solution)/shard_map/ppermute | solution.py:440
  54.4 22.1 %expert_work.1 = (bf16[4,128,640]{2,1,0:T(8,128)(2,1)}, bf16[2,128,640]{2,1,0:T(8,128)(2,1)}, bf16[2,128,640]{2,1,0:T(8,128)(2,1)}) custom-call(s32[4]{0:T(128)} %pad_add_fusion.place_ref, bf16[128,2560]{1,0:T(8,128)(2,1)} %get-tuple-element.156.own_ref.refs_0_, bf16[128,1280]{1,0:T(8,128)(2,1)} %copy-done.14, ...), custom_call_target="tpu_custom_call" | custom-call | tf_op jit(solution)/shard_map/expert_work/pallas_call | solution.py:619
  76.6 1.5 %collective-permute-start.12 = (bf16[2,128,640]{2,1,0:T(8,128)(2,1)}, bf16[2,128,640]{2,1,0:T(8,128)(2,1)S(1)}, u32[]{:S(2)}, u32[]{:S(2)}) collective-permute-start(bf16[2,128,640]{2,1,0:T(8,128)(2,1)} %get-tuple-element.192), channel_id=1, source_target_pairs={{0,2},{2,0},{1,3},{3,1},{4,6},{6,4},{5,7},{7,5},{8,10},{10,8},{9,1... | collective-permute-start | bytes 983048 | tf_op jit(solution)/shard_map/ppermute | solution.py:673
  78.7 7.0 %section_grads.3 = (f32[256,1024]{1,0:T(8,128)}, f32[256,1024]{1,0:T(8,128)}, f32[256,1024]{1,0:T(8,128)}, f32[256,1024]{1,0:T(8,128)}, f32[8,128,128]{2,1,0:T(8,128)}, /*index=5*/f32[8,256]{1,0:T(8,128)}) custom-call(s32[1]{0:T(128)} %bitcast.7.place_ref, f32[256,1024]{1,0:T(8,128)} %query_ref.4, f32[256,1024]{1,0:T(8,128)} %key_ref.4, ...), custom_call_target="tpu_custom_call" | custom-call | tf_op jit(solution)/shard_map/section_grads/pallas_call | solution.py:390
  85.6 1.9 %collective-permute-done.12.got = bf16[2,128,640]{2,1,0:T(8,128)(2,1)S(1)} collective-permute-done((bf16[2,128,640]{2,1,0:T(8,128)(2,1)}, bf16[2,128,640]{2,1,0:T(8,128)(2,1)S(1)}, u32[]{:S(2)}, u32[]{:S(2)}) %collective-permute-start.12) | collective-permute-done | bytes 327712 | tf_op jit(solution)/shard_map/ppermute | solution.py:673
  87.6 3.4 %collective-permute-start.13 = (bf16[128,640]{1,0:T(8,128)(2,1)S(1)}, bf16[128,640]{1,0:T(8,128)(2,1)S(1)}, u32[]{:S(2)}, u32[]{:S(2)}) collective-permute-start(bf16[128,640]{1,0:T(8,128)(2,1)S(1)} %get-tuple-element.216), channel_id=1, source_target_pairs={{0,8},{4,12},{8,0},{12,4},{1,9},{5,13},{9,1},{13,5},{2,10},{6,14},... | collective-permute-start | bytes 491528 | tf_op jit(solution)/shard_map/ppermute | solution.py:678
  91.0 2.0 %collective-permute-start.14 = (bf16[128,640]{1,0:T(8,128)(2,1)S(1)}, bf16[128,640]{1,0:T(8,128)(2,1)S(1)}, u32[]{:S(2)}, u32[]{:S(2)}) collective-permute-start(bf16[128,640]{1,0:T(8,128)(2,1)S(1)} %get-tuple-element.217), channel_id=1, source_target_pairs={{0,12},{4,0},{8,4},{12,8},{1,13},{5,1},{9,5},{13,9},{2,14},{6,2},{... | collective-permute-start | bytes 491528 | tf_op jit(solution)/shard_map/ppermute | solution.py:678
  93.0 4.9 %section_grads.4 = (f32[256,1024]{1,0:T(8,128)}, f32[256,1024]{1,0:T(8,128)}, f32[256,1024]{1,0:T(8,128)}, f32[256,1024]{1,0:T(8,128)}, f32[8,128,128]{2,1,0:T(8,128)}, /*index=5*/f32[8,256]{1,0:T(8,128)}) custom-call(s32[1]{0:T(128)} %bitcast.7.place_ref, ...), custom_call_target="tpu_custom_call", output_to_operand_aliasing={{0}: (17, {}), {1}: (18, {}), {2}: (19, {}), {3}: (20, {}),... | custom-call | tf_op jit(solution)/shard_map/section_grads/pallas_call | solution.py:390
  98.0 4.9 %section_grads.5 = (f32[256,1024]{1,0:T(8,128)}, f32[256,1024]{1,0:T(8,128)}, f32[256,1024]{1,0:T(8,128)}, f32[256,1024]{1,0:T(8,128)}, f32[8,128,128]{2,1,0:T(8,128)}, /*index=5*/f32[8,256]{1,0:T(8,128)}) custom-call(s32[1]{0:T(128)} %bitcast.7.place_ref, ...), custom_call_target="tpu_custom_call", output_to_operand_aliasing={{0}: (17, {}), {1}: (18, {}), {2}: (19, {}), {3}: (20, {}),... | custom-call | tf_op jit(solution)/shard_map/section_grads/pallas_call | solution.py:390
  103.0 2.2 %collective-permute-done.16.refs_2_ = bf16[128,640]{1,0:T(8,128)(2,1)S(1)} collective-permute-done((bf16[128,640]{1,0:T(8,128)(2,1)S(1)}, bf16[128,640]{1,0:T(8,128)(2,1)S(1)}, u32[]{:S(2)}, u32[]{:S(2)}) %collective-permute-start.16) | collective-permute-done | bytes 163872 | tf_op jit(solution)/shard_map/ppermute | solution.py:678
  105.1 0.9 home.1
  (58 shorter events, 5.1 us)
Async XLA Ops:
  0.6 26.8 %copy-start.1 = (f32[8,128,128]{2,1,0:T(8,128)S(1)}, f32[8,128,128]{2,1,0:T(8,128)}, u32[]{:S(2)}) copy-start(f32[8,128,128]{2,1,0:T(8,128)} %end_ref.3) | copy-start | bytes 1572868
  0.6 26.8 %copy-start = (f32[8,128,128]{2,1,0:T(8,128)S(1)}, f32[8,128,128]{2,1,0:T(8,128)}, u32[]{:S(2)}) copy-start(f32[8,128,128]{2,1,0:T(8,128)} %start_ref.3) | copy-start | bytes 1572868
  3.7 20.8 %collective-permute-start.2 = (bf16[8,576,512]{2,1,0:T(8,128)(2,1)}, bf16[8,576,512]{2,1,0:T(8,128)(2,1)}, u32[]{:S(2)}, u32[]{:S(2)}) collective-permute-start(bf16[8,576,512]{2,1,0:T(8,128)(2,1)} %refs_6_), channel_id=1, source_target_pairs={{0,1},{1,0},{2,3},{3,2},{4,5},{5,4},{6,7},{7,6},{8,9},{9,8},{10,11... | collective-permute-start | bytes 14155784 | tf_op jit(solution)/shard_map/ppermute | solution.py:673
  4.2 20.4 %collective-permute-start.3 = (bf16[8,576,512]{2,1,0:T(8,128)(2,1)}, bf16[8,576,512]{2,1,0:T(8,128)(2,1)}, u32[]{:S(2)}, u32[]{:S(2)}) collective-permute-start(bf16[8,576,512]{2,1,0:T(8,128)(2,1)} %refs_8_), channel_id=1, source_target_pairs={{0,1},{1,0},{2,3},{3,2},{4,5},{5,4},{6,7},{7,6},{8,9},{9,8},{10,11... | collective-permute-start | bytes 14155784 | tf_op jit(solution)/shard_map/ppermute | solution.py:673
  4.2 15.6 %collective-permute-start.1 = (bf16[128,1280]{1,0:T(8,128)(2,1)}, bf16[128,1280]{1,0:T(8,128)(2,1)S(1)}, u32[]{:S(2)}, u32[]{:S(2)}) collective-permute-start(bf16[128,1280]{1,0:T(8,128)(2,1)} %get-tuple-element.169), channel_id=1, source_target_pairs={{0,12},{4,0},{8,4},{12,8},{1,13},{5,1},{9,5},{13,9},{2,14},{6,2},{... | collective-permute-start | bytes 983048 | tf_op jit(solution)/shard_map/ppermute | solution.py:678
  9.3 15.3 %collective-permute-start = (bf16[128,1280]{1,0:T(8,128)(2,1)}, bf16[128,1280]{1,0:T(8,128)(2,1)S(1)}, u32[]{:S(2)}, u32[]{:S(2)}) collective-permute-start(bf16[128,1280]{1,0:T(8,128)(2,1)} %get-tuple-element.169), channel_id=1, source_target_pairs={{0,4},{4,8},{8,12},{12,0},{1,5},{5,9},{9,13},{13,1},{2,6},{6,10},{... | collective-permute-start | bytes 983048 | tf_op jit(solution)/shard_map/ppermute | solution.py:678
  19.9 25.7 %copy-start.13 = (bf16[128,1280]{1,0:T(8,128)(2,1)}, bf16[128,1280]{1,0:T(8,128)(2,1)S(1)}, u32[]{:S(2)}) copy-start(bf16[128,1280]{1,0:T(8,128)(2,1)S(1)} %collective-permute-done.1.refs_1_.refs_3_) | copy-start | bytes 983044
  24.6 29.9 %collective-permute-start.10 = (bf16[8,576,512]{2,1,0:T(8,128)(2,1)}, bf16[8,576,512]{2,1,0:T(8,128)(2,1)}, u32[]{:S(2)}, u32[]{:S(2)}) collective-permute-start(bf16[8,576,512]{2,1,0:T(8,128)(2,1)} %bitcast.14), channel_id=1, source_target_pairs={{0,1},{1,0},{2,3},{3,2},{4,5},{5,4},{6,7},{7,6},{8,9},{9,8},{10,11... | collective-permute-start | bytes 14155784 | tf_op jit(solution)/shard_map/ppermute | solution.py:673
  24.6 18.4 %collective-permute-start.4 = (bf16[128,1280]{1,0:T(8,128)(2,1)}, bf16[128,1280]{1,0:T(8,128)(2,1)}, u32[]{:S(2)}, u32[]{:S(2)}) collective-permute-start(bf16[128,1280]{1,0:T(8,128)(2,1)} %get-tuple-element.169), channel_id=1, source_target_pairs={{0,8},{4,12},{8,0},{12,4},{1,9},{5,13},{9,1},{13,5},{2,10},{6,14},... | collective-permute-start | bytes 983048 | tf_op jit(solution)/shard_map/ppermute | solution.py:678
  25.4 17.6 %collective-permute-start.5 = (bf16[128,1280]{1,0:T(8,128)(2,1)S(1)}, bf16[128,1280]{1,0:T(8,128)(2,1)S(1)}, u32[]{:S(2)}, u32[]{:S(2)}) collective-permute-start(bf16[128,1280]{1,0:T(8,128)(2,1)S(1)} %collective-permute-done.refs_0_.refs_1_), channel_id=1, source_target_pairs={{0,2},{2,0},{1,3},{3,1},{4,6},{6,4},{5,7},{7,5},{8,10},{10,8},{9,1... | collective-permute-start | bytes 983048 | tf_op jit(solution)/shard_map/ppermute | solution.py:673
  26.9 16.1 %collective-permute-start.6 = (bf16[128,1280]{1,0:T(8,128)(2,1)S(1)}, bf16[128,1280]{1,0:T(8,128)(2,1)S(1)}, u32[]{:S(2)}, u32[]{:S(2)}) collective-permute-start(bf16[128,1280]{1,0:T(8,128)(2,1)S(1)} %collective-permute-done.1.refs_1_.refs_3_), channel_id=1, source_target_pairs={{0,2},{2,0},{1,3},{3,1},{4,6},{6,4},{5,7},{7,5},{8,10},{10,8},{9,1... | collective-permute-start | bytes 983048 | tf_op jit(solution)/shard_map/ppermute | solution.py:673
  30.6 22.1 %copy-start.6 = (bf16[8,128,128]{2,1,0:T(8,128)(2,1)S(1)}, bf16[8,128,128]{2,1,0:T(8,128)(2,1)}, u32[]{:S(2)}) copy-start(bf16[8,128,128]{2,1,0:T(8,128)(2,1)} %get-tuple-element.171.transfer_ref) | copy-start | bytes 786436
  30.6 22.1 %copy-start.8 = (bf16[8,128,128]{2,1,0:T(8,128)(2,1)S(1)}, bf16[8,128,128]{2,1,0:T(8,128)(2,1)}, u32[]{:S(2)}) copy-start(bf16[8,128,128]{2,1,0:T(8,128)(2,1)} %get-tuple-element.172.carried_ref) | copy-start | bytes 786436
  30.6 22.1 %copy-start.10 = (bf16[8,128,128]{2,1,0:T(8,128)(2,1)S(1)}, bf16[8,128,128]{2,1,0:T(8,128)(2,1)}, u32[]{:S(2)}) copy-start(bf16[8,128,128]{2,1,0:T(8,128)(2,1)} %get-tuple-element.173.own_ref) | copy-start | bytes 786436
  30.6 8.9 %collective-permute-start.7 = (bf16[8,128,128]{2,1,0:T(8,128)(2,1)S(1)}, bf16[8,128,128]{2,1,0:T(8,128)(2,1)S(1)}, u32[]{:S(2)}, u32[]{:S(2)}) collective-permute-start(bf16[8,128,128]{2,1,0:T(8,128)(2,1)S(1)} %hop.3), channel_id=1, source_target_pairs={{0,4},{12,8},{1,5},{13,9},{2,6},{14,10},{3,7},{15,11},{16,20},{28,... | collective-permute-start | bytes 786440 | tf_op jit(solution)/shard_map/ppermute | solution.py:440
  43.0 9.6 %collective-permute-start.8 = (bf16[128,1280]{1,0:T(8,128)(2,1)}, bf16[128,1280]{1,0:T(8,128)(2,1)}, u32[]{:S(2)}, u32[]{:S(2)}) collective-permute-start(bf16[128,1280]{1,0:T(8,128)(2,1)} %collective-permute-done.4.refs_2_), channel_id=1, source_target_pairs={{0,2},{2,0},{1,3},{3,1},{4,6},{6,4},{5,7},{7,5},{8,10},{10,8},{9,1... | collective-permute-start | bytes 983048 | tf_op jit(solution)/shard_map/ppermute | solution.py:673
  44.8 7.5 %collective-permute-start.9 = (bf16[8,128,128]{2,1,0:T(8,128)(2,1)S(1)}, bf16[8,128,128]{2,1,0:T(8,128)(2,1)S(1)}, u32[]{:S(2)}, u32[]{:S(2)}) collective-permute-start(bf16[8,128,128]{2,1,0:T(8,128)(2,1)S(1)} %hop.4), channel_id=1, source_target_pairs={{4,8},{8,4},{5,9},{9,5},{6,10},{10,6},{7,11},{11,7},{20,24},{24,20... | collective-permute-start | bytes 786440 | tf_op jit(solution)/shard_map/ppermute | solution.py:440
  52.4 24.2 %copy-start.3 = (bf16[8,128,128]{2,1,0:T(8,128)(2,1)}, bf16[8,128,128]{2,1,0:T(8,128)(2,1)S(1)}, u32[]{:S(2)}) copy-start(bf16[8,128,128]{2,1,0:T(8,128)(2,1)S(1)} %collective-permute-done.9.refs_0_.refs_1_) | copy-start | bytes 786436
  52.9 23.6 %collective-permute-start.11 = (bf16[8,128,128]{2,1,0:T(8,128)(2,1)S(1)}, bf16[8,128,128]{2,1,0:T(8,128)(2,1)S(1)}, u32[]{:S(2)}, u32[]{:S(2)}) collective-permute-start(bf16[8,128,128]{2,1,0:T(8,128)(2,1)S(1)} %hop.5), channel_id=1, source_target_pairs={{8,12},{4,0},{9,13},{5,1},{10,14},{6,2},{11,15},{7,3},{24,28},{20,... | collective-permute-start | bytes 786440 | tf_op jit(solution)/shard_map/ppermute | solution.py:440
  76.6 10.9 %collective-permute-start.12 = (bf16[2,128,640]{2,1,0:T(8,128)(2,1)}, bf16[2,128,640]{2,1,0:T(8,128)(2,1)S(1)}, u32[]{:S(2)}, u32[]{:S(2)}) collective-permute-start(bf16[2,128,640]{2,1,0:T(8,128)(2,1)} %get-tuple-element.192), channel_id=1, source_target_pairs={{0,2},{2,0},{1,3},{3,1},{4,6},{6,4},{5,7},{7,5},{8,10},{10,8},{9,1... | collective-permute-start | bytes 983048 | tf_op jit(solution)/shard_map/ppermute | solution.py:673
  78.1 19.7 %collective-permute-start.15 = (bf16[2,128,640]{2,1,0:T(8,128)(2,1)}, bf16[2,128,640]{2,1,0:T(8,128)(2,1)S(1)}, u32[]{:S(2)}, u32[]{:S(2)}) collective-permute-start(bf16[2,128,640]{2,1,0:T(8,128)(2,1)} %get-tuple-element.218), channel_id=1, source_target_pairs={{0,2},{2,0},{1,3},{3,1},{4,6},{6,4},{5,7},{7,5},{8,10},{10,8},{9,1... | collective-permute-start | bytes 983048 | tf_op jit(solution)/shard_map/ppermute | solution.py:673
  87.6 15.4 %collective-permute-start.13 = (bf16[128,640]{1,0:T(8,128)(2,1)S(1)}, bf16[128,640]{1,0:T(8,128)(2,1)S(1)}, u32[]{:S(2)}, u32[]{:S(2)}) collective-permute-start(bf16[128,640]{1,0:T(8,128)(2,1)S(1)} %get-tuple-element.216), channel_id=1, source_target_pairs={{0,8},{4,12},{8,0},{12,4},{1,9},{5,13},{9,1},{13,5},{2,10},{6,14},... | collective-permute-start | bytes 491528 | tf_op jit(solution)/shard_map/ppermute | solution.py:678
  91.0 12.0 %collective-permute-start.14 = (bf16[128,640]{1,0:T(8,128)(2,1)S(1)}, bf16[128,640]{1,0:T(8,128)(2,1)S(1)}, u32[]{:S(2)}, u32[]{:S(2)}) collective-permute-start(bf16[128,640]{1,0:T(8,128)(2,1)S(1)} %get-tuple-element.217), channel_id=1, source_target_pairs={{0,12},{4,0},{8,4},{12,8},{1,13},{5,1},{9,5},{13,9},{2,14},{6,2},{... | collective-permute-start | bytes 491528 | tf_op jit(solution)/shard_map/ppermute | solution.py:678
  98.0 7.2 %collective-permute-start.16 = (bf16[128,640]{1,0:T(8,128)(2,1)S(1)}, bf16[128,640]{1,0:T(8,128)(2,1)S(1)}, u32[]{:S(2)}, u32[]{:S(2)}) collective-permute-start(bf16[128,640]{1,0:T(8,128)(2,1)S(1)} %get-tuple-element.257), channel_id=1, source_target_pairs={{0,4},{4,8},{8,12},{12,0},{1,5},{5,9},{9,13},{13,1},{2,6},{6,10},{... | collective-permute-start | bytes 491528 | tf_op jit(solution)/shard_map/ppermute | solution.py:678
  (10 other events, 57.8 us)
